TPU v7x, 32 devices: a whole 2x2x4 slice. The times are simulated.
32 devices in a mesh: seq: 4 (over y, core), ctx: 8 (over z, x).
Axes of the slice: x: 2, y: 2, z: 4, core: 2. Of those that a mesh axis runs over, the one named last changes fastest.
Arguments:
- hidden: bfloat16 [4, 2048, 2048], P('seq', 'ctx'), may hold values from -6 to 6
- out_grad: bfloat16 [4, 2048, 2048], P('seq', 'ctx'), may hold values from -6 to 6
- norm_first: float32 [2048], replicated, may hold values from 0.5 to 1.5
- norm_second: float32 [2048], replicated, may hold values from 0.5 to 1.5
- joint_weight: bfloat16 [2048, 4096], P(('seq', 'ctx')), may hold values from -0.125 to 0.125
- out_weight: bfloat16 [2048, 2048], P(('seq', 'ctx')), may hold values from -0.5 to 0.5
- gate_weight: bfloat16 [2048, 8192], P(('seq', 'ctx')), may hold values from -0.125 to 0.125
- up_weight: bfloat16 [2048, 8192], P(('seq', 'ctx')), may hold values from -0.125 to 0.125
- down_weight: bfloat16 [8192, 2048], P(('seq', 'ctx')), may hold values from -0.0625 to 0.0625
- joint_left: bfloat16 [8, 2048, 16], replicated, may hold values from -0.125 to 0.125
- joint_right: bfloat16 [8, 16, 4096], replicated, may hold values from -1.5 to 1.5
- out_left: bfloat16 [8, 2048, 16], replicated, may hold values from -0.5 to 0.5
- out_right: bfloat16 [8, 16, 2048], replicated, may hold values from -1.5 to 1.5
- gate_left: bfloat16 [8, 2048, 16], replicated, may hold values from -0.125 to 0.125
- gate_right: bfloat16 [8, 16, 8192], replicated, may hold values from -1.5 to 1.5
- up_left: bfloat16 [8, 2048, 16], replicated, may hold values from -0.125 to 0.125
- up_right: bfloat16 [8, 16, 8192], replicated, may hold values from -1.5 to 1.5
- down_left: bfloat16 [8, 8192, 16], replicated, may hold values from -0.0625 to 0.0625
- down_right: bfloat16 [8, 16, 2048], replicated, may hold values from -1.5 to 1.5
- doc_lengths: int32 [4, 6], P('seq'), may hold values from 1 to 1536, as said below
- adapter_ids: int32 [4], P('seq'), may hold values from 0 to 7
Outputs:
- layer_output: bfloat16 [4, 2048, 2048], P('seq', 'ctx')
- input_delta: bfloat16 [4, 2048, 2048], P('seq', 'ctx')
- delta_joint_left: float32 [8, 2048, 16], replicated
- delta_joint_right: float32 [8, 16, 4096], replicated
- delta_out_left: float32 [8, 2048, 16], replicated
- delta_out_right: float32 [8, 16, 2048], replicated
- delta_gate_left: float32 [8, 2048, 16], replicated
- delta_gate_right: float32 [8, 16, 8192], replicated
- delta_up_left: float32 [8, 2048, 16], replicated
- delta_up_right: float32 [8, 16, 8192], replicated
- delta_down_left: float32 [8, 8192, 16], replicated
- delta_down_right: float32 [8, 16, 2048], replicated
Inputs may be any that keep to these rules, and one draw needn't show every extreme that they name: `doc_lengths`: the lengths of each sequence sum to 2048; its first document holds 1536 tokens.
All inputs are finite; a program needn't handle non-finite values.
Results may differ from a plain program's by a relative error of at most 0.02.
Values may be sent and summed in bfloat16 or wider, within the bound.
No kernel may reach another device: no remote copies, remote signals or barrier semaphores. Data moves between devices by JAX's collectives and lax.ppermute only.
A program may use at most 320 MiB of HBM per device.

v0:
```python
import jax
import jax.numpy as jnp
from jax import lax
from jax.sharding import PartitionSpec as P

HEADS = 16
KV_HEADS = 8
HEAD_DIM = 128
WINDOW = 1024


epsilon = 1e-06
rotary_base = 1000000.0
masked_score = -1e30


def product(left, right):
    return jnp.dot(left, right, preferred_element_type=jnp.float32)


def across(left, right):
    return lax.dot_general(
        left, right, (((0,), (0,)), ((), ())), preferred_element_type=jnp.float32
    )


def against(left, right):
    return lax.dot_general(
        left, right, (((1,), (1,)), ((), ())), preferred_element_type=jnp.float32
    )


def norm_forward(values, gain):
    factor = lax.rsqrt(jnp.mean(values * values, axis=-1, keepdims=True) + epsilon)
    return (values * factor * gain, factor)


def norm_backward(values, factor, gain, incoming):
    scaled = incoming * gain
    return factor * scaled - values * (factor * factor * factor) * jnp.mean(
        scaled * values, axis=-1, keepdims=True
    )


def dealt_places(first_row, count, row_count, length):
    index = first_row + jnp.arange(count, dtype=jnp.int32)
    owner = index // row_count
    within = index % row_count
    half = row_count // 2
    return jnp.where(
        within < half, owner * half + within, length - (owner + 1) * half + within - half
    )


def document_of(places, lengths):
    ends = jnp.cumsum(lengths)
    return jnp.sum((places[:, None] >= ends[None, :]).astype(jnp.int32), axis=1)


def rotary(places):
    inverse = rotary_base ** (-jnp.arange(HEAD_DIM // 2, dtype=jnp.float32) * 2.0 / HEAD_DIM)
    angles = places.astype(jnp.float32)[:, None] * inverse[None, :]
    return (
        jnp.concatenate([jnp.cos(angles)] * 2, axis=1),
        jnp.concatenate([jnp.sin(angles)] * 2, axis=1),
    )


def rotate(flat, cosine, sine, heads):
    shaped = flat.reshape(flat.shape[0], heads, HEAD_DIM)
    half = HEAD_DIM // 2
    turned = jnp.concatenate([-shaped[..., half:], shaped[..., :half]], axis=-1)
    return (shaped * cosine[:, None, :] + turned * sine[:, None, :]).reshape(
        flat.shape[0], heads * HEAD_DIM
    )


def unrotate(flat, cosine, sine, heads):
    shaped = flat.reshape(flat.shape[0], heads, HEAD_DIM)
    half = HEAD_DIM // 2
    spun = shaped * sine[:, None, :]
    back = jnp.concatenate([spun[..., half:], -spun[..., :half]], axis=-1)
    return (shaped * cosine[:, None, :] + back).reshape(flat.shape[0], heads * HEAD_DIM)


def per_device(
    hidden,
    out_grad,
    norm_first,
    norm_second,
    joint_weight,
    out_weight,
    gate_weight,
    up_weight,
    down_weight,
    joint_left,
    joint_right,
    out_left,
    out_right,
    gate_left,
    gate_right,
    up_left,
    up_right,
    down_left,
    down_right,
    doc_lengths,
    adapter_ids,
):
    row_count = hidden.shape[1]
    length = row_count * lax.axis_size("ctx")
    group = HEADS // KV_HEADS
    query_width = HEADS * HEAD_DIM
    key_width = KV_HEADS * HEAD_DIM
    scale = HEAD_DIM ** (-0.5)
    low_type = jnp.bfloat16
    attention_full = (
        lax.all_gather(joint_weight, ("seq", "ctx"), axis=0, tiled=True),
        lax.all_gather(out_weight, ("seq", "ctx"), axis=0, tiled=True),
    )
    adapter = adapter_ids[0]
    factors = (
        joint_left,
        joint_right,
        out_left,
        out_right,
        gate_left,
        gate_right,
        up_left,
        up_right,
        down_left,
        down_right,
    )
    picked = [lax.dynamic_index_in_dim(factor, adapter, 0, keepdims=False) for factor in factors]
    own_places = dealt_places(lax.axis_index("ctx") * row_count, row_count, row_count, length)
    all_places = dealt_places(0, length, row_count, length)
    own_documents = document_of(own_places, doc_lengths[0])
    all_documents = document_of(all_places, doc_lengths[0])
    distance = own_places[:, None] - all_places[None, :]
    visible = (
        (own_documents[:, None] == all_documents[None, :]) & (distance >= 0) & (distance < WINDOW)
    )
    cosine, sine = rotary(own_places)
    tokens = hidden[0].astype(jnp.float32)
    first_values, first_factor = norm_forward(tokens, norm_first)
    first = first_values.astype(low_type)
    joint_inner = product(first, picked[0]).astype(low_type)
    joined = product(first, attention_full[0]) + product(joint_inner, picked[1])
    queries = rotate(joined[:, :query_width], cosine, sine, HEADS).astype(low_type)
    keys = rotate(joined[:, query_width : query_width + key_width], cosine, sine, KV_HEADS).astype(
        low_type
    )
    values = joined[:, query_width + key_width :].astype(low_type)
    key_all, value_all = (
        lax.all_gather(keys, "ctx", axis=0, tiled=True),
        lax.all_gather(values, "ctx", axis=0, tiled=True),
    )

    def head_inputs(head):
        query_rows = lax.dynamic_slice_in_dim(queries, head * group * HEAD_DIM, group * HEAD_DIM, 1)
        query_rows = query_rows.reshape(row_count, group, HEAD_DIM)
        key_rows = lax.dynamic_slice_in_dim(key_all, head * HEAD_DIM, HEAD_DIM, 1)
        value_rows = lax.dynamic_slice_in_dim(value_all, head * HEAD_DIM, HEAD_DIM, 1)
        raw = jnp.einsum("rgd,sd->grs", query_rows, key_rows, preferred_element_type=jnp.float32)
        scores = jnp.where(visible[None], raw * scale, masked_score)
        return (query_rows, key_rows, value_rows, scores)

    def forward_head(head):
        query_rows, key_rows, value_rows, scores = head_inputs(head)
        largest = jnp.max(scores, axis=-1, keepdims=True)
        raised = jnp.exp(scores - largest)
        total = jnp.sum(raised, axis=-1, keepdims=True)
        weights = (raised / total).astype(low_type)
        mixed_rows = jnp.einsum(
            "grs,sd->rgd", weights, value_rows, preferred_element_type=jnp.float32
        )
        return (mixed_rows.reshape(row_count, group * HEAD_DIM), (largest + jnp.log(total))[..., 0])

    mixed_heads, log_totals = lax.map(forward_head, jnp.arange(KV_HEADS))
    mixed = jnp.transpose(mixed_heads, (1, 0, 2)).reshape(row_count, query_width).astype(low_type)
    out_inner = product(mixed, picked[2]).astype(low_type)
    residual = tokens + (product(mixed, attention_full[1]) + product(out_inner, picked[3]))
    feed_full = (
        lax.all_gather(gate_weight, ("seq", "ctx"), axis=0, tiled=True),
        lax.all_gather(up_weight, ("seq", "ctx"), axis=0, tiled=True),
        lax.all_gather(down_weight, ("seq", "ctx"), axis=0, tiled=True),
    )
    second_values, second_factor = norm_forward(residual, norm_second)
    second = second_values.astype(low_type)
    gate_inner = product(second, picked[4]).astype(low_type)
    up_inner = product(second, picked[6]).astype(low_type)
    gate = product(second, feed_full[0]) + product(gate_inner, picked[5])
    up = product(second, feed_full[1]) + product(up_inner, picked[7])
    activated = (jax.nn.silu(gate) * up).astype(low_type)
    down_inner = product(activated, picked[8]).astype(low_type)
    result = residual + (product(activated, feed_full[2]) + product(down_inner, picked[9]))
    layer_output = result.astype(low_type)[None]
    attention_back = (
        lax.all_gather(joint_weight, ("seq", "ctx"), axis=0, tiled=True),
        lax.all_gather(out_weight, ("seq", "ctx"), axis=0, tiled=True),
    )
    feed_back = (
        lax.all_gather(gate_weight, ("seq", "ctx"), axis=0, tiled=True),
        lax.all_gather(up_weight, ("seq", "ctx"), axis=0, tiled=True),
        lax.all_gather(down_weight, ("seq", "ctx"), axis=0, tiled=True),
    )
    delta_output = out_grad[0]
    delta_down_inner = against(delta_output, picked[9]).astype(low_type)
    term_down_right = across(down_inner, delta_output)
    term_down_left = across(activated, delta_down_inner)
    delta_activated = against(delta_output, feed_back[2]) + against(delta_down_inner, picked[8])
    sigmoid_gate = jax.nn.sigmoid(gate)
    delta_gate = (delta_activated * up * sigmoid_gate * (1.0 + gate * (1.0 - sigmoid_gate))).astype(
        low_type
    )
    delta_up = (delta_activated * gate * sigmoid_gate).astype(low_type)
    delta_gate_inner = against(delta_gate, picked[5]).astype(low_type)
    delta_up_inner = against(delta_up, picked[7]).astype(low_type)
    term_gate_right = across(gate_inner, delta_gate)
    term_gate_left = across(second, delta_gate_inner)
    term_up_right = across(up_inner, delta_up)
    term_up_left = across(second, delta_up_inner)
    delta_second = (
        against(delta_gate, feed_back[0])
        + against(delta_up, feed_back[1])
        + against(delta_gate_inner, picked[4])
        + against(delta_up_inner, picked[6])
    )
    delta_residual = delta_output.astype(jnp.float32) + norm_backward(
        residual, second_factor, norm_second, delta_second
    )
    delta_branch = delta_residual.astype(low_type)
    delta_out_inner = against(delta_branch, picked[3]).astype(low_type)
    term_out_right = across(out_inner, delta_branch)
    term_out_left = across(mixed, delta_out_inner)
    delta_mixed = (
        against(delta_branch, attention_back[1]) + against(delta_out_inner, picked[2])
    ).astype(low_type)

    def backward_head(head):
        query_rows, key_rows, value_rows, scores = head_inputs(head)
        delta_rows = lax.dynamic_slice_in_dim(
            delta_mixed, head * group * HEAD_DIM, group * HEAD_DIM, 1
        )
        delta_rows = delta_rows.reshape(row_count, group, HEAD_DIM)
        log_total = lax.dynamic_index_in_dim(log_totals, head, 0, keepdims=False)
        chances = jnp.exp(scores - log_total[..., None])
        delta_weights = jnp.einsum(
            "rgd,sd->grs", delta_rows, value_rows, preferred_element_type=jnp.float32
        )
        inner_sum = jnp.sum(chances * delta_weights, axis=-1, keepdims=True)
        delta_raw = (chances * (delta_weights - inner_sum) * scale).astype(low_type)
        delta_query = jnp.einsum(
            "grs,sd->rgd", delta_raw, key_rows, preferred_element_type=jnp.float32
        )
        delta_key = jnp.einsum(
            "grs,rgd->sd", delta_raw, query_rows, preferred_element_type=jnp.float32
        )
        delta_value = jnp.einsum(
            "grs,rgd->sd", chances.astype(low_type), delta_rows, preferred_element_type=jnp.float32
        )
        return (delta_query.reshape(row_count, group * HEAD_DIM), delta_key, delta_value)

    delta_query_heads, delta_key_heads, delta_value_heads = lax.map(
        backward_head, jnp.arange(KV_HEADS)
    )
    delta_queries = jnp.transpose(delta_query_heads, (1, 0, 2)).reshape(row_count, query_width)
    key_terms = jnp.transpose(delta_key_heads, (1, 0, 2)).reshape(length, key_width)
    value_terms = jnp.transpose(delta_value_heads, (1, 0, 2)).reshape(length, key_width)
    delta_keys, delta_values = (
        lax.psum_scatter(
            key_terms.astype(jnp.bfloat16), "ctx", scatter_dimension=0, tiled=True
        ).astype(jnp.float32),
        lax.psum_scatter(
            value_terms.astype(jnp.bfloat16), "ctx", scatter_dimension=0, tiled=True
        ).astype(jnp.float32),
    )
    delta_joined = jnp.concatenate(
        [
            unrotate(delta_queries, cosine, sine, HEADS),
            unrotate(delta_keys, cosine, sine, KV_HEADS),
            delta_values,
        ],
        axis=1,
    ).astype(low_type)
    delta_joint_inner = against(delta_joined, picked[1]).astype(low_type)
    term_joint_right = across(joint_inner, delta_joined)
    term_joint_left = across(first, delta_joint_inner)
    delta_first = against(delta_joined, attention_back[0]) + against(delta_joint_inner, picked[0])
    input_delta = (
        delta_residual + norm_backward(tokens, first_factor, norm_first, delta_first)
    ).astype(low_type)[None]
    chosen = (jnp.arange(joint_left.shape[0], dtype=jnp.int32) == adapter).astype(jnp.float32)
    terms = (
        term_joint_left,
        term_joint_right,
        term_out_left,
        term_out_right,
        term_gate_left,
        term_gate_right,
        term_up_left,
        term_up_right,
        term_down_left,
        term_down_right,
    )
    placed = [chosen[:, None, None] * term[None] for term in terms]
    summed = lax.psum(
        (
            placed[0],
            placed[1],
            placed[2],
            placed[3],
            placed[4],
            placed[5],
            placed[6],
            placed[7],
            placed[8],
            placed[9],
        ),
        ("seq", "ctx"),
    )
    return (
        layer_output,
        input_delta,
        summed[0],
        summed[1],
        summed[2],
        summed[3],
        summed[4],
        summed[5],
        summed[6],
        summed[7],
        summed[8],
        summed[9],
    )


def solution(mesh):
    placed = (
        P("seq", "ctx", None),
        P("seq", "ctx", None),
        P(),
        P(),
        P(("seq", "ctx"), None),
        P(("seq", "ctx"), None),
        P(("seq", "ctx"), None),
        P(("seq", "ctx"), None),
        P(("seq", "ctx"), None),
        P(),
        P(),
        P(),
        P(),
        P(),
        P(),
        P(),
        P(),
        P(),
        P(),
        P("seq", None),
        P("seq"),
    )
    return jax.shard_map(
        per_device,
        mesh=mesh,
        in_specs=placed,
        out_specs=(
            P("seq", "ctx", None),
            P("seq", "ctx", None),
            P(),
            P(),
            P(),
            P(),
            P(),
            P(),
            P(),
            P(),
            P(),
            P(),
        ),
        check_vma=False,
    )
```

profile of v0, /device:TPU:0, one launch (start us, length us, event | category | flops | bytes accessed | tf_op | source)
XLA Modules:
  0.0 1890.4 jit_solution(5282031337670399445)
XLA Ops:
  13.2 115.5 %all-gather.8.cloned.1.call-done = bf16[2048,4096]{1,0:T(8,128)(2,1)} async-done(((bf16[64,4096]{1,0:T(8,128)(2,1)}), bf16[2048,4096]{1,0:T(8,128)(2,1)}) %all-gather.8.cloned.1.call-update) | async-done | bytes 16777232 | tf_op jit(solution)/shard_map/all_gather | solution.py:117
  128.7 8.2 fusion.79
  159.5 54.2 %all-gather.12.cloned.1.call-done = bf16[2048,1024]{1,0:T(8,128)(2,1)} async-done(((bf16[256,1024]{1,0:T(8,128)(2,1)}), bf16[2048,1024]{1,0:T(8,128)(2,1)}) %all-gather.12.cloned.1.call-update) | async-done | bytes 4194320 | tf_op jit(solution)/shard_map/all_gather | solution.py:154
  213.8 74.4 %all-gather.10.cloned.1.call-done = bf16[2048,1024]{1,0:T(8,128)(2,1)} async-done(((bf16[256,1024]{1,0:T(8,128)(2,1)}), bf16[2048,1024]{1,0:T(8,128)(2,1)}) %all-gather.10.cloned.1.call-update) | async-done | bytes 4194320 | tf_op jit(solution)/shard_map/all_gather | solution.py:155
  288.2 73.5 %while.34 = (s32[]{:T(128)}, bf16[8,256,256]{1,2,0:T(8,128)(2,1)S(1)}, f32[8,2,256]{2,1,0:T(2,128)}, s32[8]{0:T(128)S(1)}, bf16[2048,1024]{1,0:T(8,128)(2,1)}, /...) while((s32[]{:T(128)}, ...), condition=%wide.region_7.8_spmd.clone.clone, body=%wide.region_4.7_spmd.clone.sunk.clone | while | flops 548404736 | bytes 15502069 | solution.py:178
  378.1 184.9 %all-gather.18.cloned.1.call-done = bf16[2048,8192]{1,0:T(8,128)(2,1)} async-done(((bf16[64,8192]{1,0:T(8,128)(2,1)}), bf16[2048,8192]{1,0:T(8,128)(2,1)}) %all-gather.18.cloned.1.call-update) | async-done | bytes 33554448 | tf_op jit(solution)/shard_map/all_gather | solution.py:184
  563.0 17.9 fusion.170
  580.9 8.1 convolution_add_fusion.1
  589.0 169.9 %all-gather.16.cloned.1.call-done = bf16[2048,8192]{1,0:T(8,128)(2,1)} async-done(((bf16[64,8192]{1,0:T(8,128)(2,1)}), bf16[2048,8192]{1,0:T(8,128)(2,1)}) %all-gather.16.cloned.1.call-update) | async-done | bytes 33554448 | tf_op jit(solution)/shard_map/all_gather | solution.py:183
  758.8 18.0 fusion.169
  776.9 8.1 convolution_add_fusion.2
  785.0 169.8 %all-gather.20.cloned.1.call-done = bf16[8192,2048]{1,0:T(8,128)(2,1)} async-done(((bf16[256,2048]{1,0:T(8,128)(2,1)}), bf16[8192,2048]{1,0:T(8,128)(2,1)}) %all-gather.20.cloned.1.call-update) | async-done | bytes 33554448 | tf_op jit(solution)/shard_map/all_gather | solution.py:185
  954.8 18.5 fusion.73
  973.3 12.5 multiply_convert_fusion
  992.4 16.9 fusion.172
  1009.3 17.8 convolution_add_fusion.10
  1038.8 293.3 %while.35 = (s32[]{:T(128)}, f32[8,256,256]{1,2,0:T(8,128)}, bf16[8,2048,128]{2,1,0:T(8,128)(2,1)}, bf16[8,2048,128]{2,1,0:T(8,128)(2,1)}, s32[8]{0:T(128)S(1)},...) while((s32[]{:T(128)}, f32[8,256,256]{1,2,0:T(8,128)}, ...), condition=%wide.region_12.13_spmd.clone.clone, body=%wide.region_10.12_spmd.clone.sunk.clone | while | flops 1360008192 | bytes 52996304 | solution.py:263
  1092.3 8.1 fusion.292
  1275.5 8.1 fusion.292
  1373.5 49.8 %reduce-scatter.3.cloned.1.call-done = bf16[256,1024]{1,0:T(8,128)(2,1)} async-done(((bf16[2048,1024]{1,0:T(8,128)(2,1)}), bf16[256,1024]{1,0:T(8,128)(2,1)}) %reduce-scatter.3.cloned.1.call-update) | async-done | bytes 524304 | tf_op jit(solution)/shard_map/reduce_scatter | solution.py:270
  1427.4 87.7 %reduce-scatter.5.cloned.1.call-done = bf16[256,1024]{1,0:T(8,128)(2,1)} async-done(((bf16[2048,1024]{1,0:T(8,128)(2,1)}), bf16[256,1024]{1,0:T(8,128)(2,1)}) %reduce-scatter.5.cloned.1.call-update) | async-done | bytes 524304 | tf_op jit(solution)/shard_map/reduce_scatter | solution.py:273
  1523.5 18.3 fusion.171
  1544.1 12.7 fusion.164
  1560.8 302.5 %all-reduce.3.cloned.1.call-done = (f32[8,2048,16]{1,2,0:T(8,128)}, f32[8,16,4096]{2,1,0:T(8,128)}, f32[8,2048,16]{1,2,0:T(8,128)}, f32[8,16,2048]{2,1,0:T(8,128...) async-done(((f32[8,2048,16]{1,2,0:T(8,128)}, ...) | async-done | bytes 20971536 | tf_op jit(solution)/shard_map/psum | solution.py:306
  (515 shorter events, 453.4 us)
Async XLA Ops:
  7.2 966.2 %copy-start = (bf16[8,8192,16]{1,2,0:T(8,128)(2,1)S(1)}, bf16[8,8192,16]{1,2,0:T(8,128)(2,1)}, u32[]{:S(2)}) copy-start(bf16[8,8192,16]{1,2,0:T(8,128)(2,1)} %param.42) | copy-start | bytes 6291460
  7.2 121.5 %copy-start.17 = (bf16[1,256,2048]{2,1,0:T(8,128)(2,1)S(1)}, bf16[1,256,2048]{2,1,0:T(8,128)(2,1)}, u32[]{:S(2)}) copy-start(bf16[1,256,2048]{2,1,0:T(8,128)(2,1)} %param.25) | copy-start | bytes 3145732
  7.2 121.5 %copy-start.61 = (f32[2048]{0:T(1024)S(1)}, f32[2048]{0:T(1024)}, u32[]{:S(2)}) copy-start(f32[2048]{0:T(1024)} %param.27) | copy-start | bytes 24580
  7.2 121.5 %all-gather.8.cloned.1.call-start = ((), (), s32[]{:S(2)}) async-start(), calls=%async_computation.2 | async-start | bytes 17301504 | tf_op jit(solution)/shard_map/all_gather | solution.py:117
  8.0 205.8 %all-gather.12.cloned.1.call-start = ((), (), s32[]{:S(2)}) async-start(), calls=%async_computation.4 | async-start | bytes 4718592 | tf_op jit(solution)/shard_map/all_gather | solution.py:154
  9.4 142.6 %copy-start.30 = (f32[256,128]{1,0:T(8,128)}, f32[256,128]{1,0:T(8,128)S(1)}, u32[]{:S(2)}) copy-start(f32[256,128]{1,0:T(8,128)S(1)} %get-tuple-element.475) | copy-start | bytes 393220
  11.5 125.4 %copy-start.69 = (f32[256]{0:T(256)}, f32[256]{0:T(256)S(1)}, u32[]{:S(2)}) copy-start(f32[256]{0:T(256)S(1)} %get-tuple-element.457) | copy-start | bytes 3076
  13.2 123.7 %copy-start.64 = (bf16[256,16]{0,1:T(8,128)(2,1)}, bf16[256,16]{0,1:T(8,128)(2,1)S(1)}, u32[]{:S(2)}) copy-start(bf16[256,16]{0,1:T(8,128)(2,1)S(1)} %convolution_convert_fusion.6) | copy-start | bytes 24580
  142.0 146.1 %all-gather.10.cloned.1.call-start = ((), (), s32[]{:S(2)}) async-start(), calls=%async_computation.3 | async-start | bytes 4718592 | tf_op jit(solution)/shard_map/all_gather | solution.py:155
  144.2 222.5 %all-gather.14.cloned.1.call-start = ((), (), s32[]{:S(2)}) async-start(), calls=%async_computation.5 | async-start | bytes 8650752 | tf_op jit(solution)/shard_map/all_gather | solution.py:118
  144.8 418.2 %all-gather.18.cloned.1.call-start = ((), (), s32[]{:S(2)}) async-start(), calls=%async_computation.7 | async-start | bytes 34603008 | tf_op jit(solution)/shard_map/all_gather | solution.py:184
  145.4 613.5 %all-gather.16.cloned.1.call-start = ((), (), s32[]{:S(2)}) async-start(), calls=%async_computation.6 | async-start | bytes 34603008 | tf_op jit(solution)/shard_map/all_gather | solution.py:183
  146.0 808.9 %all-gather.20.cloned.1.call-start = ((), (), s32[]{:S(2)}) async-start(), calls=%async_computation.8 | async-start | bytes 34603008 | tf_op jit(solution)/shard_map/all_gather | solution.py:185
  146.7 1276.6 %reduce-scatter.3.cloned.1.call-start = ((), (), s32[]{:S(2)}) async-start(), calls=%async_computation.9 | async-start | bytes 4718592 | tf_op jit(solution)/shard_map/reduce_scatter | solution.py:270
  149.0 824.3 %copy-start.58 = (bf16[16,256]{1,0:T(8,128)(2,1)}, bf16[16,256]{1,0:T(8,128)(2,1)S(1)}, u32[]{:S(2)}) copy-start(bf16[16,256]{1,0:T(8,128)(2,1)S(1)} %convolution_convert_fusion.3) | copy-start | bytes 24580
  376.9 204.0 %copy-start.47 = (bf16[256,16]{0,1:T(8,128)(2,1)}, bf16[256,16]{0,1:T(8,128)(2,1)S(1)}, u32[]{:S(2)}) copy-start(bf16[256,16]{0,1:T(8,128)(2,1)S(1)} %convolution_convert_fusion.4) | copy-start | bytes 24580
  378.1 398.8 %copy-start.49 = (bf16[256,16]{0,1:T(8,128)(2,1)}, bf16[256,16]{0,1:T(8,128)(2,1)S(1)}, u32[]{:S(2)}) copy-start(bf16[256,16]{0,1:T(8,128)(2,1)S(1)} %convolution_convert_fusion.5) | copy-start | bytes 24580
  990.2 36.8 %copy-start.53 = (bf16[256,16]{0,1:T(8,128)(2,1)}, bf16[256,16]{0,1:T(8,128)(2,1)S(1)}, u32[]{:S(2)}) copy-start(bf16[256,16]{0,1:T(8,128)(2,1)S(1)} %convolution_convert_fusion.8) | copy-start | bytes 24580
  992.4 36.9 %copy-start.51 = (bf16[256,16]{0,1:T(8,128)(2,1)}, bf16[256,16]{0,1:T(8,128)(2,1)S(1)}, u32[]{:S(2)}) copy-start(bf16[256,16]{0,1:T(8,128)(2,1)S(1)} %convolution_convert_fusion.7) | copy-start | bytes 24580
  1336.9 178.1 %reduce-scatter.5.cloned.1.call-start = ((), (), s32[]{:S(2)}) async-start(), calls=%async_computation.10 | async-start | bytes 4718592 | tf_op jit(solution)/shard_map/reduce_scatter | solution.py:273
  1353.0 510.3 %all-reduce.3.cloned.1.call-start = ((), (), s32[]{:S(2)}) async-start(), calls=%async_computation.11 | async-start | bytes 41943040 | tf_op jit(solution)/shard_map/psum | solution.py:306
  1366.6 148.4 %copy-start.33 = (bf16[256,2048]{1,0:T(8,128)(2,1)}, bf16[256,2048]{1,0:T(8,128)(2,1)S(1)}, u32[]{:S(2)}) copy-start(bf16[256,2048]{1,0:T(8,128)(2,1)S(1)} %fusion.62) | copy-start | bytes 3145732
  1425.2 89.9 %copy-start.65 = (bf16[256,16]{0,1:T(8,128)(2,1)S(1)}, bf16[256,16]{0,1:T(8,128)(2,1)}, u32[]{:S(2)}) copy-start(bf16[256,16]{0,1:T(8,128)(2,1)} %copy-done.64) | copy-start | bytes 24580
  1523.5 18.3 copy-start.3
  (105 other events, 346.5 us)
Sparse Core Ops, SparseCore 0:
  11.0 117.5 all-gather.7
  142.2 71.5 all-gather.11
  216.5 71.6 all-gather.9
  291.0 75.6 all-gather.13
  369.5 193.4 all-gather.17
  565.8 192.9 all-gather.15
  761.8 192.9 all-gather.19
  1337.0 86.2 reduce-scatter.2
  1427.4 87.6 reduce-scatter.4
  1523.6 339.5 all-reduce.2
where the time goes:
time: 1900 us; the launch traced here: 1890 us
  waiting for transfers between devices  1220 us (64%)
  matrix products  449 us (24%)
  local copies, waits for them, and re-layouts  97.1 us (5%)
  other arithmetic  72.7 us (4%)
  loops' own time  39.2 us (2%)
    psum x1, waiting for transfers between devices, per_device(): lax.psum((placed[0], placed[1], placed[2], placed[3], placed[4], placed[5...  302 us
    all_gather x1, waiting for transfers between devices, per_device(): lax.all_gather(up_weight, ('seq', 'ctx'), axis=0, tiled=True)  185 us
    all_gather x1, waiting for transfers between devices, per_device(): lax.all_gather(gate_weight, ('seq', 'ctx'), axis=0, tiled=True)  170 us
    all_gather x1, waiting for transfers between devices, per_device(): lax.all_gather(down_weight, ('seq', 'ctx'), axis=0, tiled=True)  170 us
    all_gather x1, waiting for transfers between devices, per_device(): lax.all_gather(joint_weight, ('seq', 'ctx'), axis=0, tiled=True)  115 us
    dot_general x15, matrix products, against(): lax.dot_general(left, right, (((1,), (1,)), ((), ())), preferred_element_...  99.6 us
    dot_general x15, matrix products, product(): return jnp.dot(left, right, preferred_element_type=jnp.float32)  96.3 us
    reduce_scatter x1, waiting for transfers between devices, per_device(): lax.psum_scatter(value_terms.astype(jnp.bfloat16), 'ctx', scatter_dimensi...  87.7 us
  transfers between devices with their start and end apart: 10, of which 10 were waited for; matrix products, arithmetic and copies ran while one was open for 11% of the time, Pallas kernels for 0%

commit v1 on v0

v1 whole, which is shorter than its diff:
```python
import functools

import jax
import jax.numpy as jnp
from jax import lax
from jax.experimental import pallas as pl
from jax.experimental.pallas import tpu as pltpu
from jax.sharding import Mesh, PartitionSpec as P

HEADS = 16
KV_HEADS = 8
HEAD_DIM = 128
WINDOW = 1024
FIRST_DOC = 1536
RANK = 16
PAD = 128
TP = 4

epsilon = 1e-06
rotary_base = 1000000.0
masked_score = -1e30

BF = jnp.bfloat16
F32 = jnp.float32
MIB = 1024 * 1024


def dot(left, right):
    return jnp.dot(left, right, preferred_element_type=F32)


def dot_t(left, right):
    return lax.dot_general(left, right, (((1,), (1,)), ((), ())), preferred_element_type=F32)


def t_dot(left, right):
    return lax.dot_general(left, right, (((0,), (0,)), ((), ())), preferred_element_type=F32)


def params(mib, grid=0):
    extra = {"dimension_semantics": ("arbitrary",) * grid} if grid else {}
    return pltpu.CompilerParams(vmem_limit_bytes=mib * MIB, **extra)


def cost(flops, nbytes, trans=0):
    return pl.CostEstimate(flops=int(flops), bytes_accessed=int(nbytes), transcendentals=int(trans))


VM = pl.BlockSpec(memory_space=pltpu.VMEM)
SM = pl.BlockSpec(memory_space=pltpu.SMEM)
ANY = pl.BlockSpec(memory_space=pl.ANY)


def half_range(side, h, span, length):
    start = span * h if side == 0 else length - span * (h + 1)
    return (start, start + span)


def may_see(q, k):
    grain = 64
    for q0 in range(q[0], q[1], grain):
        for k0 in range(k[0], k[1], grain):
            same = (q0 >= FIRST_DOC) == (k0 >= FIRST_DOC)
            if same and k0 < q0 + grain and q0 - (k0 + grain - 1) < WINDOW:
                return True
    return False


def key_plan(halves, span, length):
    slots = []
    for shift in list(range(halves - 1, 0, -1)) + list(range(-1, -halves, -1)):
        for side in (0, 1):
            pairs = []
            for h in range(halves):
                source = h - shift
                if not 0 <= source < halves:
                    continue
                wanted = half_range(side, source, span, length)
                if any(may_see(half_range(s, h, span, length), wanted) for s in (0, 1)):
                    pairs.append((source, h))
            if pairs:
                slots.append((shift, side, tuple(pairs)))
    tile = min(256, span)
    step = 128
    ranges = []
    for i in range(2 * span // tile):
        low, high = (1 << 30, 0)
        for h in range(halves):
            side, inside = divmod(i * tile, span)
            base = half_range(side, h, span, length)[0] + inside
            held = []
            for shift, key_side, pairs in slots:
                held.append(
                    half_range(key_side, h - shift, span, length) if (h - shift, h) in pairs else None
                )
            held += [half_range(s, h, span, length) for s in (0, 1)]
            for index, region in enumerate(held):
                if region is None:
                    continue
                for offset in range(0, span, step):
                    block = (region[0] + offset, region[0] + min(offset + step, span))
                    if may_see((base, base + tile), block):
                        low = min(low, index * span + offset)
                        high = max(high, index * span + offset + step)
        ranges.append((low, min(high, (len(slots) + 2) * span)))
    return (slots, tile, ranges)


def place_rows(me, r, rows):
    half = rows // 2
    other = me ^ r
    first = pl.multiple_of(other * half, half)
    second = pl.multiple_of(TP * half + (TP - 1 - other) * half, half)
    return ((0, first), (half, second))


def qkv_kernel(me_ref, x0, x1, x2, x3, w_ref, jr_ref, cos_ref, sin_ref, q_ref, kv_ref):
    me = me_ref[0]
    rows, wide = x0.shape
    d = wide - PAD
    half = rows // 2
    nq = q_ref.shape[1] // HEAD_DIM
    nk = kv_ref.shape[1] // HEAD_DIM // 2
    for r, x_ref in enumerate((x0, x1, x2, x3)):
        joined = dot(x_ref[:, :d], w_ref[...]) + dot(x_ref[:, d:], jr_ref[...])
        for source, target in place_rows(me, r, rows):
            part = joined[source : source + half]
            cosine = cos_ref[pl.ds(target, half), :]
            sine = sin_ref[pl.ds(target, half), :]
            for head in range(nq + nk):
                u = part[:, head * HEAD_DIM : (head + 1) * HEAD_DIM]
                turned = (u * cosine + pltpu.roll(u, HEAD_DIM // 2, 1) * sine).astype(BF)
                if head < nq:
                    q_ref[pl.ds(target, half), head * HEAD_DIM : (head + 1) * HEAD_DIM] = turned
                else:
                    at = head - nq
                    kv_ref[pl.ds(target, half), at * HEAD_DIM : (at + 1) * HEAD_DIM] = turned
            kv_ref[pl.ds(target, half), nk * HEAD_DIM :] = part[:, (nq + nk) * HEAD_DIM :].astype(BF)


def head_columns(ref, rows, first, count):
    return jnp.concatenate(
        [ref[rows, (first + i) * HEAD_DIM : (first + i + 1) * HEAD_DIM] for i in range(count)], axis=0
    )


def bias_of(qpos_ref, kpos_ref, rows, low, high, group):
    distance = qpos_ref[rows, :] - kpos_ref[:, low:high]
    bias = jnp.where((distance >= 0) & (distance < WINDOW), 0.0, masked_score).astype(F32)
    return jnp.concatenate([bias] * group, axis=0)


def attend_kernel(tile, ranges, me_ref, q_ref, kv_ref, qpos_ref, kpos_ref, mixed_ref, lse_ref, held):
    me = me_ref[0]
    rows = mixed_ref.shape[1]
    half = rows // 2
    nk = kv_ref.shape[1] // HEAD_DIM // 2
    group = q_ref.shape[1] // HEAD_DIM // nk
    scale = HEAD_DIM ** (-0.5)
    for i, (low, high) in enumerate(ranges):
        here = slice(i * tile, (i + 1) * tile)
        bias = bias_of(qpos_ref, kpos_ref, here, low, high, group)
        for head in range(nk):
            q = head_columns(q_ref, here, head * group, group)
            k = kv_ref[low:high, head * HEAD_DIM : (head + 1) * HEAD_DIM]
            v = kv_ref[low:high, (nk + head) * HEAD_DIM : (nk + head + 1) * HEAD_DIM]
            scores = dot_t(q, k) * scale + bias
            largest = jnp.max(scores, axis=-1, keepdims=True)
            raised = jnp.exp(scores - largest)
            total = jnp.sum(raised, axis=-1, keepdims=True)
            out = dot((raised * (1.0 / total)).astype(BF), v).astype(BF)
            lse = largest + jnp.log(total)
            for g in range(group):
                at = head * group + g
                held[here, at * HEAD_DIM : (at + 1) * HEAD_DIM] = out[g * tile : (g + 1) * tile]
                lse_ref[here, at : at + 1] = lse[g * tile : (g + 1) * tile]
    for r in range(TP):
        for source, target in place_rows(me, r, rows):
            mixed_ref[r, source : source + half, :] = held[pl.ds(target, half), :]


def attend_back_kernel(
    tile,
    ranges,
    me_ref,
    q_ref,
    kv_ref,
    qpos_ref,
    kpos_ref,
    lse_ref,
    mixed_ref,
    d0,
    d1,
    d2,
    d3,
    cos_ref,
    sin_ref,
    dq_ref,
    dkv_ref,
    dslot_ref,
    held,
    given,
    total_ref,
):
    me = me_ref[0]
    rows = mixed_ref.shape[1]
    half = rows // 2
    nk = kv_ref.shape[1] // HEAD_DIM // 2
    group = q_ref.shape[1] // HEAD_DIM // nk
    scale = HEAD_DIM ** (-0.5)
    for r, d_ref in enumerate((d0, d1, d2, d3)):
        for source, target in place_rows(me, r, rows):
            held[pl.ds(target, half), :] = mixed_ref[r, source : source + half, :]
            given[pl.ds(target, half), :] = d_ref[source : source + half, :]
    total_ref[...] = jnp.zeros_like(total_ref)
    for i, (low, high) in enumerate(ranges):
        here = slice(i * tile, (i + 1) * tile)
        bias = bias_of(qpos_ref, kpos_ref, here, low, high, group)
        cosine = cos_ref[here, :]
        sine = sin_ref[here, :]
        for head in range(nk):
            key_columns = slice(head * HEAD_DIM, (head + 1) * HEAD_DIM)
            value_columns = slice((nk + head) * HEAD_DIM, (nk + head + 1) * HEAD_DIM)
            q = head_columns(q_ref, here, head * group, group)
            out = head_columns(held, here, head * group, group)
            delta = head_columns(given, here, head * group, group)
            lse = jnp.concatenate(
                [lse_ref[here, head * group + g : head * group + g + 1] for g in range(group)], axis=0
            )
            k = kv_ref[low:high, key_columns]
            v = kv_ref[low:high, value_columns]
            chances = jnp.exp(dot_t(q, k) * scale + bias - lse)
            inner = jnp.sum(out.astype(F32) * delta.astype(F32), axis=-1, keepdims=True)
            raw = (chances * (dot_t(delta, v) - inner) * scale).astype(BF)
            dq = dot(raw, k)
            for g in range(group):
                at = head * group + g
                e = dq[g * tile : (g + 1) * tile]
                back = e * cosine - pltpu.roll(e, HEAD_DIM // 2, 1) * sine
                dq_ref[here, at * HEAD_DIM : (at + 1) * HEAD_DIM] = back.astype(BF)
            total_ref[low:high, key_columns] += t_dot(raw, q)
            total_ref[low:high, value_columns] += t_dot(chances.astype(BF), delta)
    extra = dslot_ref.shape[0]
    dslot_ref[...] = total_ref[:extra, :].astype(BF)
    dkv_ref[...] = total_ref[extra:, :]


def out_kernel(
    me_ref, m_ref, w_ref, olt_ref, or_ref, x_ref, gain_ref, lgu_ref, aug_ref, res_ref, oi_ref, acc, inner
):
    r = pl.program_id(0)
    d = x_ref.shape[1]

    @pl.when(r == 0)
    def _():
        acc[...] = x_ref[...].astype(F32)
        inner[...] = jnp.zeros_like(inner)

    m = m_ref[0]
    acc[...] += dot(m, w_ref[...])
    inner[...] += dot_t(m, olt_ref[...])

    @pl.when(r == TP - 1)
    def _():
        low = inner[...].astype(BF)
        oi_ref[...] = low
        residual = acc[...] + dot(low, or_ref[...])
        res_ref[...] = residual
        factor = lax.rsqrt(jnp.mean(residual * residual, axis=-1, keepdims=True) + epsilon)
        second = (residual * factor * gain_ref[...]).astype(BF)
        aug_ref[:, :d] = second
        aug_ref[:, d:] = dot_t(second, lgu_ref[...]).astype(BF)


def out_back_kernel(
    me_ref,
    p0,
    p1,
    p2,
    p3,
    dy_ref,
    res_ref,
    gain_ref,
    or_ref,
    olt_ref,
    oi_ref,
    w_ref,
    m_ref,
    dmix_ref,
    dres_ref,
    tor_ref,
    tol_ref,
    branch,
    inner,
):
    r = pl.program_id(0)

    @pl.when(r == 0)
    def _():
        gain = gain_ref[...]
        incoming = (
            p0[...].astype(F32) + p1[...].astype(F32) + p2[...].astype(F32) + p3[...].astype(F32)
        )
        v = res_ref[...]
        factor = lax.rsqrt(jnp.mean(v * v, axis=-1, keepdims=True) + epsilon)
        scaled = incoming * gain
        back = factor * scaled - v * (factor * factor * factor) * jnp.mean(
            scaled * v, axis=-1, keepdims=True
        )
        delta = dy_ref[...].astype(F32) + back
        dres_ref[...] = delta
        low = delta.astype(BF)
        branch[...] = low
        inner[...] = dot_t(low, or_ref[...]).astype(BF)
        tor_ref[...] = t_dot(oi_ref[...], low)

    dmix_ref[0] = (dot_t(branch[...], w_ref[...]) + dot(inner[...], olt_ref[...])).astype(BF)
    tol_ref[...] = t_dot(inner[...], m_ref[0])


def feed_kernel(
    x0,
    x1,
    x2,
    x3,
    y0,
    y1,
    y2,
    y3,
    gate_ref,
    up_ref,
    down_ref,
    dlt_ref,
    rg_ref,
    ru_ref,
    dr_ref,
    lgu_ref,
    o0,
    o1,
    o2,
    o3,
    s0,
    s1,
    s2,
    s3,
    tdl_ref,
    tgr_ref,
    tur_ref,
    tlast_ref,
    x_all,
    y_all,
    acc_out,
    acc_second,
    acc_inner,
    tails,
    sem,
):
    j = pl.program_id(0)
    rows = x0.shape[0]
    d = acc_out.shape[1]

    @pl.when(j == 0)
    def _():
        copies = []
        for r, ref in enumerate((x0, x1, x2, x3)):
            copies.append(pltpu.make_async_copy(ref, x_all.at[pl.ds(r * rows, rows), :], sem.at[r]))
        for r, ref in enumerate((y0, y1, y2, y3)):
            copies.append(
                pltpu.make_async_copy(ref, y_all.at[pl.ds(r * rows, rows), :], sem.at[TP + r])
            )
        for copy in copies:
            copy.start()
        acc_out[...] = jnp.zeros_like(acc_out)
        acc_second[...] = jnp.zeros_like(acc_second)
        acc_inner[...] = jnp.zeros_like(acc_inner)
        for copy in copies:
            copy.wait()
        tails[...] = x_all[:, d:] + y_all[:, d:]

    block = gate_ref.shape[-1]
    gate_w = gate_ref[...].reshape(d, block)
    up_w = up_ref[...].reshape(d, block)
    down_w = down_ref[...].reshape(block, d)
    dlt, rg, ru = (dlt_ref[...], rg_ref[...], ru_ref[...])
    term_dl = jnp.zeros((PAD, block), F32)
    term_g = jnp.zeros((PAD, block), F32)
    term_u = jnp.zeros((PAD, block), F32)
    take = min(512, TP * rows)
    for start in range(0, TP * rows, take):
        here = slice(start, start + take)
        x = x_all[here, :d]
        y = y_all[here, :d]
        xi = x_all[here, d:]
        yi = y_all[here, d:]
        gate = dot(x, gate_w) + dot(xi, rg)
        up = dot(x, up_w) + dot(xi, ru)
        delta = dot_t(y, down_w) + dot(yi, dlt)
        sigmoid = jax.nn.sigmoid(gate)
        silu = gate * sigmoid
        act = (silu * up).astype(BF)
        delta_gate = (delta * up * sigmoid * (1.0 + gate * (1.0 - sigmoid))).astype(BF)
        delta_up = (delta * silu).astype(BF)
        acc_out[here, :] += dot(act, down_w)
        acc_second[here, :] += dot_t(delta_gate, gate_w) + dot_t(delta_up, up_w)
        acc_inner[here, :] += dot_t(act, dlt) + dot_t(delta_gate, rg) + dot_t(delta_up, ru)
        tail = tails[here, :]
        term_dl += t_dot(tail, act)
        term_g += t_dot(tail, delta_gate)
        term_u += t_dot(tail, delta_up)
    tdl_ref[...] = term_dl[:RANK]
    tgr_ref[...] = term_g[RANK : 2 * RANK]
    tur_ref[...] = term_u[2 * RANK : 3 * RANK]

    @pl.when(j == pl.num_programs(0) - 1)
    def _():
        inner = acc_inner[...].astype(BF)
        term_y = t_dot(inner, y_all[:, :d])
        tlast_ref[0] = term_y[:RANK]
        term_x = t_dot(inner, x_all[:, :d])
        tlast_ref[1] = term_x[RANK : 2 * RANK]
        tlast_ref[2] = term_x[2 * RANK : 3 * RANK]
        for r, (o_ref, s_ref) in enumerate(zip((o0, o1, o2, o3), (s0, s1, s2, s3))):
            here = slice(r * rows, (r + 1) * rows)
            part = inner[here]
            s_ref[...] = (acc_second[here, :] + dot(part, lgu_ref[...])).astype(BF)
            o_ref[...] = (acc_out[here, :] + dot(part, dr_ref[...])).astype(BF)


def joint_back_kernel(
    sides,
    me_ref,
    dq_ref,
    dkv_ref,
    *rest,
):
    extra = rest[: len(sides)]
    (cos_ref, sin_ref, w_ref, jr_ref, jlt_ref, x0, x1, x2, x3) = rest[len(sides) : len(sides) + 9]
    (f0, f1, f2, f3, tjr_ref, tjl_ref, keys, dj) = rest[len(sides) + 9 :]
    me = me_ref[0]
    rows, wide = x0.shape
    d = wide - PAD
    half = rows // 2
    span = TP * half
    nk = dkv_ref.shape[1] // HEAD_DIM // 2
    query_width = dq_ref.shape[1]
    for side in (0, 1):
        here = slice(side * span, (side + 1) * span)
        total = dkv_ref[here, :]
        for ref, owner in zip(extra, sides):
            if owner == side:
                total = total + ref[...].astype(F32)
        for head in range(nk):
            e = total[:, head * HEAD_DIM : (head + 1) * HEAD_DIM]
            back = e * cos_ref[here, :] - pltpu.roll(e, HEAD_DIM // 2, 1) * sin_ref[here, :]
            keys[here, head * HEAD_DIM : (head + 1) * HEAD_DIM] = back.astype(BF)
        keys[here, nk * HEAD_DIM :] = total[:, nk * HEAD_DIM :].astype(BF)
    for r in range(TP):
        for source, target in place_rows(me, r, rows):
            to = slice(r * rows + source, r * rows + source + half)
            dj[to, :query_width] = dq_ref[pl.ds(target, half), :]
            dj[to, query_width:] = keys[pl.ds(target, half), :]
    term_r = jnp.zeros((PAD, dj.shape[1]), F32)
    term_l = jnp.zeros((PAD, d), F32)
    for r, (x_ref, f_ref) in enumerate(zip((x0, x1, x2, x3), (f0, f1, f2, f3))):
        part = dj[r * rows : (r + 1) * rows, :]
        inner = dot_t(part, jr_ref[...]).astype(BF)
        f_ref[...] = (dot_t(part, w_ref[...]) + dot(inner, jlt_ref[...])).astype(BF)
        term_r += t_dot(x_ref[:, d:], part)
        term_l += t_dot(inner, x_ref[:, :d])
    tjr_ref[...] = term_r[:RANK]
    tjl_ref[...] = term_l[:RANK]


def shape(dims, dtype=BF):
    return jax.ShapeDtypeStruct(dims, dtype)


def swap(value, r):
    return lax.ppermute(value, "t", [(i, i ^ r) for i in range(TP)])


def norm_back(values, gain, incoming):
    factor = lax.rsqrt(jnp.mean(values * values, axis=-1, keepdims=True) + epsilon)
    scaled = incoming * gain
    return factor * scaled - values * (factor * factor * factor) * jnp.mean(
        scaled * values, axis=-1, keepdims=True
    )


def per_device(
    hidden,
    out_grad,
    norm_first,
    norm_second,
    joint_weight,
    out_weight,
    gate_weight,
    up_weight,
    down_weight,
    joint_left,
    joint_right,
    out_left,
    out_right,
    gate_left,
    gate_right,
    up_left,
    up_right,
    down_left,
    down_right,
    doc_lengths,
    adapter_ids,
):
    seqs = lax.axis_size("s")
    halves = lax.axis_size("h")
    groups = seqs * halves
    rows, d = hidden.shape[1:]
    half = rows // 2
    span = TP * half
    tokens = TP * rows
    length = rows * TP * halves
    strip = joint_weight.shape[0]
    ff = gate_weight.shape[1]
    own_ff = down_weight.shape[0]
    slice_ff = groups * own_ff
    wide = d + PAD
    nq = HEADS // TP
    nk = KV_HEADS // TP
    qw = nq * HEAD_DIM
    kw = nk * HEAD_DIM
    cols = qw + 2 * kw
    me = lax.axis_index("t")
    h = lax.axis_index("h")
    me_ref = me.reshape(1).astype(jnp.int32)
    slots, tile, ranges = key_plan(halves, span, length)

    q_end = HEADS * HEAD_DIM
    k_end = q_end + KV_HEADS * HEAD_DIM
    joint_cut = jnp.concatenate(
        [
            joint_weight[:, :q_end].reshape(strip, TP, qw),
            joint_weight[:, q_end:k_end].reshape(strip, TP, kw),
            joint_weight[:, k_end:].reshape(strip, TP, kw),
        ],
        axis=2,
    ).transpose(1, 0, 2)
    joint_cut = lax.all_to_all(joint_cut, "t", 0, 0, tiled=True).reshape(TP * strip, cols)
    joint_w = lax.all_gather(joint_cut, ("s", "h"), axis=0, tiled=True)

    adapter = adapter_ids[0]

    def pick(factor):
        return lax.dynamic_index_in_dim(factor, adapter, 0, keepdims=False)

    def pick_left(factor):
        return pick(jnp.swapaxes(factor, 1, 2))

    def padded(value, first):
        return jnp.pad(value, ((first, PAD - first - value.shape[0]), (0, 0)))

    def ff_slice(value):
        return lax.dynamic_index_in_dim(
            value.reshape(RANK, groups, TP, own_ff), me, 2, keepdims=False
        ).reshape(RANK, slice_ff)

    jr = pick(joint_right)
    jr_own = jnp.concatenate(
        [
            lax.dynamic_slice_in_dim(jr[:, :q_end], me * qw, qw, 1),
            lax.dynamic_slice_in_dim(jr[:, q_end:k_end], me * kw, kw, 1),
            lax.dynamic_slice_in_dim(jr[:, k_end:], me * kw, kw, 1),
        ],
        axis=1,
    )
    jr_pad = padded(jr_own, 0)
    jlt_pad = padded(pick_left(joint_left), 0)
    olt = pick_left(out_left)
    orr = pick(out_right)
    lgu = jnp.pad(
        jnp.concatenate([pick_left(gate_left), pick_left(up_left)], axis=0),
        ((RANK, PAD - 3 * RANK), (0, 0)),
    )
    rg = padded(ff_slice(pick(gate_right)), RANK)
    ru = padded(ff_slice(pick(up_right)), 2 * RANK)
    dlt = padded(ff_slice(pick_left(down_left)), 0)
    dr_pad = padded(pick(down_right), 0)

    index = jnp.arange(span, dtype=jnp.int32)

    def side_places(side, at):
        return (span * at if side == 0 else length - span * (at + 1)) + index

    ends = jnp.cumsum(doc_lengths[0])

    def marked(places):
        documents = jnp.sum((places[:, None] >= ends[None, :]).astype(jnp.int32), axis=1)
        return places + documents * (4 * length)

    own_places = jnp.concatenate([side_places(0, h), side_places(1, h)])
    own_marks = marked(own_places)
    slot_marks = []
    for shift, side, pairs in slots:
        valid = functools.reduce(jnp.logical_or, [h == target for _, target in pairs])
        slot_marks.append(jnp.where(valid, marked(side_places(side, h - shift)), 1 << 29))
    key_marks = jnp.concatenate(slot_marks + [own_marks])[None, :]
    query_marks = own_marks[:, None]
    inverse = rotary_base ** (-jnp.arange(HEAD_DIM // 2, dtype=F32) * 2.0 / HEAD_DIM)
    angles = own_places.astype(F32)[:, None] * inverse[None, :]
    cosine = jnp.concatenate([jnp.cos(angles)] * 2, axis=1)
    sine = jnp.sin(angles)
    sine = jnp.concatenate([-sine, sine], axis=1)

    x_own = hidden[0]
    x32 = x_own.astype(F32)
    first = (
        x32 * lax.rsqrt(jnp.mean(x32 * x32, axis=-1, keepdims=True) + epsilon) * norm_first
    ).astype(BF)
    first_aug = jnp.concatenate([first, dot_t(first, jlt_pad).astype(BF)], axis=1)
    firsts = [first_aug] + [swap(first_aug, r) for r in (1, 2, 3)]

    feed_cut = jnp.stack([gate_weight, up_weight]).reshape(2, strip, groups, TP, own_ff)
    feed_cut = feed_cut.transpose(3, 0, 1, 2, 4).reshape(TP, 2, strip, slice_ff)
    feed_cut = lax.all_to_all(feed_cut, "t", 0, 0, tiled=True)
    feed_cut = feed_cut.transpose(1, 0, 2, 3).reshape(2, TP * strip, slice_ff)

    q, kv = pl.pallas_call(
        qkv_kernel,
        out_shape=(shape((tokens, qw)), shape((tokens, 2 * kw))),
        in_specs=[SM] + [VM] * 8,
        out_specs=(VM, VM),
        compiler_params=params(48),
        cost_estimate=cost(2 * tokens * wide * cols, 10 * MIB),
        name="qkv",
    )(me_ref, *firsts, joint_w, jr_pad, cosine, sine)

    pieces = [
        lax.ppermute(kv[side * span : (side + 1) * span], "h", pairs) for shift, side, pairs in slots
    ]
    kv_all = jnp.concatenate(pieces + [kv], axis=0)
    key_rows = kv_all.shape[0]
    pairs_done = sum((high - low) * tile for low, high in ranges) * nq

    out_w = lax.all_gather(out_weight, ("s", "h", "t"), axis=0, tiled=True)
    feed_w = lax.all_gather(feed_cut[None], ("s", "h"), axis=0, tiled=True)
    down_w = lax.all_gather(down_weight[None], ("s", "h"), axis=0, tiled=True)

    mixed, lse = pl.pallas_call(
        functools.partial(attend_kernel, tile, ranges),
        out_shape=(shape((TP, rows, qw)), shape((tokens, nq), F32)),
        in_specs=[SM] + [VM] * 4,
        out_specs=(VM, VM),
        scratch_shapes=[pltpu.VMEM((tokens, qw), BF)],
        compiler_params=params(48),
        cost_estimate=cost(4 * pairs_done * HEAD_DIM, 6 * MIB, pairs_done),
        name="attend",
    )(me_ref, q, kv_all, query_marks, key_marks)

    mine = jnp.stack([mixed[0]] + [swap(mixed[r], r) for r in (1, 2, 3)])

    second_aug, residual, out_inner = pl.pallas_call(
        out_kernel,
        grid_spec=pltpu.PrefetchScalarGridSpec(
            num_scalar_prefetch=1,
            grid=(TP,),
            in_specs=[
                pl.BlockSpec((1, rows, qw), lambda r, m: (r, 0, 0)),
                pl.BlockSpec((qw, d), lambda r, m: (m[0] ^ r, 0)),
                pl.BlockSpec((RANK, qw), lambda r, m: (0, m[0] ^ r)),
                pl.BlockSpec((RANK, d), lambda r, m: (0, 0)),
                pl.BlockSpec((rows, d), lambda r, m: (0, 0)),
                pl.BlockSpec((1, d), lambda r, m: (0, 0)),
                pl.BlockSpec((PAD, d), lambda r, m: (0, 0)),
            ],
            out_specs=[
                pl.BlockSpec((rows, wide), lambda r, m: (0, 0)),
                pl.BlockSpec((rows, d), lambda r, m: (0, 0)),
                pl.BlockSpec((rows, RANK), lambda r, m: (0, 0)),
            ],
            scratch_shapes=[pltpu.VMEM((rows, d), F32), pltpu.VMEM((rows, RANK), F32)],
        ),
        out_shape=(shape((rows, wide)), shape((rows, d), F32), shape((rows, RANK))),
        compiler_params=params(48, 1),
        cost_estimate=cost(2 * rows * d * d, 12 * MIB),
        name="out",
    )(me_ref, mine, out_w, olt, orr, x_own, norm_second[None], lgu)

    dy = out_grad[0]
    dy_aug = jnp.concatenate([dy, dot_t(dy, dr_pad).astype(BF)], axis=1)
    dys = [dy_aug] + [swap(dy_aug, r) for r in (1, 2, 3)]
    seconds = [second_aug] + [swap(second_aug, r) for r in (1, 2, 3)]

    block = max(256, own_ff)
    per = block // own_ff
    steps = slice_ff // block
    fixed2 = lambda j: (0, 0)
    term_spec = pl.BlockSpec((RANK, block), lambda j: (0, j))
    low_spec = pl.BlockSpec((PAD, block), lambda j: (0, j))
    whole = pl.BlockSpec((rows, d), fixed2, pipeline_mode=pl.Buffered(1))
    fed = pl.pallas_call(
        feed_kernel,
        grid=(steps,),
        in_specs=[ANY] * 8
        + [
            pl.BlockSpec((groups, 1, TP * strip, block), lambda j: (0, 0, 0, j)),
            pl.BlockSpec((groups, 1, TP * strip, block), lambda j: (0, 1, 0, j)),
            pl.BlockSpec((per, own_ff, d), lambda j: (j, 0, 0)),
            low_spec,
            low_spec,
            low_spec,
            pl.BlockSpec((PAD, d), fixed2, pipeline_mode=pl.Buffered(1)),
            pl.BlockSpec((PAD, d), fixed2, pipeline_mode=pl.Buffered(1)),
        ],
        out_specs=[whole] * 8
        + [term_spec] * 3
        + [pl.BlockSpec((3, RANK, d), lambda j: (0, 0, 0), pipeline_mode=pl.Buffered(1))],
        out_shape=[shape((rows, d))] * 8
        + [shape((RANK, slice_ff), F32)] * 3
        + [shape((3, RANK, d), F32)],
        scratch_shapes=[
            pltpu.VMEM((tokens, wide), BF),
            pltpu.VMEM((tokens, wide), BF),
            pltpu.VMEM((tokens, d), F32),
            pltpu.VMEM((tokens, d), F32),
            pltpu.VMEM((tokens, PAD), F32),
            pltpu.VMEM((tokens, PAD), BF),
            pltpu.SemaphoreType.DMA((2 * TP,)),
        ],
        compiler_params=params(60, 1),
        cost_estimate=cost(2 * tokens * d * slice_ff * 6, 50 * MIB),
        name="feed",
    )(*seconds, *dys, feed_w, feed_w, down_w, dlt, rg, ru, dr_pad, lgu)
    out_parts, second_parts = (fed[:4], fed[4:8])
    term_dl, term_gr, term_ur, term_last = fed[8:]

    second_got = [second_parts[0]] + [swap(second_parts[r], r) for r in (1, 2, 3)]

    dmix, delta_residual, term_or, term_ol = pl.pallas_call(
        out_back_kernel,
        grid_spec=pltpu.PrefetchScalarGridSpec(
            num_scalar_prefetch=1,
            grid=(TP,),
            in_specs=[pl.BlockSpec((rows, d), lambda r, m: (0, 0))] * 6
            + [
                pl.BlockSpec((1, d), lambda r, m: (0, 0)),
                pl.BlockSpec((RANK, d), lambda r, m: (0, 0)),
                pl.BlockSpec((RANK, qw), lambda r, m: (0, m[0] ^ r)),
                pl.BlockSpec((rows, RANK), lambda r, m: (0, 0)),
                pl.BlockSpec((qw, d), lambda r, m: (m[0] ^ r, 0)),
                pl.BlockSpec((1, rows, qw), lambda r, m: (r, 0, 0)),
            ],
            out_specs=[
                pl.BlockSpec((1, rows, qw), lambda r, m: (r, 0, 0)),
                pl.BlockSpec((rows, d), lambda r, m: (0, 0)),
                pl.BlockSpec((RANK, d), lambda r, m: (0, 0)),
                pl.BlockSpec((RANK, qw), lambda r, m: (0, m[0] ^ r)),
            ],
            scratch_shapes=[pltpu.VMEM((rows, d), BF), pltpu.VMEM((rows, RANK), BF)],
        ),
        out_shape=(
            shape((TP, rows, qw)),
            shape((rows, d), F32),
            shape((RANK, d), F32),
            shape((RANK, d), F32),
        ),
        compiler_params=params(48, 1),
        cost_estimate=cost(2 * rows * d * d, 16 * MIB),
        name="out_back",
    )(me_ref, *second_got, dy, residual, norm_second[None], orr, olt, out_inner, out_w, mine)

    deltas = [dmix[0]] + [swap(dmix[r], r) for r in (1, 2, 3)]

    out_got = [out_parts[0]] + [swap(out_parts[r], r) for r in (1, 2, 3)]
    layer_output = (
        residual
        + (out_got[0].astype(F32) + out_got[1].astype(F32))
        + (out_got[2].astype(F32) + out_got[3].astype(F32))
    ).astype(BF)[None]

    by_slice = jnp.concatenate([term_gr, term_ur, term_dl], axis=0).astype(BF)
    by_slice = lax.psum_scatter(by_slice, "h", scatter_dimension=0, tiled=True)
    by_rows = jnp.concatenate([term_last.reshape(3 * RANK, d), term_or, term_ol], axis=0).astype(BF)
    by_rows = lax.psum_scatter(by_rows, ("h", "t"), scatter_dimension=0, tiled=True)
    early = lax.all_gather(jnp.concatenate([by_slice, by_rows], axis=0), ("s", "h", "t"))
    ids = lax.all_gather(adapter_ids, "s", axis=0, tiled=True)

    dq, dkv, dslot = pl.pallas_call(
        functools.partial(attend_back_kernel, tile, ranges),
        out_shape=(
            shape((tokens, qw)),
            shape((tokens, 2 * kw), F32),
            shape((key_rows - tokens, 2 * kw)),
        ),
        in_specs=[SM] + [VM] * 12,
        out_specs=(VM, VM, VM),
        scratch_shapes=[
            pltpu.VMEM((tokens, qw), BF),
            pltpu.VMEM((tokens, qw), BF),
            pltpu.VMEM((key_rows, 2 * kw), F32),
        ],
        compiler_params=params(56),
        cost_estimate=cost(10 * pairs_done * HEAD_DIM, 12 * MIB, pairs_done),
        name="attend_back",
    )(me_ref, q, kv_all, query_marks, key_marks, lse, mixed, *deltas, cosine, sine)

    returned = [
        lax.ppermute(dslot[i * span : (i + 1) * span], "h", [(b, a) for a, b in pairs])
        for i, (shift, side, pairs) in enumerate(slots)
    ]
    sides = tuple(side for _, side, _ in slots)
    back = pl.pallas_call(
        functools.partial(joint_back_kernel, sides),
        out_shape=[shape((rows, d))] * 4 + [shape((RANK, cols), F32), shape((RANK, d), F32)],
        in_specs=[SM] + [VM] * (2 + len(sides) + 9),
        out_specs=[VM] * 6,
        scratch_shapes=[pltpu.VMEM((tokens, 2 * kw), BF), pltpu.VMEM((tokens, cols), BF)],
        compiler_params=params(56),
        cost_estimate=cost(2 * tokens * d * cols, 16 * MIB),
        name="joint_back",
    )(me_ref, dq, dkv, *returned, cosine, sine, joint_w, jr_pad, jlt_pad, *firsts)
    first_parts, term_jr, term_jl = (back[:4], back[4], back[5])

    got = [first_parts[0]] + [swap(first_parts[r], r) for r in (1, 2, 3)]
    delta_first = (got[0].astype(F32) + got[1].astype(F32)) + (
        got[2].astype(F32) + got[3].astype(F32)
    )
    input_delta = (delta_residual + norm_back(x32, norm_first, delta_first)).astype(BF)[None]

    late = lax.all_gather(
        jnp.concatenate([term_jl, term_jr], axis=1).astype(BF), ("s", "h", "t")
    ).reshape(seqs, halves, TP, RANK, d + cols)

    chosen = (ids[None, :] == jnp.arange(joint_left.shape[0], dtype=jnp.int32)[:, None]).astype(F32)

    def slotted(value):
        value = value.astype(F32)
        return sum(chosen[:, i, None, None] * value[i][None] for i in range(seqs))

    early = early.reshape(seqs, halves, TP, -1, d)
    cut = 3 * RANK // halves
    by_slice = early[:, :, :, :cut].transpose(0, 2, 1, 3, 4).reshape(seqs, TP, 3, RANK, groups, own_ff)
    by_slice = by_slice.transpose(0, 2, 3, 4, 1, 5).reshape(seqs, 3, RANK, ff)
    by_rows = early[:, :, :, cut:].reshape(seqs, 5, RANK, d)
    d_gr, d_ur, d_dl = [slotted(by_slice[:, i]) for i in range(3)]
    d_dr, d_gl, d_ul, d_or, d_ol = [slotted(by_rows[:, i]) for i in range(5)]
    late = late.astype(F32)
    d_jl = slotted(jnp.sum(late[..., :d], axis=(1, 2)))
    late_r = jnp.sum(late[..., d:], axis=1).transpose(0, 2, 1, 3)
    d_jr = slotted(
        jnp.concatenate(
            [
                late_r[..., :qw].reshape(seqs, RANK, q_end),
                late_r[..., qw : qw + kw].reshape(seqs, RANK, k_end - q_end),
                late_r[..., qw + kw :].reshape(seqs, RANK, k_end - q_end),
            ],
            axis=2,
        )
    )

    def left(value):
        return jnp.swapaxes(value, 1, 2)

    return (
        layer_output,
        input_delta,
        left(d_jl),
        d_jr,
        left(d_ol),
        d_or,
        left(d_gl),
        d_gr,
        left(d_ul),
        d_ur,
        left(d_dl),
        d_dr,
    )


def solution(mesh):
    seqs, ctx = (mesh.shape["seq"], mesh.shape["ctx"])
    inner = Mesh(mesh.devices.reshape(seqs, ctx // TP, TP), ("s", "h", "t"))
    acts = P("s", ("h", "t"), None)
    weight = P(("s", "h", "t"), None)
    placed = (
        (acts, acts, P(), P())
        + (weight,) * 5
        + (P(),) * 10
        + (P("s", None), P("s"))
    )
    return jax.shard_map(
        per_device,
        mesh=inner,
        in_specs=placed,
        out_specs=(acts, acts) + (P(),) * 10,
        check_vma=False,
    )
```

time: 1900 us -> 950 us (0.50)
  waiting for transfers between devices: 1220 us -> 559 us
  matrix products: 449 us -> 0.82 us
  Pallas kernels: 0 us -> 157 us
  blocking collectives: 0 us -> 61.8 us
  loops' own time: 39.2 us -> 0 us
  other arithmetic: 72.7 us -> 44.9 us
  starting transfers between devices: 0.61 us -> 27.5 us
  local copies, waits for them, and re-layouts: 97.1 us -> 72 us
    all_gather x7 -> x6, waiting for transfers between devices: 773 us -> 133 us  [the longest x1 94.1 us: per_device(): feed_w = lax.all_gather(feed_cut[None], ('s', 'h'), axis=0, tiled=True)]
    dot_general x96 -> x2, matrix products: 449 us -> 0.82 us  [dot_t(): lax.dot_general(left, right, (((1,), (1,)), ((), ())), preferred_element_...]
    ppermute x0 -> x26, waiting for transfers between devices: none -> 374 us  [the longest x24 320 us: swap(): return lax.ppermute(value, 't', [(i, i ^ r) for i in range(TP)])]
    psum x1 -> x0, waiting for transfers between devices: 302 us -> none  [per_device(): lax.psum((placed[0], placed[1], placed[2], placed[3], placed[4], placed[5...]
    pallas_call x0 -> x7, Pallas kernels: none -> 157 us  [the longest x1 86.2 us: per_device(): pl.pallas_call(feed_kernel, grid=(steps,), in_specs=[ANY] * 8 + [pl.Block...]
    reduce_scatter x2 -> x1, waiting for transfers between devices: 137 us -> 14.5 us  [per_device(): by_slice = lax.psum_scatter(by_slice, 'h', scatter_dimension=0, tiled=True)]
    all_to_all x0 -> x2, blocking collectives: none -> 56.8 us  [the longest x1 43.1 us: per_device(): feed_cut = lax.all_to_all(feed_cut, 't', 0, 0, tiled=True)]
    another operation x2 -> x0, loops' own time: 39.2 us -> none  [the longest x1 28.3 us: per_device(): lax.map(backward_head, jnp.arange(KV_HEADS))]
  transfers between devices with their start and end apart: 10 -> 34, of which waited for: 10 -> 29; matrix products, arithmetic and copies ran while one was open for 11% -> 7% of each run, Pallas kernels for 0% -> 4%
where the time goes in v1:
time: 950 us; the launch traced here: 940 us
  waiting for transfers between devices  559 us (59%)
  Pallas kernels  157 us (17%)
  local copies, waits for them, and re-layouts  72 us (8%)
  blocking collectives  61.8 us (7%)
  other arithmetic  44.9 us (5%)
  starting transfers between devices  27.5 us (3%)
  between operations  16.9 us (2%)
    ppermute x24, waiting for transfers between devices, swap(): return lax.ppermute(value, 't', [(i, i ^ r) for i in range(TP)])  320 us
    all_gather x1, waiting for transfers between devices, per_device(): feed_w = lax.all_gather(feed_cut[None], ('s', 'h'), axis=0, tiled=True)  94.1 us
    pallas_call x1, Pallas kernels, per_device(): pl.pallas_call(feed_kernel, grid=(steps,), in_specs=[ANY] * 8 + [pl.Block...  86.2 us
    all_to_all x1, blocking collectives, per_device(): feed_cut = lax.all_to_all(feed_cut, 't', 0, 0, tiled=True)  43.1 us
    all_gather x1, waiting for transfers between devices, per_device(): lax.all_gather(jnp.concatenate([by_slice, by_rows], axis=0), ('s', 'h', '...  37.6 us
    unnamed x9, waiting for transfers between devices  37.3 us
    ppermute x1, waiting for transfers between devices, per_device(): lax.ppermute(kv[side * span:(side + 1) * span], 'h', pairs)  28.4 us
    ppermute x1, waiting for transfers between devices, per_device(): lax.ppermute(dslot[i * span:(i + 1) * span], 'h', [(b, a) for a, b in pai...  25.9 us
  transfers between devices with their start and end apart: 34, of which 29 were waited for; matrix products, arithmetic and copies ran while one was open for 7% of the time, Pallas kernels for 4%

profile of v1, /device:TPU:0, one launch (start us, length us, event | category | flops | bytes accessed | tf_op | source)
XLA Modules:
  0.0 940.5 jit_solution(7207501200969387244)
XLA Ops:
  9.5 13.6 %all_to_all.10 = bf16[4,64,1024]{2,1,0:T(8,128)(2,1)} all-to-all(bf16[4,64,1024]{2,1,0:T(8,128)(2,1)S(1)} %maximum_bitcast_fusion.1), channel_id=1, replica_groups=mesh['s'=4,'h'=2,'t'=4] {'t'}, dimensions={0} | all-to-all | bytes 1048576 | tf_op jit(solution)/shard_map/all_to_all | solution.py:546
  36.5 43.1 %all_to_all.11 = bf16[4,2,64,2048]{3,2,1,0:T(8,128)(2,1)S(1)} all-to-all(bf16[4,2,64,2048]{3,2,1,0:T(8,128)(2,1)} %reshape.311), channel_id=1, replica_groups=mesh['s'=4,'h'=2,'t'=4] {'t'}, dimensions={0} | all-to-all | bytes 4194304 | tf_op jit(solution)/shard_map/all_to_all | solution.py:622
  101.3 19.1 %collective-permute-done.x1.rest_7_ = bf16[256,2176]{1,0:T(8,128)(2,1)} collective-permute-done((bf16[256,2176]{1,0:T(8,128)(2,1)}, bf16[256,2176]{1,0:T(8,128)(2,1)}, u32[]{:S(2)}, u32[]{:S(2)}) %collective-permute-start) | collective-permute-done | bytes 1114144 | tf_op jit(solution)/shard_map/ppermute | solution.py:479
  127.9 39.0 %collective-permute-done.2.x3.rest_9_ = bf16[256,2176]{1,0:T(8,128)(2,1)} collective-permute-done((bf16[256,2176]{1,0:T(8,128)(2,1)}, bf16[256,2176]{1,0:T(8,128)(2,1)}, u32[]{:S(2)}, u32[]{:S(2)}) %collective-permute-start.2) | collective-permute-done | bytes 1114144 | tf_op jit(solution)/shard_map/ppermute | solution.py:479
  181.4 28.4 %collective-permute-done.3 = bf16[512,512]{1,0:T(8,128)(2,1)S(1)} collective-permute-done((bf16[512,512]{1,0:T(8,128)(2,1)S(1)}, bf16[512,512]{1,0:T(8,128)(2,1)S(1)}, u32[]{:S(2)}, u32[]{:S(2)}) %collective-permute-start.3) | collective-permute-done | bytes 524320 | tf_op jit(solution)/shard_map/ppermute | solution.py:636
  234.9 12.3 %collective-permute-done.6 = bf16[256,512]{1,0:T(8,128)(2,1)S(1)} collective-permute-done((bf16[256,512]{1,0:T(8,128)(2,1)S(1)}, bf16[256,512]{1,0:T(8,128)(2,1)S(1)}, u32[]{:S(2)}, u32[]{:S(2)}) %collective-permute-start.6) | collective-permute-done | bytes 262176 | tf_op jit(solution)/shard_map/ppermute | solution.py:479
  277.8 15.7 %collective-permute-done.12.y3 = bf16[256,2176]{1,0:T(8,128)(2,1)} collective-permute-done((bf16[256,2176]{1,0:T(8,128)(2,1)}, bf16[256,2176]{1,0:T(8,128)(2,1)}, u32[]{:S(2)}, u32[]{:S(2)}) %collective-permute-start.12) | collective-permute-done | bytes 1114144 | tf_op jit(solution)/shard_map/ppermute | solution.py:479
  298.2 25.7 %collective-permute-done.8.x2 = bf16[256,2176]{1,0:T(8,128)(2,1)} collective-permute-done((bf16[256,2176]{1,0:T(8,128)(2,1)}, bf16[256,2176]{1,0:T(8,128)(2,1)}, u32[]{:S(2)}, u32[]{:S(2)}) %collective-permute-start.8) | collective-permute-done | bytes 1114144 | tf_op jit(solution)/shard_map/ppermute | solution.py:479
  323.9 37.9 %collective-permute-done.9.x3 = bf16[256,2176]{1,0:T(8,128)(2,1)} collective-permute-done((bf16[256,2176]{1,0:T(8,128)(2,1)}, bf16[256,2176]{1,0:T(8,128)(2,1)}, u32[]{:S(2)}, u32[]{:S(2)}) %collective-permute-start.9) | collective-permute-done | bytes 1114144 | tf_op jit(solution)/shard_map/ppermute | solution.py:479
  361.8 94.1 %all-gather.14.cloned.1.call-done.gate_ref.up_ref = bf16[8,2,256,2048]{3,2,1,0:T(8,128)(2,1)} async-done(((bf16[1,2,256,2048]{3,2,1,0:T(8,128)(2,1)}), bf16[8,2,256,2048]{3,2,1,0:T(8,128)(2,1)}) %all-gather.14.cloned.1.call-update) | async-done | bytes 16777232 | tf_op jit(solution)/shard_map/all_gather | solution.py:643
  455.9 86.2 %feed.1 = (bf16[256,2048]{1,0:T(8,128)(2,1)}, bf16[256,2048]{1,0:T(8,128)(2,1)}, bf16[256,2048]{1,0:T(8,128)(2,1)}, bf16[256,2048]{1,0:T(8,128)(2,1)}, bf16[256,...) custom-call(bf16[256,2176]{1,0:T(8,128)(2,1)} %get-tuple-element.48., ...), custom_call_target="tpu_custom_call" | custom-call | flops 51539607552 | bytes 52428800 | tf_op jit(solution)/shard_map/feed/pallas_call | solution.py:698
  545.6 22.0 %collective-permute-done.16.p1 = bf16[256,2048]{1,0:T(8,128)(2,1)S(1)} collective-permute-done((bf16[256,2048]{1,0:T(8,128)(2,1)}, bf16[256,2048]{1,0:T(8,128)(2,1)S(1)}, u32[]{:S(2)}, u32[]{:S(2)}) %collective-permute-start.16) | collective-permute-done | bytes 1048608 | tf_op jit(solution)/shard_map/ppermute | solution.py:479
  569.8 21.5 %collective-permute-done.18.p3 = bf16[256,2048]{1,0:T(8,128)(2,1)S(1)} collective-permute-done((bf16[256,2048]{1,0:T(8,128)(2,1)}, bf16[256,2048]{1,0:T(8,128)(2,1)S(1)}, u32[]{:S(2)}, u32[]{:S(2)}) %collective-permute-start.18) | collective-permute-done | bytes 1048608 | tf_op jit(solution)/shard_map/ppermute | solution.py:479
  592.5 9.9 %out_back.1 = (bf16[4,256,512]{2,1,0:T(8,128)(2,1)S(1)}, f32[256,2048]{1,0:T(8,128)}, f32[16,2048]{1,0:T(8,128)S(1)}, f32[16,2048]{1,0:T(8,128)S(1)}) custom-call(s32[1]{0:T(128)} %bitcast.me_ref, bf16[256,2048]{1,0:T(8,128)(2,1)S(1)} %copy-done.7, bf16[256,2048]{1,0:T(8,128)(2,1)S(1)} %collective-permute-done.16.p1, ...), custom_call_target="tpu_custom_call" | custom-call | flops 2147483648 | bytes 16777216 | tf_op jit(solution)/shard_map/out_back/pallas_call | solution.py:736
  618.0 20.5 %attend_back.1 = (bf16[1024,512]{1,0:T(8,128)(2,1)}, f32[1024,512]{1,0:T(8,128)}, bf16[512,512]{1,0:T(8,128)(2,1)}) custom-call(s32[1]{0:T(128)} %bitcast.me_ref, bf16[1024,512]{1,0:T(8,128)(2,1)} %copy-done.16, bf16[1536,512]{1,0:T(8,128)(2,1)} %copy-done.13, s32[1024,1]{1,0:T(8,128)} %copy.116.qpos_ref, s32[1,1536]{1,0:T(1,128)} %copy-done.15, ...), custom_call_target="tpu_custom_call" | custom-call | flops 5704253440 | bytes 12582912 | tf_op jit(solution)/shard_map/attend_back/pallas_call | solution.py:785
  642.4 25.9 %collective-permute-done.22.rest_0_ = bf16[512,512]{1,0:T(8,128)(2,1)S(1)} collective-permute-done((bf16[512,512]{1,0:T(8,128)(2,1)}, bf16[512,512]{1,0:T(8,128)(2,1)S(1)}, u32[]{:S(2)}, u32[]{:S(2)}) %collective-permute-start.22) | collective-permute-done | bytes 524320 | tf_op jit(solution)/shard_map/ppermute | solution.py:805
  669.1 13.7 %joint_back.1 = (bf16[256,2048]{1,0:T(8,128)(2,1)}, bf16[256,2048]{1,0:T(8,128)(2,1)}, bf16[256,2048]{1,0:T(8,128)(2,1)}, bf16[256,2048]{1,0:T(8,128)(2,1)}, f32[16,1024]{1,0:T(8,128)}, /*index=5*/f32[16,2048]{1,0:T(8,128)}) custom-call(s32[1]{0:T(128)} %bitcast.me_ref, bf16[1024,512]{1,0:T(8,128)(2,1)} %get-tuple-element.61.dq_ref, ...), custom_call_target="tpu_custom_call" | custom-call | flops 4294967296 | bytes 16777216 | tf_op jit(solution)/shard_map/joint_back/pallas_call | solution.py:809
  686.6 35.8 %all-reduce.11.cloned.1.call-done = bf16[80,2048]{1,0:T(8,128)(2,1)} async-done(((bf16[80,2048]{1,0:T(8,128)(2,1)}), bf16[80,2048]{1,0:T(8,128)(2,1)}) %all-reduce.11.cloned.1.call-update) | async-done | bytes 327696
  723.3 14.5 %reduce-scatter.2.cloned.1.call-done = bf16[24,2048]{1,0:T(8,128)(2,1)} async-done(((bf16[48,2048]{1,0:T(8,128)(2,1)}), bf16[24,2048]{1,0:T(8,128)(2,1)}) %reduce-scatter.2.cloned.1.call-update) | async-done | bytes 98320 | tf_op jit(solution)/shard_map/reduce_scatter | solution.py:779
  750.8 15.7 %collective-permute-done.13 = bf16[256,2048]{1,0:T(8,128)(2,1)} collective-permute-done((bf16[256,2048]{1,0:T(8,128)(2,1)}, bf16[256,2048]{1,0:T(8,128)(2,1)}, u32[]{:S(2)}, u32[]{:S(2)}) %collective-permute-start.13) | collective-permute-done | bytes 1048608 | tf_op jit(solution)/shard_map/ppermute | solution.py:479
  770.8 23.2 %collective-permute-done.15 = bf16[256,2048]{1,0:T(8,128)(2,1)} collective-permute-done((bf16[256,2048]{1,0:T(8,128)(2,1)}, bf16[256,2048]{1,0:T(8,128)(2,1)}, u32[]{:S(2)}, u32[]{:S(2)}) %collective-permute-start.15) | collective-permute-done | bytes 1048608 | tf_op jit(solution)/shard_map/ppermute | solution.py:479
  798.1 20.0 %collective-permute-done.23 = bf16[256,2048]{1,0:T(8,128)(2,1)S(1)} collective-permute-done((bf16[256,2048]{1,0:T(8,128)(2,1)}, bf16[256,2048]{1,0:T(8,128)(2,1)S(1)}, u32[]{:S(2)}, u32[]{:S(2)}) %collective-permute-start.23) | collective-permute-done | bytes 1048608 | tf_op jit(solution)/shard_map/ppermute | solution.py:479
  826.9 22.7 %collective-permute-done.25 = bf16[256,2048]{1,0:T(8,128)(2,1)S(1)} collective-permute-done((bf16[256,2048]{1,0:T(8,128)(2,1)}, bf16[256,2048]{1,0:T(8,128)(2,1)S(1)}, u32[]{:S(2)}, u32[]{:S(2)}) %collective-permute-start.25) | collective-permute-done | bytes 1048608 | tf_op jit(solution)/shard_map/ppermute | solution.py:479
  860.0 37.6 %all-gather.20.cloned.1.call-done = bf16[32,34,2048]{2,1,0:T(8,128)(2,1)} async-done(((bf16[1,34,2048]{2,1,0:T(8,128)(2,1)}), bf16[32,34,2048]{2,1,0:T(8,128)(2,1)}) %all-gather.20.cloned.1.call-update) | async-done | bytes 4456464 | tf_op jit(solution)/shard_map/all_gather | solution.py:782
  (294 shorter events, 225.3 us)
Async XLA Ops:
  7.2 159.7 %all-gather.10.cloned.1.call-start = ((), (), s32[]{:S(2)}) async-start(), calls=%async_computation.3 | async-start | bytes 4718592 | tf_op jit(solution)/shard_map/all_gather | solution.py:547
  23.1 225.2 %all-gather.12.cloned.1.call-start = ((), (), s32[]{:S(2)}) async-start(), calls=%async_computation.4 | async-start | bytes 8650752 | tf_op jit(solution)/shard_map/all_gather | solution.py:642
  23.9 271.2 %all-gather.18.cloned.1.call-start = ((), (), s32[]{:S(2)}) async-start(), calls=%async_computation.8 | async-start | bytes 9437184 | tf_op jit(solution)/shard_map/all_gather | solution.py:644
  24.6 431.2 %all-gather.14.cloned.1.call-start = ((), (), s32[]{:S(2)}) async-start(), calls=%async_computation.5 | async-start | bytes 18874368 | tf_op jit(solution)/shard_map/all_gather | solution.py:643
  81.1 641.3 %all-reduce.11.cloned.1.call-start = ((), (), s32[]{:S(2)}) async-start(), calls=%async_computation.10 | async-start | bytes 655360
  85.9 34.5 %collective-permute-start = (bf16[256,2176]{1,0:T(8,128)(2,1)}, bf16[256,2176]{1,0:T(8,128)(2,1)}, u32[]{:S(2)}, u32[]{:S(2)}) collective-permute-start(bf16[256,2176]{1,0:T(8,128)(2,1)} %pad_maximum_fusion.x0.rest_6_), channel_id=1, source_target_pairs={{0,1},{1,0},{2,3},{3,2},{4,5},{5,4},{6,7},{7,6},{8,9},{9,8},{10,11... | collective-permute-start | bytes 3342344 | tf_op jit(solution)/shard_map/ppermute | solution.py:479
  87.0 40.8 %collective-permute-start.1 = (bf16[256,2176]{1,0:T(8,128)(2,1)}, bf16[256,2176]{1,0:T(8,128)(2,1)}, u32[]{:S(2)}, u32[]{:S(2)}) collective-permute-start(bf16[256,2176]{1,0:T(8,128)(2,1)} %pad_maximum_fusion.x0.rest_6_), channel_id=1, source_target_pairs={{0,2},{1,3},{2,0},{3,1},{4,6},{5,7},{6,4},{7,5},{8,10},{9,11},{10,... | collective-permute-start | bytes 3342344 | tf_op jit(solution)/shard_map/ppermute | solution.py:479
  87.0 79.9 %collective-permute-start.2 = (bf16[256,2176]{1,0:T(8,128)(2,1)}, bf16[256,2176]{1,0:T(8,128)(2,1)}, u32[]{:S(2)}, u32[]{:S(2)}) collective-permute-start(bf16[256,2176]{1,0:T(8,128)(2,1)} %pad_maximum_fusion.x0.rest_6_), channel_id=1, source_target_pairs={{0,3},{1,2},{2,1},{3,0},{4,7},{5,6},{6,5},{7,4},{8,11},{9,10},{10,... | collective-permute-start | bytes 3342344 | tf_op jit(solution)/shard_map/ppermute | solution.py:479
  92.3 168.6 %collective-permute-start.10 = (bf16[256,2176]{1,0:T(8,128)(2,1)}, bf16[256,2176]{1,0:T(8,128)(2,1)}, u32[]{:S(2)}, u32[]{:S(2)}) collective-permute-start(bf16[256,2176]{1,0:T(8,128)(2,1)} %pad_maximum_fusion.1.y0), channel_id=1, source_target_pairs={{0,1},{1,0},{2,3},{3,2},{4,5},{5,4},{6,7},{7,6},{8,9},{9,8},{10,11... | collective-permute-start | bytes 3342344 | tf_op jit(solution)/shard_map/ppermute | solution.py:479
  93.5 184.2 %collective-permute-start.11 = (bf16[256,2176]{1,0:T(8,128)(2,1)}, bf16[256,2176]{1,0:T(8,128)(2,1)}, u32[]{:S(2)}, u32[]{:S(2)}) collective-permute-start(bf16[256,2176]{1,0:T(8,128)(2,1)} %pad_maximum_fusion.1.y0), channel_id=1, source_target_pairs={{0,2},{1,3},{2,0},{3,1},{4,6},{5,7},{6,4},{7,5},{8,10},{9,11},{10,... | collective-permute-start | bytes 3342344 | tf_op jit(solution)/shard_map/ppermute | solution.py:479
  177.9 31.9 %collective-permute-start.3 = (bf16[512,512]{1,0:T(8,128)(2,1)S(1)}, bf16[512,512]{1,0:T(8,128)(2,1)S(1)}, u32[]{:S(2)}, u32[]{:S(2)}) collective-permute-start(bf16[512,512]{1,0:T(8,128)(2,1)S(1)} %slice.296), channel_id=1, source_target_pairs={{0,4},{1,5},{2,6},{3,7},{8,12},{9,13},{10,14},{11,15},{16,20},{17,... | collective-permute-start | bytes 1572872 | tf_op jit(solution)/shard_map/ppermute | solution.py:636
  228.5 65.0 %collective-permute-start.12 = (bf16[256,2176]{1,0:T(8,128)(2,1)}, bf16[256,2176]{1,0:T(8,128)(2,1)}, u32[]{:S(2)}, u32[]{:S(2)}) collective-permute-start(bf16[256,2176]{1,0:T(8,128)(2,1)} %pad_maximum_fusion.1.y0), channel_id=1, source_target_pairs={{0,3},{1,2},{2,1},{3,0},{4,7},{5,6},{6,5},{7,4},{8,11},{9,10},{10,... | collective-permute-start | bytes 3342344 | tf_op jit(solution)/shard_map/ppermute | solution.py:479
  260.3 37.9 %collective-permute-start.7 = (bf16[256,2176]{1,0:T(8,128)(2,1)}, bf16[256,2176]{1,0:T(8,128)(2,1)}, u32[]{:S(2)}, u32[]{:S(2)}) collective-permute-start(bf16[256,2176]{1,0:T(8,128)(2,1)} %get-tuple-element.48.x0), channel_id=1, source_target_pairs={{0,1},{1,0},{2,3},{3,2},{4,5},{5,4},{6,7},{7,6},{8,9},{9,8},{10,11... | collective-permute-start | bytes 3342344 | tf_op jit(solution)/shard_map/ppermute | solution.py:479
  261.0 62.9 %collective-permute-start.8 = (bf16[256,2176]{1,0:T(8,128)(2,1)}, bf16[256,2176]{1,0:T(8,128)(2,1)}, u32[]{:S(2)}, u32[]{:S(2)}) collective-permute-start(bf16[256,2176]{1,0:T(8,128)(2,1)} %get-tuple-element.48.x0), channel_id=1, source_target_pairs={{0,2},{1,3},{2,0},{3,1},{4,6},{5,7},{6,4},{7,5},{8,10},{9,11},{10,... | collective-permute-start | bytes 3342344 | tf_op jit(solution)/shard_map/ppermute | solution.py:479
  261.0 100.8 %collective-permute-start.9 = (bf16[256,2176]{1,0:T(8,128)(2,1)}, bf16[256,2176]{1,0:T(8,128)(2,1)}, u32[]{:S(2)}, u32[]{:S(2)}) collective-permute-start(bf16[256,2176]{1,0:T(8,128)(2,1)} %get-tuple-element.48.x0), channel_id=1, source_target_pairs={{0,3},{1,2},{2,1},{3,0},{4,7},{5,6},{6,5},{7,4},{8,11},{9,10},{10,... | collective-permute-start | bytes 3342344 | tf_op jit(solution)/shard_map/ppermute | solution.py:479
  543.6 47.7 %collective-permute-start.18 = (bf16[256,2048]{1,0:T(8,128)(2,1)}, bf16[256,2048]{1,0:T(8,128)(2,1)S(1)}, u32[]{:S(2)}, u32[]{:S(2)}) collective-permute-start(bf16[256,2048]{1,0:T(8,128)(2,1)} %get-tuple-element.56), channel_id=1, source_target_pairs={{0,3},{1,2},{2,1},{3,0},{4,7},{5,6},{6,5},{7,4},{8,11},{9,10},{10,... | collective-permute-start | bytes 3145736 | tf_op jit(solution)/shard_map/ppermute | solution.py:479
  640.6 97.1 %reduce-scatter.2.cloned.1.call-start = ((), (), s32[]{:S(2)}) async-start(), calls=%async_computation.7 | async-start | bytes 294912 | tf_op jit(solution)/shard_map/reduce_scatter | solution.py:779
  642.3 211.0 %all-gather.16.cloned.1.call-start = ((), (), s32[]{:S(2)}) async-start(), calls=%async_computation.6 | async-start | bytes 3244032 | tf_op jit(solution)/shard_map/all_gather | solution.py:827
  685.3 212.3 %all-gather.20.cloned.1.call-start = ((), (), s32[]{:S(2)}) async-start(), calls=%async_computation.9 | async-start | bytes 5406720 | tf_op jit(solution)/shard_map/all_gather | solution.py:782
  740.9 29.9 %collective-permute-start.14 = (bf16[256,2048]{1,0:T(8,128)(2,1)}, bf16[256,2048]{1,0:T(8,128)(2,1)}, u32[]{:S(2)}, u32[]{:S(2)}) collective-permute-start(bf16[256,2048]{1,0:T(8,128)(2,1)} %get-tuple-element.51), channel_id=1, source_target_pairs={{0,2},{1,3},{2,0},{3,1},{4,6},{5,7},{6,4},{7,5},{8,10},{9,11},{10,... | collective-permute-start | bytes 3145736 | tf_op jit(solution)/shard_map/ppermute | solution.py:479
  740.9 53.1 %collective-permute-start.15 = (bf16[256,2048]{1,0:T(8,128)(2,1)}, bf16[256,2048]{1,0:T(8,128)(2,1)}, u32[]{:S(2)}, u32[]{:S(2)}) collective-permute-start(bf16[256,2048]{1,0:T(8,128)(2,1)} %get-tuple-element.52), channel_id=1, source_target_pairs={{0,3},{1,2},{2,1},{3,0},{4,7},{5,6},{6,5},{7,4},{8,11},{9,10},{10,... | collective-permute-start | bytes 3145736 | tf_op jit(solution)/shard_map/ppermute | solution.py:479
  749.3 68.8 %collective-permute-start.23 = (bf16[256,2048]{1,0:T(8,128)(2,1)}, bf16[256,2048]{1,0:T(8,128)(2,1)S(1)}, u32[]{:S(2)}, u32[]{:S(2)}) collective-permute-start(bf16[256,2048]{1,0:T(8,128)(2,1)} %get-tuple-element.65), channel_id=1, source_target_pairs={{0,1},{1,0},{2,3},{3,2},{4,5},{5,4},{6,7},{7,6},{8,9},{9,8},{10,11... | collective-permute-start | bytes 3145736 | tf_op jit(solution)/shard_map/ppermute | solution.py:479
  750.8 76.1 %collective-permute-start.24 = (bf16[256,2048]{1,0:T(8,128)(2,1)}, bf16[256,2048]{1,0:T(8,128)(2,1)S(1)}, u32[]{:S(2)}, u32[]{:S(2)}) collective-permute-start(bf16[256,2048]{1,0:T(8,128)(2,1)} %get-tuple-element.66), channel_id=1, source_target_pairs={{0,2},{1,3},{2,0},{3,1},{4,6},{5,7},{6,4},{7,5},{8,10},{9,11},{10,... | collective-permute-start | bytes 3145736 | tf_op jit(solution)/shard_map/ppermute | solution.py:479
  766.5 83.1 %collective-permute-start.25 = (bf16[256,2048]{1,0:T(8,128)(2,1)}, bf16[256,2048]{1,0:T(8,128)(2,1)S(1)}, u32[]{:S(2)}, u32[]{:S(2)}) collective-permute-start(bf16[256,2048]{1,0:T(8,128)(2,1)} %get-tuple-element.67), channel_id=1, source_target_pairs={{0,3},{1,2},{2,1},{3,0},{4,7},{5,6},{6,5},{7,4},{8,11},{9,10},{10,... | collective-permute-start | bytes 3145736 | tf_op jit(solution)/shard_map/ppermute | solution.py:479
  (52 other events, 1104.1 us)
Sparse Core Ops, SparseCore 0:
  23.3 54.2 all-gather.9
  80.5 119.7 all-gather.11
  202.2 92.7 all-gather.17
  297.4 158.4 all-gather.13
  640.8 81.5 all-reduce.10
  724.6 13.1 reduce-scatter.1
  741.7 84.6 all-gather.15
  830.3 67.2 all-gather.19

commit v2 on v1

--- a/solution.py
+++ b/solution.py
@@ -114,15 +114,94 @@
     return ((0, first), (half, second))
 
 
-def qkv_kernel(me_ref, x0, x1, x2, x3, w_ref, jr_ref, cos_ref, sin_ref, q_ref, kv_ref):
+def cut_kernel(wide, me_ref, joint_ref, gate_ref, up_ref, *outs):
     me = me_ref[0]
+    joints, feeds = (outs[:TP], outs[TP:])
+    cols = joints[0].shape[1]
+    kw = KV_HEADS // TP * HEAD_DIM
+    qw = cols - 2 * kw
+    for r in range(TP):
+        other = me ^ r
+        start = 0
+        base = 0
+        for width, count in ((qw, TP), (kw, TP), (kw, TP)):
+            joints[r][:, start : start + width] = joint_ref[
+                :, pl.ds(pl.multiple_of(base + other * width, HEAD_DIM), width)
+            ]
+            start += width
+            base += width * count
+        for g in range(feeds[r].shape[2] // wide if feeds else 0):
+            at = pl.ds(pl.multiple_of((g * TP + other) * wide, wide), wide)
+            feeds[r][0, :, g * wide : (g + 1) * wide] = gate_ref[:, at]
+            feeds[r][1, :, g * wide : (g + 1) * wide] = up_ref[:, at]
+
+
+def natural_kernel(count, me_ref, *refs):
+    parts, (out_ref, sem) = (refs[:count], refs[-2:])
+    me = me_ref[0]
+    strip = parts[0].shape[-2]
+    copies = []
+    for r, ref in enumerate(parts):
+        rows = pl.ds(pl.multiple_of((me ^ r) * strip, strip), strip)
+        to = out_ref.at[rows, :] if len(ref.shape) == 2 else out_ref.at[:, rows, :]
+        copies.append(pltpu.make_async_copy(ref, to, sem.at[r]))
+    for copy in copies:
+        copy.start()
+    for copy in copies:
+        copy.wait()
+
+
+def strips_kernel(layout, strip, me_ref, *refs):
+    out_ref, sem = refs[-2:]
+    me, place = (me_ref[0], me_ref[1])
+    copies = []
+    for ref, (r, groups) in zip(refs, layout):
+        for i, group in enumerate(groups):
+            row = pl.multiple_of(((place ^ group) * TP + (me ^ r)) * strip, strip)
+            copies.append(
+                pltpu.make_async_copy(
+                    ref.at[pl.ds(i * strip, strip), :],
+                    out_ref.at[pl.ds(row, strip), :],
+                    sem.at[len(copies)],
+                )
+            )
+    for copy in copies:
+        copy.start()
+    for copy in copies:
+        copy.wait()
+
+
+def load_pieces(place, pieces, target, sem):
+    strip = pieces[0].shape[0]
+    if len(pieces) == 1:
+        copies = [pltpu.make_async_copy(pieces[0], target, sem.at[0])]
+        copies[0].start()
+        return copies
+    copies = []
+    for r, ref in enumerate(pieces):
+        rows = pl.ds(pl.multiple_of((place ^ r) * strip, strip), strip)
+        copies.append(pltpu.make_async_copy(ref, target.at[rows, :], sem.at[r]))
+    for copy in copies:
+        copy.start()
+    return copies
+
+
+def qkv_kernel(count, me_ref, *refs):
+    pieces = refs[:count]
+    (x0, x1, x2, x3a, x3b, jr_ref, cos_ref, sin_ref) = refs[count : count + 8]
+    (q_ref, kv_ref, w_ref, sem) = refs[-4:]
+    me = me_ref[0]
+    copies = load_pieces(me_ref[1], pieces, w_ref, sem)
     rows, wide = x0.shape
     d = wide - PAD
     half = rows // 2
     nq = q_ref.shape[1] // HEAD_DIM
     nk = kv_ref.shape[1] // HEAD_DIM // 2
-    for r, x_ref in enumerate((x0, x1, x2, x3)):
-        joined = dot(x_ref[:, :d], w_ref[...]) + dot(x_ref[:, d:], jr_ref[...])
+    for copy in copies:
+        copy.wait()
+    for r, x_refs in enumerate(((x0,), (x1,), (x2,), (x3a, x3b))):
+        x = jnp.concatenate([ref[...] for ref in x_refs], axis=0)
+        joined = dot(x[:, :d], w_ref[...]) + dot(x[:, d:], jr_ref[...])
         for source, target in place_rows(me, r, rows):
             part = joined[source : source + half]
             cosine = cos_ref[pl.ds(target, half), :]
@@ -286,20 +365,22 @@
     oi_ref,
     w_ref,
     m_ref,
+    tdr_ref,
     dmix_ref,
     dres_ref,
-    tor_ref,
-    tol_ref,
     branch,
     inner,
+    terms,
 ):
     r = pl.program_id(0)
+    rows, d = dy_ref.shape
+    width = d // TP
 
     @pl.when(r == 0)
     def _():
         gain = gain_ref[...]
-        incoming = (
-            p0[...].astype(F32) + p1[...].astype(F32) + p2[...].astype(F32) + p3[...].astype(F32)
+        incoming = (p0[:rows].astype(F32) + p1[:rows].astype(F32)) + (
+            p2[:rows].astype(F32) + p3[:rows].astype(F32)
         )
         v = res_ref[...]
         factor = lax.rsqrt(jnp.mean(v * v, axis=-1, keepdims=True) + epsilon)
@@ -312,130 +393,166 @@
         low = delta.astype(BF)
         branch[...] = low
         inner[...] = dot_t(low, or_ref[...]).astype(BF)
-        tor_ref[...] = t_dot(oi_ref[...], low)
-
-    dmix_ref[0] = (dot_t(branch[...], w_ref[...]) + dot(inner[...], olt_ref[...])).astype(BF)
-    tol_ref[...] = t_dot(inner[...], m_ref[0])
-
-
-def feed_kernel(
-    x0,
-    x1,
-    x2,
-    x3,
-    y0,
-    y1,
-    y2,
-    y3,
-    gate_ref,
-    up_ref,
-    down_ref,
-    dlt_ref,
-    rg_ref,
-    ru_ref,
-    dr_ref,
-    lgu_ref,
-    o0,
-    o1,
-    o2,
-    o3,
-    s0,
-    s1,
-    s2,
-    s3,
-    tdl_ref,
-    tgr_ref,
-    tur_ref,
-    tlast_ref,
-    x_all,
-    y_all,
-    acc_out,
-    acc_second,
-    acc_inner,
-    tails,
-    sem,
-):
-    j = pl.program_id(0)
-    rows = x0.shape[0]
-    d = acc_out.shape[1]
-
-    @pl.when(j == 0)
+        terms[:RANK] = tdr_ref[...]
+        terms[RANK:] = t_dot(oi_ref[...], low)
+
+    dmix_ref[0, :rows] = (dot_t(branch[...], w_ref[...]) + dot(inner[...], olt_ref[...])).astype(BF)
+    at = pl.ds(pl.multiple_of((me_ref[0] ^ r) * width, width), width)
+    dmix_ref[0, rows : rows + 2 * RANK] = terms[:, at].astype(BF)
+    dmix_ref[0, rows + 2 * RANK :] = t_dot(inner[...], m_ref[0]).astype(BF)
+
+
+def load_rows(refs, stores, sem):
+    copies = []
+    stores = stores if isinstance(stores, tuple) else (stores,)
+    for index, store in enumerate(stores):
+        at = 0
+        for ref in refs[5 * index : 5 * index + 5]:
+            copies.append(
+                pltpu.make_async_copy(
+                    ref, store.at[pl.ds(at, ref.shape[0]), :], sem.at[len(copies)]
+                )
+            )
+            at += ref.shape[0]
+    for copy in copies:
+        copy.start()
+    for copy in copies:
+        copy.wait()
+
+
+def gate_kernel(*refs):
+    xs, refs = (refs[:5], refs[5:])
+    (gate_ref, up_ref, rg_ref, ru_ref, act_ref, silu_ref, slope_ref, x_all, sem) = refs
+    d = x_all.shape[1] - PAD
+
+    @pl.when(pl.program_id(0) == 0)
     def _():
-        copies = []
-        for r, ref in enumerate((x0, x1, x2, x3)):
-            copies.append(pltpu.make_async_copy(ref, x_all.at[pl.ds(r * rows, rows), :], sem.at[r]))
-        for r, ref in enumerate((y0, y1, y2, y3)):
-            copies.append(
-                pltpu.make_async_copy(ref, y_all.at[pl.ds(r * rows, rows), :], sem.at[TP + r])
-            )
-        for copy in copies:
-            copy.start()
-        acc_out[...] = jnp.zeros_like(acc_out)
-        acc_second[...] = jnp.zeros_like(acc_second)
-        acc_inner[...] = jnp.zeros_like(acc_inner)
-        for copy in copies:
-            copy.wait()
-        tails[...] = x_all[:, d:] + y_all[:, d:]
+        load_rows(xs, x_all, sem)
 
     block = gate_ref.shape[-1]
     gate_w = gate_ref[...].reshape(d, block)
     up_w = up_ref[...].reshape(d, block)
-    down_w = down_ref[...].reshape(block, d)
+    count = x_all.shape[0]
+    take = min(512, count)
+    for start in range(0, count, take):
+        here = slice(start, start + take)
+        x = x_all[here, :d]
+        xi = x_all[here, d:]
+        gate = dot(x, gate_w) + dot(xi, rg_ref[...])
+        up = dot(x, up_w) + dot(xi, ru_ref[...])
+        sigmoid = jax.nn.sigmoid(gate)
+        silu = gate * sigmoid
+        act_ref[here, :] = (silu * up).astype(BF)
+        silu_ref[here, :] = silu.astype(BF)
+        slope_ref[here, :] = (up * sigmoid * (1.0 + gate * (1.0 - sigmoid))).astype(BF)
+
+
+def feed_back_kernel(me_ref, *refs):
+    xs, ys, refs = (refs[:5], refs[5:10], refs[10:])
+    (gate_ref, up_ref, down_ref, silu_ref, slope_ref, dlt_ref, rg_ref, ru_ref, lgu_ref, *refs) = refs
+    (s0, s1, s2, s3, tgr_ref, tur_ref, x_all, y_all, acc_second, acc_inner, sem) = refs
+    me = me_ref[0]
+    j = pl.program_id(0)
+    d = acc_second.shape[1]
+    rows = x_all.shape[0] // TP
+
+    @pl.when(j == 0)
+    def _():
+        load_rows(list(xs) + list(ys), (x_all, y_all), sem)
+        acc_second[...] = jnp.zeros_like(acc_second)
+        acc_inner[...] = jnp.zeros_like(acc_inner)
+
+    block = gate_ref.shape[-1]
+    gate_w = gate_ref[...].reshape(d, block)
+    up_w = up_ref[...].reshape(d, block)
+    down_w = down_ref[...]
     dlt, rg, ru = (dlt_ref[...], rg_ref[...], ru_ref[...])
-    term_dl = jnp.zeros((PAD, block), F32)
     term_g = jnp.zeros((PAD, block), F32)
     term_u = jnp.zeros((PAD, block), F32)
     take = min(512, TP * rows)
     for start in range(0, TP * rows, take):
         here = slice(start, start + take)
-        x = x_all[here, :d]
-        y = y_all[here, :d]
-        xi = x_all[here, d:]
-        yi = y_all[here, d:]
-        gate = dot(x, gate_w) + dot(xi, rg)
-        up = dot(x, up_w) + dot(xi, ru)
-        delta = dot_t(y, down_w) + dot(yi, dlt)
-        sigmoid = jax.nn.sigmoid(gate)
-        silu = gate * sigmoid
-        act = (silu * up).astype(BF)
-        delta_gate = (delta * up * sigmoid * (1.0 + gate * (1.0 - sigmoid))).astype(BF)
-        delta_up = (delta * silu).astype(BF)
-        acc_out[here, :] += dot(act, down_w)
+        delta = dot_t(y_all[here, :d], down_w) + dot(y_all[here, d:], dlt)
+        delta_gate = (delta * slope_ref[here, :].astype(F32)).astype(BF)
+        delta_up = (delta * silu_ref[here, :].astype(F32)).astype(BF)
         acc_second[here, :] += dot_t(delta_gate, gate_w) + dot_t(delta_up, up_w)
-        acc_inner[here, :] += dot_t(act, dlt) + dot_t(delta_gate, rg) + dot_t(delta_up, ru)
-        tail = tails[here, :]
-        term_dl += t_dot(tail, act)
+        acc_inner[here, :] += dot_t(delta_gate, rg) + dot_t(delta_up, ru)
+        tail = x_all[here, d:]
         term_g += t_dot(tail, delta_gate)
         term_u += t_dot(tail, delta_up)
-    tdl_ref[...] = term_dl[:RANK]
     tgr_ref[...] = term_g[RANK : 2 * RANK]
     tur_ref[...] = term_u[2 * RANK : 3 * RANK]
 
     @pl.when(j == pl.num_programs(0) - 1)
     def _():
         inner = acc_inner[...].astype(BF)
-        term_y = t_dot(inner, y_all[:, :d])
-        tlast_ref[0] = term_y[:RANK]
-        term_x = t_dot(inner, x_all[:, :d])
-        tlast_ref[1] = term_x[RANK : 2 * RANK]
-        tlast_ref[2] = term_x[2 * RANK : 3 * RANK]
-        for r, (o_ref, s_ref) in enumerate(zip((o0, o1, o2, o3), (s0, s1, s2, s3))):
+        width = d // TP
+        for r, s_ref in enumerate((s0, s1, s2, s3)):
             here = slice(r * rows, (r + 1) * rows)
-            part = inner[here]
-            s_ref[...] = (acc_second[here, :] + dot(part, lgu_ref[...])).astype(BF)
-            o_ref[...] = (acc_out[here, :] + dot(part, dr_ref[...])).astype(BF)
-
-
-def joint_back_kernel(
-    sides,
-    me_ref,
-    dq_ref,
-    dkv_ref,
-    *rest,
-):
-    extra = rest[: len(sides)]
-    (cos_ref, sin_ref, w_ref, jr_ref, jlt_ref, x0, x1, x2, x3) = rest[len(sides) : len(sides) + 9]
-    (f0, f1, f2, f3, tjr_ref, tjl_ref, keys, dj) = rest[len(sides) + 9 :]
+            s_ref[:rows, :] = (acc_second[here, :] + dot(inner[here], lgu_ref[...])).astype(BF)
+            at = pl.ds(pl.multiple_of((me ^ r) * width, width), width)
+            term = t_dot(inner, x_all[:, at]).astype(BF)
+            s_ref[rows:, :width] = term[RANK : 2 * RANK]
+            s_ref[rows:, width : 2 * width] = term[2 * RANK : 3 * RANK]
+            s_ref[rows:, 2 * width :] = jnp.zeros((RANK, d - 2 * width), BF)
+
+
+def down_kernel(*refs):
+    ys, refs = (refs[:5], refs[5:])
+    (down_ref, act_ref, dlt_ref, dr_ref, o0, o1, o2, o3, tdl_ref, tdr_ref, *refs) = refs
+    (y_all, acc, acc_inner, sem) = refs
+    j = pl.program_id(0)
+    rows = o0.shape[0]
+    d = acc.shape[1]
+
+    @pl.when(j == 0)
+    def _():
+        load_rows(ys, y_all, sem)
+        acc[...] = jnp.zeros_like(acc)
+        acc_inner[...] = jnp.zeros_like(acc_inner)
+
+    acc[...] += dot(act_ref[...], down_ref[...])
+    acc_inner[...] += dot_t(act_ref[...], dlt_ref[...])
+    tdl_ref[...] = t_dot(y_all[:, d:], act_ref[...])[:RANK]
+
+    @pl.when(j == pl.num_programs(0) - 1)
+    def _():
+        inner = acc_inner[...].astype(BF)
+        tdr_ref[...] = t_dot(inner, y_all[:, :d])[:RANK]
+        for r, o_ref in enumerate((o0, o1, o2, o3)):
+            here = slice(r * rows, (r + 1) * rows)
+            o_ref[...] = (acc[here, :] + dot(inner[here], dr_ref[...])).astype(BF)
+
+
+def slot_kernel(plan, adapters, got_ref, *outs):
+    seqs, halves = got_ref.shape[:2]
+    marks = []
+    for i in range(seqs):
+        ids = got_ref[i, 0, 0, :, -PAD:].astype(F32)
+        marks.append(
+            [
+                jnp.max(jnp.where(ids == float(e), 1.0, 0.0), axis=1, keepdims=True)
+                for e in range(adapters)
+            ]
+        )
+    for out_ref, parts in zip(outs, plan):
+        for to, width, sources in parts:
+            values = []
+            for i in range(seqs):
+                total = None
+                for h, t, at in sources:
+                    part = got_ref[i, h, t, :, at : at + width].astype(F32)
+                    total = part if total is None else total + part
+                values.append(total)
+            for e in range(adapters):
+                out_ref[e, :, to : to + width] = sum(
+                    marks[i][e] * values[i] for i in range(seqs)
+                )
+
+
+def joint_terms_kernel(sides, me_ref, dq_ref, dkv_ref, *refs):
+    extra, refs = (refs[: len(sides)], refs[len(sides) :])
+    (cos_ref, sin_ref, jr_ref, x0, x1, x2, x3a, x3b, dj, inner_ref, tjr_ref, tjl_ref, keys) = refs
     me = me_ref[0]
     rows, wide = x0.shape
     d = wide - PAD
@@ -461,22 +578,80 @@
             dj[to, query_width:] = keys[pl.ds(target, half), :]
     term_r = jnp.zeros((PAD, dj.shape[1]), F32)
     term_l = jnp.zeros((PAD, d), F32)
-    for r, (x_ref, f_ref) in enumerate(zip((x0, x1, x2, x3), (f0, f1, f2, f3))):
-        part = dj[r * rows : (r + 1) * rows, :]
-        inner = dot_t(part, jr_ref[...]).astype(BF)
-        f_ref[...] = (dot_t(part, w_ref[...]) + dot(inner, jlt_ref[...])).astype(BF)
-        term_r += t_dot(x_ref[:, d:], part)
-        term_l += t_dot(inner, x_ref[:, :d])
+    for r, x_refs in enumerate(((x0,), (x1,), (x2,), (x3a, x3b))):
+        x = jnp.concatenate([ref[...] for ref in x_refs], axis=0)
+        here = slice(r * rows, (r + 1) * rows)
+        inner = dot_t(dj[here, :], jr_ref[...]).astype(BF)
+        inner_ref[here, :] = inner
+        term_r += t_dot(x[:, d:], dj[here, :])
+        term_l += t_dot(inner, x[:, :d])
     tjr_ref[...] = term_r[:RANK]
     tjl_ref[...] = term_l[:RANK]
 
 
+def joint_back_kernel(me_ref, *refs):
+    pieces = refs[:-9]
+    (dj, inner, jlt_ref, f0, f1, f2, f3, w_ref, sem) = refs[-9:]
+    for copy in load_pieces(me_ref[1], pieces, w_ref, sem):
+        copy.wait()
+    rows = f0.shape[0]
+    for r, f_ref in enumerate((f0, f1, f2, f3)):
+        here = slice(r * rows, (r + 1) * rows)
+        f_ref[...] = (dot_t(dj[here, :], w_ref[...]) + dot(inner[here, :], jlt_ref[...])).astype(BF)
+
+
 def shape(dims, dtype=BF):
     return jax.ShapeDtypeStruct(dims, dtype)
 
 
 def swap(value, r):
     return lax.ppermute(value, "t", [(i, i ^ r) for i in range(TP)])
+
+
+def near_far(value):
+    return (swap(value, 1), swap(value, 2))
+
+
+def corners(near, far):
+    half = near.shape[0] // 2
+    return (swap(near[:half], 2), swap(far[half:], 1))
+
+
+def sent(parts):
+    return [parts[0]] + [swap(parts[r], r) for r in range(1, TP)]
+
+
+def after(value, *others):
+    return lax.optimization_barrier((value, others))[0]
+
+
+def together(*values):
+    return lax.optimization_barrier(values)
+
+
+def flip(value, axis, bit):
+    size = lax.axis_size(axis)
+    return lax.ppermute(value, axis, [(i, i ^ bit) for i in range(size)])
+
+
+def collect_first(value, seqs, halves):
+    held = {0: value}
+    for i in range(halves.bit_length() - 1):
+        held[1 << i] = flip(value, "h", 1 << i)
+    for i in range(1, seqs.bit_length() - 1):
+        held[halves << i] = flip(value, "s", 1 << i)
+    return held
+
+
+def collect_rest(held, seqs, halves):
+    held = dict(held)
+    bits = [("h", 1 << i, 1 << i) for i in range(halves.bit_length() - 1)]
+    bits += [("s", 1 << i, halves << i) for i in range(1, seqs.bit_length() - 1)]
+    for axis, bit, offset in bits:
+        for index in sorted(held):
+            if index < offset and index | offset not in held:
+                held[index | offset] = flip(held[index], axis, bit)
+    return held
 
 
 def norm_back(values, gain, incoming):
@@ -530,32 +705,62 @@
     cols = qw + 2 * kw
     me = lax.axis_index("t")
     h = lax.axis_index("h")
-    me_ref = me.reshape(1).astype(jnp.int32)
+    s_at = lax.axis_index("s")
+    place = s_at * halves + h
+    me_ref = jnp.stack([me, place]).astype(jnp.int32)
     slots, tile, ranges = key_plan(halves, span, length)
+
+    adapter = adapter_ids[0]
+
+    def pick(factor):
+        return lax.dynamic_index_in_dim(factor, adapter, 0, keepdims=False)
+
+    def pick_left(factor):
+        return pick(jnp.swapaxes(factor, 1, 2))
+
+    def padded(value, first):
+        return jnp.pad(value, ((first, PAD - first - value.shape[0]), (0, 0)))
 
     q_end = HEADS * HEAD_DIM
     k_end = q_end + KV_HEADS * HEAD_DIM
-    joint_cut = jnp.concatenate(
-        [
-            joint_weight[:, :q_end].reshape(strip, TP, qw),
-            joint_weight[:, q_end:k_end].reshape(strip, TP, kw),
-            joint_weight[:, k_end:].reshape(strip, TP, kw),
-        ],
-        axis=2,
-    ).transpose(1, 0, 2)
-    joint_cut = lax.all_to_all(joint_cut, "t", 0, 0, tiled=True).reshape(TP * strip, cols)
-    joint_w = lax.all_gather(joint_cut, ("s", "h"), axis=0, tiled=True)
-
-    adapter = adapter_ids[0]
-
-    def pick(factor):
-        return lax.dynamic_index_in_dim(factor, adapter, 0, keepdims=False)
-
-    def pick_left(factor):
-        return pick(jnp.swapaxes(factor, 1, 2))
-
-    def padded(value, first):
-        return jnp.pad(value, ((first, PAD - first - value.shape[0]), (0, 0)))
+    x_own = hidden[0]
+    x32 = x_own.astype(F32)
+    first = (
+        x32 * lax.rsqrt(jnp.mean(x32 * x32, axis=-1, keepdims=True) + epsilon) * norm_first
+    ).astype(BF)
+    jlt_pad = padded(pick_left(joint_left), 0)
+    first_aug = jnp.concatenate([first, dot_t(first, jlt_pad).astype(BF)], axis=1)
+
+    whole_lanes = own_ff % HEAD_DIM == 0
+    feed_shapes = [shape((2, strip, slice_ff))] * (TP if whole_lanes else 0)
+    cut = pl.pallas_call(
+        functools.partial(cut_kernel, own_ff),
+        out_shape=[shape((strip, cols))] * TP + feed_shapes,
+        in_specs=[SM] + [VM] * 3,
+        out_specs=[VM] * (TP + len(feed_shapes)),
+        compiler_params=params(24),
+        cost_estimate=cost(0, 6 * MIB),
+        name="cut",
+    )(me_ref, joint_weight, gate_weight, up_weight)
+    feed_parts = cut[TP:]
+    if not whole_lanes:
+        both = jnp.stack([gate_weight, up_weight]).reshape(2, strip, groups, TP, own_ff)
+        feed_parts = [
+            lax.dynamic_index_in_dim(both, me ^ r, 3, keepdims=False).reshape(2, strip, slice_ff)
+            for r in range(TP)
+        ]
+
+    def natural(parts, out, *others):
+        return pl.pallas_call(
+            functools.partial(natural_kernel, TP),
+            out_shape=out,
+            in_specs=[SM] + [ANY] * (TP + len(others)),
+            out_specs=ANY,
+            scratch_shapes=[pltpu.SemaphoreType.DMA((TP,))],
+            compiler_params=params(8),
+            cost_estimate=cost(0, 4 * MIB),
+            name="natural",
+        )(me_ref, *parts, *others)
 
     def ff_slice(value):
         return lax.dynamic_index_in_dim(
@@ -572,7 +777,6 @@
         axis=1,
     )
     jr_pad = padded(jr_own, 0)
-    jlt_pad = padded(pick_left(joint_left), 0)
     olt = pick_left(out_left)
     orr = pick(out_right)
     lgu = jnp.pad(
@@ -582,7 +786,6 @@
     rg = padded(ff_slice(pick(gate_right)), RANK)
     ru = padded(ff_slice(pick(up_right)), 2 * RANK)
     dlt = padded(ff_slice(pick_left(down_left)), 0)
-    dr_pad = padded(pick(down_right), 0)
 
     index = jnp.arange(span, dtype=jnp.int32)
 
@@ -609,39 +812,50 @@
     sine = jnp.sin(angles)
     sine = jnp.concatenate([-sine, sine], axis=1)
 
-    x_own = hidden[0]
-    x32 = x_own.astype(F32)
-    first = (
-        x32 * lax.rsqrt(jnp.mean(x32 * x32, axis=-1, keepdims=True) + epsilon) * norm_first
-    ).astype(BF)
-    first_aug = jnp.concatenate([first, dot_t(first, jlt_pad).astype(BF)], axis=1)
-    firsts = [first_aug] + [swap(first_aug, r) for r in (1, 2, 3)]
-
-    feed_cut = jnp.stack([gate_weight, up_weight]).reshape(2, strip, groups, TP, own_ff)
-    feed_cut = feed_cut.transpose(3, 0, 1, 2, 4).reshape(TP, 2, strip, slice_ff)
-    feed_cut = lax.all_to_all(feed_cut, "t", 0, 0, tiled=True)
-    feed_cut = feed_cut.transpose(1, 0, 2, 3).reshape(2, TP * strip, slice_ff)
+    dy = out_grad[0]
+    dr_pad = padded(pick(down_right), 0)
+    dy_aug = jnp.concatenate([dy, dot_t(dy, dr_pad).astype(BF)], axis=1)
+
+    joint_sent, out_held = together(sent(cut[:TP]), collect_first(out_weight, seqs, halves))
+    joint_cut = natural(joint_sent, shape((TP * strip, cols)))
+    joint_w = lax.all_gather(joint_cut, ("s", "h"), axis=0, tiled=True)
+
+    feed_parts, first_aug, out_held, _ = together(feed_parts, first_aug, out_held, joint_cut)
+    feed_sent, first_got, (rg, ru, dlt, lgu, olt, orr, dr_pad, dy_aug) = together(
+        sent(feed_parts), near_far(first_aug), (rg, ru, dlt, lgu, olt, orr, dr_pad, dy_aug)
+    )
+    out_held = collect_rest(after(out_held, first_got), seqs, halves)
+    feed_cut = natural(feed_sent, shape((2, TP * strip, slice_ff)))
+    feed_w = lax.all_gather(feed_cut[None], ("s", "h"), axis=0, tiled=True)
+
+    first_ends, out_held = together(corners(*first_got), out_held)
+    held_groups = tuple(sorted(out_held))
+    out_mine = jnp.concatenate([out_held[i] for i in held_groups], axis=0)
+    firsts = [first_aug, *first_got, *first_ends]
 
     q, kv = pl.pallas_call(
-        qkv_kernel,
+        functools.partial(qkv_kernel, 1),
         out_shape=(shape((tokens, qw)), shape((tokens, 2 * kw))),
-        in_specs=[SM] + [VM] * 8,
+        in_specs=[SM] + [ANY] + [VM] * 8,
         out_specs=(VM, VM),
+        scratch_shapes=[pltpu.VMEM((d, cols), BF), pltpu.SemaphoreType.DMA((1,))],
         compiler_params=params(48),
         cost_estimate=cost(2 * tokens * wide * cols, 10 * MIB),
         name="qkv",
-    )(me_ref, *firsts, joint_w, jr_pad, cosine, sine)
-
-    pieces = [
-        lax.ppermute(kv[side * span : (side + 1) * span], "h", pairs) for shift, side, pairs in slots
-    ]
+    )(me_ref, joint_w, *firsts, jr_pad, cosine, sine)
+
+    out_mine = after(out_mine, q)
+    pieces, out_got, own_core = together(
+        [
+            lax.ppermute(kv[side * span : (side + 1) * span], "h", pairs)
+            for shift, side, pairs in slots
+        ],
+        near_far(out_mine),
+        flip(out_mine, "s", 1),
+    )
     kv_all = jnp.concatenate(pieces + [kv], axis=0)
     key_rows = kv_all.shape[0]
     pairs_done = sum((high - low) * tile for low, high in ranges) * nq
-
-    out_w = lax.all_gather(out_weight, ("s", "h", "t"), axis=0, tiled=True)
-    feed_w = lax.all_gather(feed_cut[None], ("s", "h"), axis=0, tiled=True)
-    down_w = lax.all_gather(down_weight[None], ("s", "h"), axis=0, tiled=True)
 
     mixed, lse = pl.pallas_call(
         functools.partial(attend_kernel, tile, ranges),
@@ -654,7 +868,28 @@
         name="attend",
     )(me_ref, q, kv_all, query_marks, key_marks)
 
-    mine = jnp.stack([mixed[0]] + [swap(mixed[r], r) for r in (1, 2, 3)])
+    out_got = after(out_got, mixed)
+    mine, out_ends, out_cores = together(
+        sent(mixed), corners(*out_got), [flip(block, "s", 1) for block in out_got]
+    )
+    down_w = lax.all_gather(after(down_weight, mixed), ("s", "h"), axis=0, tiled=True)
+    mine = jnp.stack(mine)
+    end_cores = together(*[flip(block, "s", 1) for block in out_ends])
+    out_blocks = [out_mine, *out_got, *out_ends, own_core, *out_cores, *end_cores]
+    cut_at = len(held_groups) // 2
+    layout = [(0, held_groups), (1, held_groups), (2, held_groups)]
+    layout += [(3, held_groups[:cut_at]), (3, held_groups[cut_at:])]
+    layout += [(r, tuple(i | halves for i in some)) for r, some in layout]
+    out_w = pl.pallas_call(
+        functools.partial(strips_kernel, tuple(layout), strip),
+        out_shape=shape((d, d)),
+        in_specs=[SM] + [ANY] * len(layout),
+        out_specs=ANY,
+        scratch_shapes=[pltpu.SemaphoreType.DMA((groups * TP,))],
+        compiler_params=params(8),
+        cost_estimate=cost(0, 16 * MIB),
+        name="strips",
+    )(me_ref, *out_blocks)
 
     second_aug, residual, out_inner = pl.pallas_call(
         out_kernel,
@@ -683,62 +918,143 @@
         name="out",
     )(me_ref, mine, out_w, olt, orr, x_own, norm_second[None], lgu)
 
-    dy = out_grad[0]
-    dy_aug = jnp.concatenate([dy, dot_t(dy, dr_pad).astype(BF)], axis=1)
-    dys = [dy_aug] + [swap(dy_aug, r) for r in (1, 2, 3)]
-    seconds = [second_aug] + [swap(second_aug, r) for r in (1, 2, 3)]
+    second_got = together(*near_far(second_aug))
+    second_ends = corners(*second_got)
+    second_ends = together(*second_ends)
+    dy_aug = after(dy_aug, second_ends)
+    dy_far = swap(dy_aug, 3)
+    dy_ends = (dy_far[: rows // 2], dy_far[rows // 2 :])
+    dy_got = near_far(dy_aug)
+    dys = [dy_aug, *dy_got, *dy_ends]
+    seconds = [second_aug, *second_got, *second_ends]
 
     block = max(256, own_ff)
-    per = block // own_ff
     steps = slice_ff // block
-    fixed2 = lambda j: (0, 0)
-    term_spec = pl.BlockSpec((RANK, block), lambda j: (0, j))
-    low_spec = pl.BlockSpec((PAD, block), lambda j: (0, j))
-    whole = pl.BlockSpec((rows, d), fixed2, pipeline_mode=pl.Buffered(1))
-    fed = pl.pallas_call(
-        feed_kernel,
+    fixed = lambda j: (0, 0)
+    column = lambda j: (0, j)
+    term_spec = pl.BlockSpec((RANK, block), column)
+    low_spec = pl.BlockSpec((PAD, block), column)
+    wide_spec = pl.BlockSpec((tokens, block), column)
+    down_spec = pl.BlockSpec((block, d), lambda j: (j, 0))
+    once = dict(pipeline_mode=pl.Buffered(1))
+    kept = pl.BlockSpec((PAD, d), fixed, **once)
+    weight_specs = [
+        pl.BlockSpec((groups, 1, TP * strip, block), lambda j: (0, 0, 0, j)),
+        pl.BlockSpec((groups, 1, TP * strip, block), lambda j: (0, 1, 0, j)),
+    ]
+    act, silu, slope = pl.pallas_call(
+        gate_kernel,
         grid=(steps,),
-        in_specs=[ANY] * 8
-        + [
-            pl.BlockSpec((groups, 1, TP * strip, block), lambda j: (0, 0, 0, j)),
-            pl.BlockSpec((groups, 1, TP * strip, block), lambda j: (0, 1, 0, j)),
-            pl.BlockSpec((per, own_ff, d), lambda j: (j, 0, 0)),
-            low_spec,
-            low_spec,
-            low_spec,
-            pl.BlockSpec((PAD, d), fixed2, pipeline_mode=pl.Buffered(1)),
-            pl.BlockSpec((PAD, d), fixed2, pipeline_mode=pl.Buffered(1)),
-        ],
-        out_specs=[whole] * 8
-        + [term_spec] * 3
-        + [pl.BlockSpec((3, RANK, d), lambda j: (0, 0, 0), pipeline_mode=pl.Buffered(1))],
-        out_shape=[shape((rows, d))] * 8
-        + [shape((RANK, slice_ff), F32)] * 3
-        + [shape((3, RANK, d), F32)],
+        in_specs=[ANY] * 5 + weight_specs + [low_spec] * 2,
+        out_specs=[wide_spec] * 3,
+        scratch_shapes=[pltpu.VMEM((tokens, wide), BF), pltpu.SemaphoreType.DMA((5,))],
+        out_shape=[shape((tokens, slice_ff))] * 3,
+        compiler_params=params(56, 1),
+        cost_estimate=cost(2 * tokens * d * slice_ff * 2, 32 * MIB),
+        name="gate",
+    )(*seconds, feed_w, feed_w, rg, ru)
+
+    tall = rows + RANK
+    back = pl.pallas_call(
+        feed_back_kernel,
+        grid=(steps,),
+        in_specs=[SM]
+        + [ANY] * 10
+        + weight_specs
+        + [down_spec]
+        + [wide_spec] * 2
+        + [low_spec] * 3
+        + [kept],
+        out_specs=[pl.BlockSpec((tall, d), fixed, **once)] * 4 + [term_spec] * 2,
         scratch_shapes=[
             pltpu.VMEM((tokens, wide), BF),
             pltpu.VMEM((tokens, wide), BF),
             pltpu.VMEM((tokens, d), F32),
+            pltpu.VMEM((tokens, PAD), F32),
+            pltpu.SemaphoreType.DMA((10,)),
+        ],
+        out_shape=[shape((tall, d))] * 4 + [shape((RANK, slice_ff), F32)] * 2,
+        compiler_params=params(60, 1),
+        cost_estimate=cost(2 * tokens * d * slice_ff * 3, 50 * MIB),
+        name="feed_back",
+    )(me_ref, *seconds, *dys, feed_w, feed_w, down_w, silu, slope, dlt, rg, ru, lgu)
+    second_parts, (term_gr, term_ur) = (back[:4], back[4:])
+
+    down = pl.pallas_call(
+        down_kernel,
+        grid=(steps,),
+        in_specs=[ANY] * 5 + [down_spec, wide_spec, low_spec, kept],
+        out_specs=[pl.BlockSpec((rows, d), fixed, **once)] * 4
+        + [term_spec, pl.BlockSpec((RANK, d), fixed)],
+        scratch_shapes=[
+            pltpu.VMEM((tokens, wide), BF),
             pltpu.VMEM((tokens, d), F32),
             pltpu.VMEM((tokens, PAD), F32),
-            pltpu.VMEM((tokens, PAD), BF),
-            pltpu.SemaphoreType.DMA((2 * TP,)),
+            pltpu.SemaphoreType.DMA((5,)),
         ],
-        compiler_params=params(60, 1),
-        cost_estimate=cost(2 * tokens * d * slice_ff * 6, 50 * MIB),
-        name="feed",
-    )(*seconds, *dys, feed_w, feed_w, down_w, dlt, rg, ru, dr_pad, lgu)
-    out_parts, second_parts = (fed[:4], fed[4:8])
-    term_dl, term_gr, term_ur, term_last = fed[8:]
-
-    second_got = [second_parts[0]] + [swap(second_parts[r], r) for r in (1, 2, 3)]
-
-    dmix, delta_residual, term_or, term_ol = pl.pallas_call(
+        out_shape=[shape((rows, d))] * 4 + [shape((RANK, slice_ff), F32), shape((RANK, d), F32)],
+        compiler_params=params(56, 1),
+        cost_estimate=cost(2 * tokens * d * slice_ff, 24 * MIB),
+        name="down",
+    )(*dys, down_w, after(act, second_parts), dlt, dr_pad)
+    out_parts, (term_dl, term_dr) = (down[:4], down[4:])
+
+    adapters = joint_left.shape[0]
+    bits = halves.bit_length() - 1
+    turned = [sum(((i >> b) & 1) << (bits - 1 - b) for b in range(bits)) for i in range(halves)]
+    share = slice_ff // halves
+
+    def by_slice(at):
+        parts = []
+        for source in range(halves):
+            first_column = turned[source] * share
+            for t in range(TP):
+                for g in range(share // own_ff):
+                    group = first_column // own_ff + g
+                    to = (group * TP + t) * own_ff
+                    parts.append((to, own_ff, ((source, t, at + g * own_ff),)))
+        return tuple(parts)
+
+    def by_t(at, size, base=0, count=halves):
+        return tuple(
+            (base + t * size, size, tuple((i, t, at) for i in range(count))) for t in range(TP)
+        )
+
+    def slotted(got, plan, widths, name):
+        return pl.pallas_call(
+            functools.partial(slot_kernel, plan, adapters),
+            out_shape=[shape((adapters, RANK, size), F32) for size in widths],
+            in_specs=[VM],
+            out_specs=[VM] * len(widths),
+            compiler_params=params(48),
+            cost_estimate=cost(adapters * seqs * RANK * sum(widths), 64 * adapters * sum(widths)),
+            name=name,
+        )(got)
+
+    def over_h(value):
+        at = 1
+        while at < halves:
+            count = value.shape[1] // 2
+            upper = (h // at) % 2
+            keep = lax.dynamic_slice_in_dim(value, upper * count, count, 1)
+            give = lax.dynamic_slice_in_dim(value, (1 - upper) * count, count, 1)
+            value = keep + flip(give.astype(BF), "h", at).astype(F32)
+            at *= 2
+        return value
+
+    id_columns = jnp.full((RANK, PAD), adapter_ids[0], F32)
+    width = d // TP
+
+    second_got, out_parts = together(sent(second_parts), out_parts)
+    second_terms = sum(part[rows:, : 2 * width].astype(F32) for part in second_got)
+
+    dmix, delta_residual = pl.pallas_call(
         out_back_kernel,
         grid_spec=pltpu.PrefetchScalarGridSpec(
             num_scalar_prefetch=1,
             grid=(TP,),
-            in_specs=[pl.BlockSpec((rows, d), lambda r, m: (0, 0))] * 6
+            in_specs=[pl.BlockSpec((tall, d), lambda r, m: (0, 0))] * 4
+            + [pl.BlockSpec((rows, d), lambda r, m: (0, 0))] * 2
             + [
                 pl.BlockSpec((1, d), lambda r, m: (0, 0)),
                 pl.BlockSpec((RANK, d), lambda r, m: (0, 0)),
@@ -746,41 +1062,36 @@
                 pl.BlockSpec((rows, RANK), lambda r, m: (0, 0)),
                 pl.BlockSpec((qw, d), lambda r, m: (m[0] ^ r, 0)),
                 pl.BlockSpec((1, rows, qw), lambda r, m: (r, 0, 0)),
+                pl.BlockSpec((RANK, d), lambda r, m: (0, 0)),
             ],
             out_specs=[
-                pl.BlockSpec((1, rows, qw), lambda r, m: (r, 0, 0)),
+                pl.BlockSpec((1, rows + 3 * RANK, qw), lambda r, m: (r, 0, 0)),
                 pl.BlockSpec((rows, d), lambda r, m: (0, 0)),
-                pl.BlockSpec((RANK, d), lambda r, m: (0, 0)),
-                pl.BlockSpec((RANK, qw), lambda r, m: (0, m[0] ^ r)),
             ],
-            scratch_shapes=[pltpu.VMEM((rows, d), BF), pltpu.VMEM((rows, RANK), BF)],
+            scratch_shapes=[
+                pltpu.VMEM((rows, d), BF),
+                pltpu.VMEM((rows, RANK), BF),
+                pltpu.VMEM((2 * RANK, d), F32),
+            ],
         ),
-        out_shape=(
-            shape((TP, rows, qw)),
-            shape((rows, d), F32),
-            shape((RANK, d), F32),
-            shape((RANK, d), F32),
-        ),
+        out_shape=(shape((TP, rows + 3 * RANK, qw)), shape((rows, d), F32)),
         compiler_params=params(48, 1),
         cost_estimate=cost(2 * rows * d * d, 16 * MIB),
         name="out_back",
-    )(me_ref, *second_got, dy, residual, norm_second[None], orr, olt, out_inner, out_w, mine)
-
-    deltas = [dmix[0]] + [swap(dmix[r], r) for r in (1, 2, 3)]
-
-    out_got = [out_parts[0]] + [swap(out_parts[r], r) for r in (1, 2, 3)]
-    layer_output = (
-        residual
-        + (out_got[0].astype(F32) + out_got[1].astype(F32))
-        + (out_got[2].astype(F32) + out_got[3].astype(F32))
-    ).astype(BF)[None]
-
-    by_slice = jnp.concatenate([term_gr, term_ur, term_dl], axis=0).astype(BF)
-    by_slice = lax.psum_scatter(by_slice, "h", scatter_dimension=0, tiled=True)
-    by_rows = jnp.concatenate([term_last.reshape(3 * RANK, d), term_or, term_ol], axis=0).astype(BF)
-    by_rows = lax.psum_scatter(by_rows, ("h", "t"), scatter_dimension=0, tiled=True)
-    early = lax.all_gather(jnp.concatenate([by_slice, by_rows], axis=0), ("s", "h", "t"))
-    ids = lax.all_gather(adapter_ids, "s", axis=0, tiled=True)
+    )(me_ref, *second_got, dy, residual, norm_second[None], orr, olt, out_inner, out_w, mine, term_dr)
+
+    slice_terms = after(jnp.concatenate([term_gr, term_ur, term_dl], axis=0), dmix)
+    deltas, slice_terms = together(sent(dmix), over_h(slice_terms))
+    mixed_terms = sum(part[rows:].astype(F32) for part in deltas)
+    early_in = jnp.concatenate(
+        [slice_terms[i * RANK : (i + 1) * RANK] for i in range(3)]
+        + [second_terms]
+        + [mixed_terms[i * RANK : (i + 1) * RANK] for i in range(3)]
+        + [id_columns],
+        axis=1,
+    ).astype(BF)
+    deltas, early_in = together(deltas, early_in)
+    early = lax.all_gather(early_in, ("s", "h", "t")).reshape(seqs, halves, TP, RANK, -1)
 
     dq, dkv, dslot = pl.pallas_call(
         functools.partial(attend_back_kernel, tile, ranges),
@@ -801,58 +1112,89 @@
         name="attend_back",
     )(me_ref, q, kv_all, query_marks, key_marks, lse, mixed, *deltas, cosine, sine)
 
+    out_got = sent(after(out_parts, deltas))
+    dslot = after(dslot, out_got[1:3])
     returned = [
         lax.ppermute(dslot[i * span : (i + 1) * span], "h", [(b, a) for a, b in pairs])
         for i, (shift, side, pairs) in enumerate(slots)
     ]
+    layer_output = (
+        residual
+        + (out_got[0].astype(F32) + out_got[1].astype(F32))
+        + (out_got[2].astype(F32) + out_got[3].astype(F32))
+    ).astype(BF)[None]
     sides = tuple(side for _, side, _ in slots)
-    back = pl.pallas_call(
-        functools.partial(joint_back_kernel, sides),
-        out_shape=[shape((rows, d))] * 4 + [shape((RANK, cols), F32), shape((RANK, d), F32)],
-        in_specs=[SM] + [VM] * (2 + len(sides) + 9),
-        out_specs=[VM] * 6,
-        scratch_shapes=[pltpu.VMEM((tokens, 2 * kw), BF), pltpu.VMEM((tokens, cols), BF)],
+    dj, joint_deltas, term_jr, term_jl = pl.pallas_call(
+        functools.partial(joint_terms_kernel, sides),
+        out_shape=[
+            shape((tokens, cols)),
+            shape((tokens, PAD)),
+            shape((RANK, cols), F32),
+            shape((RANK, d), F32),
+        ],
+        in_specs=[SM] + [VM] * (2 + len(sides) + 8),
+        out_specs=[VM] * 4,
+        scratch_shapes=[pltpu.VMEM((tokens, 2 * kw), BF)],
+        compiler_params=params(56),
+        cost_estimate=cost(tokens * d * cols // 4, 12 * MIB),
+        name="joint_terms",
+    )(me_ref, dq, dkv, *returned, cosine, sine, jr_pad, *firsts)
+    left_parts = [
+        lax.dynamic_slice_in_dim(term_jl, (me ^ r) * width, width, 1).astype(BF) for r in range(TP)
+    ]
+    left_sent = sent(left_parts)
+    first_parts = pl.pallas_call(
+        joint_back_kernel,
+        out_shape=[shape((rows, d))] * 4,
+        in_specs=[SM] + [ANY] + [VM] * 3,
+        out_specs=[VM] * 4,
+        scratch_shapes=[pltpu.VMEM((d, cols), BF), pltpu.SemaphoreType.DMA((1,))],
         compiler_params=params(56),
         cost_estimate=cost(2 * tokens * d * cols, 16 * MIB),
         name="joint_back",
-    )(me_ref, dq, dkv, *returned, cosine, sine, joint_w, jr_pad, jlt_pad, *firsts)
-    first_parts, term_jr, term_jl = (back[:4], back[4], back[5])
-
-    got = [first_parts[0]] + [swap(first_parts[r], r) for r in (1, 2, 3)]
+    )(me_ref, joint_w, dj, after(joint_deltas, out_got), jlt_pad)
+
+    got = sent(first_parts)
+    early = after(early, got[1:3])
+    d_gr, d_ur, d_dl, d_gl, d_ul, d_dr, d_or, d_ol = slotted(
+        early,
+        tuple(by_slice(i * share) for i in range(3))
+        + tuple(by_t(3 * share + i * width, width) for i in range(5)),
+        (ff, ff, ff, d, d, d, d, d),
+        "slots_early",
+    )
+    late = jnp.concatenate([sum(part.astype(F32) for part in left_sent), term_jr], axis=1)
+    late = after(late, (got[1:3], d_gr))
+    at = 1
+    while at < halves:
+        late = late + flip(late.astype(BF), "h", at).astype(F32)
+        at *= 2
+    late = jnp.concatenate([late, id_columns], axis=1).astype(BF)[None]
+    at = 1
+    while at < seqs:
+        other = flip(late, "s", at)
+        upper = (s_at // at) % 2 == 1
+        late = jnp.concatenate(
+            [jnp.where(upper, other, late), jnp.where(upper, late, other)], axis=0
+        )
+        at *= 2
+    late_got = [late, swap(late, 1), swap(late, 2), swap(late, 3)]
+    low = [jnp.where(me % 2 == 1, late_got[i ^ 1], late_got[i]) for i in range(TP)]
+    late = jnp.stack([jnp.where(me >= 2, low[i ^ 2], low[i]) for i in range(TP)], axis=1)[:, None]
     delta_first = (got[0].astype(F32) + got[1].astype(F32)) + (
         got[2].astype(F32) + got[3].astype(F32)
     )
     input_delta = (delta_residual + norm_back(x32, norm_first, delta_first)).astype(BF)[None]
-
-    late = lax.all_gather(
-        jnp.concatenate([term_jl, term_jr], axis=1).astype(BF), ("s", "h", "t")
-    ).reshape(seqs, halves, TP, RANK, d + cols)
-
-    chosen = (ids[None, :] == jnp.arange(joint_left.shape[0], dtype=jnp.int32)[:, None]).astype(F32)
-
-    def slotted(value):
-        value = value.astype(F32)
-        return sum(chosen[:, i, None, None] * value[i][None] for i in range(seqs))
-
-    early = early.reshape(seqs, halves, TP, -1, d)
-    cut = 3 * RANK // halves
-    by_slice = early[:, :, :, :cut].transpose(0, 2, 1, 3, 4).reshape(seqs, TP, 3, RANK, groups, own_ff)
-    by_slice = by_slice.transpose(0, 2, 3, 4, 1, 5).reshape(seqs, 3, RANK, ff)
-    by_rows = early[:, :, :, cut:].reshape(seqs, 5, RANK, d)
-    d_gr, d_ur, d_dl = [slotted(by_slice[:, i]) for i in range(3)]
-    d_dr, d_gl, d_ul, d_or, d_ol = [slotted(by_rows[:, i]) for i in range(5)]
-    late = late.astype(F32)
-    d_jl = slotted(jnp.sum(late[..., :d], axis=(1, 2)))
-    late_r = jnp.sum(late[..., d:], axis=1).transpose(0, 2, 1, 3)
-    d_jr = slotted(
-        jnp.concatenate(
-            [
-                late_r[..., :qw].reshape(seqs, RANK, q_end),
-                late_r[..., qw : qw + kw].reshape(seqs, RANK, k_end - q_end),
-                late_r[..., qw + kw :].reshape(seqs, RANK, k_end - q_end),
-            ],
-            axis=2,
-        )
+    d_jl, d_jr = slotted(
+        late,
+        (
+            by_t(0, width, 0, 1),
+            by_t(width, qw, 0, 1)
+            + by_t(width + qw, kw, q_end, 1)
+            + by_t(width + qw + kw, kw, k_end, 1),
+        ),
+        (d, HEADS * HEAD_DIM + 2 * KV_HEADS * HEAD_DIM),
+        "slots_late",
     )
 
     def left(value):

time: 950 us -> 760 us (0.80)
  waiting for transfers between devices: 559 us -> 350 us
  starting transfers between devices: 27.5 us -> 102 us
  blocking collectives: 61.8 us -> 0 us
  Pallas kernels: 157 us -> 207 us
  other arithmetic: 44.9 us -> 25.4 us
  local copies, waits for them, and re-layouts: 72 us -> 55.4 us
    all_gather x1, waiting for transfers between devices: 94.1 us -> 0.01 us  [per_device(): feed_w = lax.all_gather(feed_cut[None], ('s', 'h'), axis=0, tiled=True)]
    ppermute x24 -> x42, waiting for transfers between devices: 320 us -> 260 us  [swap(): return lax.ppermute(value, 't', [(i, i ^ r) for i in range(TP)])]
    all_to_all x2 -> x0, blocking collectives: 56.8 us -> none  [the longest x1 43.1 us: per_device(): feed_cut = lax.all_to_all(feed_cut, 't', 0, 0, tiled=True)]
    ppermute x24 -> x42, starting transfers between devices: 24.2 us -> 77.3 us  [swap(): return lax.ppermute(value, 't', [(i, i ^ r) for i in range(TP)])]
    pallas_call x3 -> x12, Pallas kernels: 109 us -> 158 us  [the longest x1 53.2 us: per_device(): pl.pallas_call(feed_back_kernel, grid=(steps,), in_specs=[SM] + [ANY] * 1...]
    all_gather x4 -> x2, waiting for transfers between devices: 39.2 us -> 0.04 us  [the longest x1 0.02 us: per_device(): lax.all_gather(early_in, ('s', 'h', 't'))]
    unnamed x9 -> x4, waiting for transfers between devices: 37.3 us -> 0.07 us
    ppermute x0 -> x12, starting transfers between devices: none -> 19 us  [flip(): return lax.ppermute(value, axis, [(i, i ^ bit) for i in range(size)])]
  transfers between devices with their start and end apart: 34 -> 60, of which waited for: 29 -> 31; matrix products, arithmetic and copies ran while one was open for 7% -> 7% of each run, Pallas kernels for 4% -> 18%
where the time goes in v2:
time: 760 us; the launch traced here: 757 us
  waiting for transfers between devices  350 us (46%)
  Pallas kernels  207 us (27%)
  starting transfers between devices  102 us (13%)
  local copies, waits for them, and re-layouts  55.4 us (7%)
  other arithmetic  25.4 us (3%)
  between operations  15.9 us (2%)
    ppermute x42, waiting for transfers between devices, swap(): return lax.ppermute(value, 't', [(i, i ^ r) for i in range(TP)])  260 us
    ppermute x42, starting transfers between devices, swap(): return lax.ppermute(value, 't', [(i, i ^ r) for i in range(TP)])  77.3 us
    pallas_call x1, Pallas kernels, per_device(): pl.pallas_call(feed_back_kernel, grid=(steps,), in_specs=[SM] + [ANY] * 1...  53.2 us
    ppermute x1, waiting for transfers between devices, per_device(): lax.ppermute(kv[side * span:(side + 1) * span], 'h', pairs)  38.4 us
    ppermute x1, waiting for transfers between devices, per_device(): lax.ppermute(dslot[i * span:(i + 1) * span], 'h', [(b, a) for a, b in pai...  35.5 us
    unnamed x176, local copies, waits for them, and re-layouts  28 us
    pallas_call x1, Pallas kernels, per_device(): pl.pallas_call(gate_kernel, grid=(steps,), in_specs=[ANY] * 5 + weight_sp...  26.9 us
    pallas_call x1, Pallas kernels, per_device(): pl.pallas_call(down_kernel, grid=(steps,), in_specs=[ANY] * 5 + [down_spe...  20.7 us
  transfers between devices with their start and end apart: 60, of which 31 were waited for; matrix products, arithmetic and copies ran while one was open for 7% of the time, Pallas kernels for 18%

profile of v2, /device:TPU:0, one launch (start us, length us, event | category | flops | bytes accessed | tf_op | source)
XLA Modules:
  0.0 757.4 jit_solution(13078849705875849955)
XLA Ops:
  58.8 25.2 %collective-permute-done.5.refs_1_ = bf16[2,64,2048]{2,1,0:T(8,128)(2,1)S(1)} collective-permute-done((bf16[2,64,2048]{2,1,0:T(8,128)(2,1)}, bf16[2,64,2048]{2,1,0:T(8,128)(2,1)S(1)}, u32[]{:S(2)}, u32[]{:S(2)}) %collective-permute-start.5) | collective-permute-done | bytes 524320 | tf_op jit(solution)/shard_map/ppermute | solution.py:608
  84.0 17.3 %collective-permute-done.6.refs_2_ = bf16[2,64,2048]{2,1,0:T(8,128)(2,1)S(1)} collective-permute-done((bf16[2,64,2048]{2,1,0:T(8,128)(2,1)}, bf16[2,64,2048]{2,1,0:T(8,128)(2,1)S(1)}, u32[]{:S(2)}, u32[]{:S(2)}) %collective-permute-start.6) | collective-permute-done | bytes 524320 | tf_op jit(solution)/shard_map/ppermute | solution.py:608
  101.3 10.9 %collective-permute-done.7.refs_3_ = bf16[2,64,2048]{2,1,0:T(8,128)(2,1)S(1)} collective-permute-done((bf16[2,64,2048]{2,1,0:T(8,128)(2,1)}, bf16[2,64,2048]{2,1,0:T(8,128)(2,1)S(1)}, u32[]{:S(2)}, u32[]{:S(2)}) %collective-permute-start.7) | collective-permute-done | bytes 524320 | tf_op jit(solution)/shard_map/ppermute | solution.py:608
  147.8 9.2 %qkv.1 = (bf16[1024,512]{1,0:T(8,128)(2,1)S(1)}, bf16[1024,512]{1,0:T(8,128)(2,1)S(1)}) custom-call(s32[2]{0:T(128)S(1)} %pad_add_fusion.2.me_ref, bf16[2048,1024]{1,0:T(8,128)(2,1)} %all-gather.7.cloned.1.call-done.refs_0_, bf16[256,2176]{1,0:T(8,128)(2,1)} %pad_maximum_fusion.refs_1_.refs_4_, bf16[256,2176]{1,0:T(8,128)(2,1)} %collective-permute-done.8.refs_2_.refs_5_, ...), custom_call_target="tpu_custom_call" | custom-call | flops 4563402752 | bytes 10485760 | tf_op jit(solution)/shard_map/qkv/pallas_call | solution.py:836
  169.9 38.4 %collective-permute-done.13 = bf16[512,512]{1,0:T(8,128)(2,1)S(1)} collective-permute-done((bf16[512,512]{1,0:T(8,128)(2,1)S(1)}, bf16[512,512]{1,0:T(8,128)(2,1)S(1)}, u32[]{:S(2)}, u32[]{:S(2)}) %collective-permute-start.13) | collective-permute-done | bytes 524320 | tf_op jit(solution)/shard_map/ppermute | solution.py:850
  208.5 10.0 %attend.1 = (bf16[4,256,512]{2,1,0:T(8,128)(2,1)S(1)}, f32[1024,4]{1,0:T(8,128)S(1)}) custom-call(s32[2]{0:T(128)S(1)} %pad_add_fusion.2.me_ref, bf16[1024,512]{1,0:T(8,128)(2,1)S(1)} %copy-done.39, bf16[1536,512]{1,0:T(8,128)(2,1)S(1)} %constant_dynamic-update-slice_fusion.kv_ref, s32[1024,1]{1,0:T(8,128)S(1)} %copy-done.27, ...), custom_call_target="tpu_custom_call" | custom-call | flops 2281701376 | bytes 6291456 | tf_op jit(solution)/shard_map/attend/pallas_call | solution.py:860
  225.5 35.8 %collective-permute-start.18 = (bf16[256,512]{1,0:T(8,128)(2,1)S(1)}, bf16[256,512]{1,0:T(8,128)(2,1)S(1)}, u32[]{:S(2)}, u32[]{:S(2)}) collective-permute-start(bf16[256,512]{1,0:T(8,128)(2,1)S(1)} %get-tuple-element.303), channel_id=1, source_target_pairs={{0,2},{1,3},{2,0},{3,1},{4,6},{5,7},{6,4},{7,5},{8,10},{9,11},{10,... | collective-permute-start | bytes 786440 | tf_op jit(solution)/shard_map/ppermute | solution.py:608
  262.7 12.6 %collective-permute-done.18 = bf16[256,512]{1,0:T(8,128)(2,1)S(1)} collective-permute-done((bf16[256,512]{1,0:T(8,128)(2,1)S(1)}, bf16[256,512]{1,0:T(8,128)(2,1)S(1)}, u32[]{:S(2)}, u32[]{:S(2)}) %collective-permute-start.18) | collective-permute-done | bytes 262176 | tf_op jit(solution)/shard_map/ppermute | solution.py:608
  275.7 17.3 %collective-permute-done.19 = bf16[256,512]{1,0:T(8,128)(2,1)S(1)} collective-permute-done((bf16[256,512]{1,0:T(8,128)(2,1)S(1)}, bf16[256,512]{1,0:T(8,128)(2,1)S(1)}, u32[]{:S(2)}, u32[]{:S(2)}) %collective-permute-start.19) | collective-permute-done | bytes 262176 | tf_op jit(solution)/shard_map/ppermute | solution.py:608
  295.7 15.3 %strips.1.w_ref = bf16[2048,2048]{1,0:T(8,128)(2,1)S(1)} custom-call(s32[2]{0:T(128)S(1)} %pad_add_fusion.2.me_ref, bf16[256,2048]{1,0:T(8,128)(2,1)S(1)} %copy-done.9, bf16[256,2048]{1,0:T(8,128)(2,1)} %collective-permute-done.14.refs_1_, bf16[256,2048]{1,0:T(8,128)(2,1)} %collective-permute-done.15.refs_2_, ...), custom_call_target="tpu_custom_call" | custom-call | bytes 16777216 | tf_op jit(solution)/shard_map/strips/pallas_call | solution.py:883
  324.6 25.6 %collective-permute-done.26.refs_1_ = bf16[256,2176]{1,0:T(8,128)(2,1)S(1)} collective-permute-done((bf16[256,2176]{1,0:T(8,128)(2,1)S(1)}, bf16[256,2176]{1,0:T(8,128)(2,1)S(1)}, u32[]{:S(2)}, u32[]{:S(2)}) %collective-permute-start.26) | collective-permute-done | bytes 1114144 | tf_op jit(solution)/shard_map/ppermute | solution.py:608
  350.2 21.2 %collective-permute-done.27.refs_2_ = bf16[256,2176]{1,0:T(8,128)(2,1)S(1)} collective-permute-done((bf16[256,2176]{1,0:T(8,128)(2,1)S(1)}, bf16[256,2176]{1,0:T(8,128)(2,1)S(1)}, u32[]{:S(2)}, u32[]{:S(2)}) %collective-permute-start.27) | collective-permute-done | bytes 1114144 | tf_op jit(solution)/shard_map/ppermute | solution.py:608
  374.1 12.8 %collective-permute-done.28.refs_3_ = bf16[128,2176]{1,0:T(8,128)(2,1)S(1)} collective-permute-done((bf16[128,2176]{1,0:T(8,128)(2,1)S(1)}, bf16[128,2176]{1,0:T(8,128)(2,1)S(1)}, u32[]{:S(2)}, u32[]{:S(2)}) %collective-permute-start.28) | collective-permute-done | bytes 557088 | tf_op jit(solution)/shard_map/ppermute | solution.py:608
  390.5 25.1 %collective-permute-done.32 = bf16[256,2176]{1,0:T(8,128)(2,1)S(1)} collective-permute-done((bf16[256,2176]{1,0:T(8,128)(2,1)}, bf16[256,2176]{1,0:T(8,128)(2,1)S(1)}, u32[]{:S(2)}, u32[]{:S(2)}) %collective-permute-start.32) | collective-permute-done | bytes 1114144 | tf_op jit(solution)/shard_map/ppermute | solution.py:608
  416.7 26.9 %gate.1 = (bf16[1024,2048]{1,0:T(8,128)(2,1)}, bf16[1024,2048]{1,0:T(8,128)(2,1)}, bf16[1024,2048]{1,0:T(8,128)(2,1)}) custom-call(bf16[256,2176]{1,0:T(8,128)(2,1)} %copy-done.35, bf16[256,2176]{1,0:T(8,128)(2,1)} %copy-done.58, bf16[256,2176]{1,0:T(8,128)(2,1)} %copy-done.59, bf16[128,2176]{1,0:T(8,128)(2,1)} %copy-done.80, bf16[128,2176]{1,0:T(8,128)(2,1)} %copy-done.81, ...), custom_call_target="tpu_custom_call" | custom-call | flops 17179869184 | bytes 33554432 | tf_op jit(solution)/shard_map/gate/pallas_call | solution.py:945
  443.7 53.2 %feed_back.1 = (bf16[272,2048]{1,0:T(8,128)(2,1)}, bf16[272,2048]{1,0:T(8,128)(2,1)}, bf16[272,2048]{1,0:T(8,128)(2,1)}, bf16[272,2048]{1,0:T(8,128)(2,1)}, f32[16,2048]{1,0:T(8,128)}, /*index=5*/f32[16,2048]{1,0:T(8,128)}) custom-call(s32[2]{0:T(128)} %copy-done.32, bf16[256,2176]{1,0:T(8,128)(2,1)} %copy-done.35, bf16[256,2176]{1,0:T(8,128)(2,1)} %copy-done.58, ...), custom_call_target="tpu_custom_call" | custom-call | flops 25769803776 | bytes 52428800 | tf_op jit(solution)/shard_map/feed_back/pallas_call | solution.py:958
  500.5 20.7 %down.1 = (bf16[256,2048]{1,0:T(8,128)(2,1)}, bf16[256,2048]{1,0:T(8,128)(2,1)}, bf16[256,2048]{1,0:T(8,128)(2,1)}, bf16[256,2048]{1,0:T(8,128)(2,1)}, f32[16,2048]{1,0:T(8,128)}, /*index=5*/f32[16,2048]{1,0:T(8,128)}) custom-call(bf16[256,2176]{1,0:T(8,128)(2,1)} %pad_maximum_fusion.1.refs_5_.refs_0_, ...), custom_call_target="tpu_custom_call" | custom-call | flops 8589934592 | bytes 25165824 | tf_op jit(solution)/shard_map/down/pallas_call | solution.py:983
  526.3 20.7 %collective-permute-done.35.p3 = bf16[272,2048]{1,0:T(8,128)(2,1)} collective-permute-done((bf16[272,2048]{1,0:T(8,128)(2,1)}, bf16[272,2048]{1,0:T(8,128)(2,1)}, u32[]{:S(2)}, u32[]{:S(2)}) %collective-permute-start.35) | collective-permute-done | bytes 1114144 | tf_op jit(solution)/shard_map/ppermute | solution.py:608
  547.9 10.7 %out_back.1 = (bf16[4,304,512]{2,1,0:T(8,128)(2,1)}, f32[256,2048]{1,0:T(8,128)}) custom-call(s32[2]{0:T(128)S(1)} %copy-done.33, bf16[272,2048]{1,0:T(8,128)(2,1)S(1)} %copy-done.16, bf16[272,2048]{1,0:T(8,128)(2,1)} %collective-permute-done.33.p1, bf16[272,2048]{1,0:T(8,128)(2,1)} %collective-permute-done.34.p2, ...), custom_call_target="tpu_custom_call" | custom-call | flops 2147483648 | bytes 16777216 | tf_op jit(solution)/shard_map/out_back/pallas_call | solution.py:1051
  587.1 20.6 %attend_back.1 = (bf16[1024,512]{1,0:T(8,128)(2,1)}, f32[1024,512]{1,0:T(8,128)}, bf16[512,512]{1,0:T(8,128)(2,1)}) custom-call(s32[2]{0:T(128)} %copy-done.32, bf16[1024,512]{1,0:T(8,128)(2,1)} %copy-done.38, bf16[1536,512]{1,0:T(8,128)(2,1)} %copy-done.29, s32[1024,1]{1,0:T(8,128)} %copy.76.qpos_ref, s32[1,1536]{1,0:T(1,128)} %copy-done.34, ...), custom_call_target="tpu_custom_call" | custom-call | flops 5704253440 | bytes 12582912 | tf_op jit(solution)/shard_map/attend_back/pallas_call | solution.py:1096
  608.0 20.3 %collective-permute-done.41 = bf16[256,2048]{1,0:T(8,128)(2,1)S(1)} collective-permute-done((bf16[256,2048]{1,0:T(8,128)(2,1)}, bf16[256,2048]{1,0:T(8,128)(2,1)S(1)}, u32[]{:S(2)}, u32[]{:S(2)}) %collective-permute-start.41) | collective-permute-done | bytes 1048608 | tf_op jit(solution)/shard_map/ppermute | solution.py:608
  630.4 35.5 %collective-permute-done.43.refs_0_ = bf16[512,512]{1,0:T(8,128)(2,1)S(1)} collective-permute-done((bf16[512,512]{1,0:T(8,128)(2,1)}, bf16[512,512]{1,0:T(8,128)(2,1)S(1)}, u32[]{:S(2)}, u32[]{:S(2)}) %collective-permute-start.43) | collective-permute-done | bytes 524320 | tf_op jit(solution)/shard_map/ppermute | solution.py:1118
  673.8 10.9 %joint_back.1 = (bf16[256,2048]{1,0:T(8,128)(2,1)}, bf16[256,2048]{1,0:T(8,128)(2,1)}, bf16[256,2048]{1,0:T(8,128)(2,1)}, bf16[256,2048]{1,0:T(8,128)(2,1)}) custom-call(s32[2]{0:T(128)} %copy-done.32, bf16[2048,1024]{1,0:T(8,128)(2,1)} %all-gather.7.cloned.1.call-done.refs_0_, bf16[1024,1024]{1,0:T(8,128)(2,1)} %get-tuple-element.274.refs_1_, ...), custom_call_target="tpu_custom_call" | custom-call | flops 4294967296 | bytes 16777216 | tf_op jit(solution)/shard_map/joint_back/pallas_call | solution.py:1146
  689.8 17.8 %collective-permute-done.47 = bf16[16,512]{1,0:T(8,128)(2,1)S(1)} collective-permute-done((bf16[16,512]{1,0:T(8,128)(2,1)S(1)}, bf16[16,512]{1,0:T(8,128)(2,1)S(1)}, u32[]{:S(2)}, u32[]{:S(2)}) %collective-permute-start.47) | collective-permute-done | bytes 16416 | tf_op jit(solution)/shard_map/ppermute | solution.py:608
  (375 shorter events, 227.3 us)
Async XLA Ops:
  7.2 136.0 %all-gather.7.cloned.1.call-start = ((), (), s32[]{:S(2)}) async-start(), calls=%async_computation | async-start | bytes 4718592 | tf_op jit(solution)/shard_map/all_gather | solution.py:821
  32.2 384.5 %all-gather.11.cloned.1.call-start = ((), (), s32[]{:S(2)}) async-start(), calls=%async_computation.2 | async-start | bytes 18874368 | tf_op jit(solution)/shard_map/all_gather | solution.py:829
  46.0 66.3 %collective-permute-start.8 = (bf16[256,2176]{1,0:T(8,128)(2,1)}, bf16[256,2176]{1,0:T(8,128)(2,1)}, u32[]{:S(2)}, u32[]{:S(2)}) collective-permute-start(bf16[256,2176]{1,0:T(8,128)(2,1)} %pad_maximum_fusion.refs_1_.refs_4_), channel_id=1, source_target_pairs={{0,1},{1,0},{2,3},{3,2},{4,5},{5,4},{6,7},{7,6},{8,9},{9,8},{10,11... | collective-permute-start | bytes 3342344 | tf_op jit(solution)/shard_map/ppermute | solution.py:608
  46.6 65.7 %collective-permute-start.9 = (bf16[256,2176]{1,0:T(8,128)(2,1)}, bf16[256,2176]{1,0:T(8,128)(2,1)}, u32[]{:S(2)}, u32[]{:S(2)}) collective-permute-start(bf16[256,2176]{1,0:T(8,128)(2,1)} %pad_maximum_fusion.refs_1_.refs_4_), channel_id=1, source_target_pairs={{0,2},{1,3},{2,0},{3,1},{4,6},{5,7},{6,4},{7,5},{8,10},{9,11},{10,... | collective-permute-start | bytes 3342344 | tf_op jit(solution)/shard_map/ppermute | solution.py:608
  52.4 31.6 %collective-permute-start.5 = (bf16[2,64,2048]{2,1,0:T(8,128)(2,1)}, bf16[2,64,2048]{2,1,0:T(8,128)(2,1)S(1)}, u32[]{:S(2)}, u32[]{:S(2)}) collective-permute-start(bf16[2,64,2048]{2,1,0:T(8,128)(2,1)} %get-tuple-element.171), channel_id=1, source_target_pairs={{0,1},{1,0},{2,3},{3,2},{4,5},{5,4},{6,7},{7,6},{8,9},{9,8},{10,11... | collective-permute-start | bytes 1572872 | tf_op jit(solution)/shard_map/ppermute | solution.py:608
  53.9 47.4 %collective-permute-start.6 = (bf16[2,64,2048]{2,1,0:T(8,128)(2,1)}, bf16[2,64,2048]{2,1,0:T(8,128)(2,1)S(1)}, u32[]{:S(2)}, u32[]{:S(2)}) collective-permute-start(bf16[2,64,2048]{2,1,0:T(8,128)(2,1)} %copy-done.37), channel_id=1, source_target_pairs={{0,2},{1,3},{2,0},{3,1},{4,6},{5,7},{6,4},{7,5},{8,10},{9,11},{10,... | collective-permute-start | bytes 1572872 | tf_op jit(solution)/shard_map/ppermute | solution.py:608
  56.0 56.3 %collective-permute-start.7 = (bf16[2,64,2048]{2,1,0:T(8,128)(2,1)}, bf16[2,64,2048]{2,1,0:T(8,128)(2,1)S(1)}, u32[]{:S(2)}, u32[]{:S(2)}) collective-permute-start(bf16[2,64,2048]{2,1,0:T(8,128)(2,1)} %copy-done.36), channel_id=1, source_target_pairs={{0,3},{1,2},{2,1},{3,0},{4,7},{5,6},{6,5},{7,4},{8,11},{9,10},{10,... | collective-permute-start | bytes 1572872 | tf_op jit(solution)/shard_map/ppermute | solution.py:608
  114.2 329.5 %all-gather.9.cloned.1.call-start = ((), (), s32[]{:S(2)}) async-start(), calls=%async_computation.1 | async-start | bytes 9437184 | tf_op jit(solution)/shard_map/all_gather | solution.py:875
  158.9 49.4 %collective-permute-start.14 = (bf16[256,2048]{1,0:T(8,128)(2,1)S(1)}, bf16[256,2048]{1,0:T(8,128)(2,1)}, u32[]{:S(2)}, u32[]{:S(2)}) collective-permute-start(bf16[256,2048]{1,0:T(8,128)(2,1)S(1)} %pad_maximum_fusion.2.refs_0_), channel_id=1, source_target_pairs={{0,1},{1,0},{2,3},{3,2},{4,5},{5,4},{6,7},{7,6},{8,9},{9,8},{10,11... | collective-permute-start | bytes 3145736 | tf_op jit(solution)/shard_map/ppermute | solution.py:608
  158.9 49.4 %collective-permute-start.15 = (bf16[256,2048]{1,0:T(8,128)(2,1)S(1)}, bf16[256,2048]{1,0:T(8,128)(2,1)}, u32[]{:S(2)}, u32[]{:S(2)}) collective-permute-start(bf16[256,2048]{1,0:T(8,128)(2,1)S(1)} %pad_maximum_fusion.2.refs_0_), channel_id=1, source_target_pairs={{0,2},{1,3},{2,0},{3,1},{4,6},{5,7},{6,4},{7,5},{8,10},{9,11},{10,... | collective-permute-start | bytes 3145736 | tf_op jit(solution)/shard_map/ppermute | solution.py:608
  160.9 47.4 %collective-permute-start.16 = (bf16[256,2048]{1,0:T(8,128)(2,1)S(1)}, bf16[256,2048]{1,0:T(8,128)(2,1)}, u32[]{:S(2)}, u32[]{:S(2)}) collective-permute-start(bf16[256,2048]{1,0:T(8,128)(2,1)S(1)} %pad_maximum_fusion.2.refs_0_), channel_id=1, source_target_pairs={{0,8},{8,0},{16,24},{24,16},{1,9},{9,1},{17,25},{25,17},{2,10},{10... | collective-permute-start | bytes 3145736 | tf_op jit(solution)/shard_map/ppermute | solution.py:634
  163.9 44.5 %collective-permute-start.13 = (bf16[512,512]{1,0:T(8,128)(2,1)S(1)}, bf16[512,512]{1,0:T(8,128)(2,1)S(1)}, u32[]{:S(2)}, u32[]{:S(2)}) collective-permute-start(bf16[512,512]{1,0:T(8,128)(2,1)S(1)} %slice.113), channel_id=1, source_target_pairs={{0,4},{1,5},{2,6},{3,7},{8,12},{9,13},{10,14},{11,15},{16,20},{17,... | collective-permute-start | bytes 1572872 | tf_op jit(solution)/shard_map/ppermute | solution.py:850
  220.4 489.9 %all-gather.13.cloned.1.call-start = ((), (), s32[]{:S(2)}) async-start(), calls=%async_computation.3 | async-start | bytes 6082560 | tf_op jit(solution)/shard_map/all_gather | solution.py:1094
  220.5 72.5 %collective-permute-start.22 = (bf16[256,2048]{1,0:T(8,128)(2,1)}, bf16[256,2048]{1,0:T(8,128)(2,1)S(1)}, u32[]{:S(2)}, u32[]{:S(2)}) collective-permute-start(bf16[256,2048]{1,0:T(8,128)(2,1)} %collective-permute-done.14.refs_1_), channel_id=1, source_target_pairs={{0,8},{8,0},{16,24},{24,16},{1,9},{9,1},{17,25},{25,17},{2,10},{10... | collective-permute-start | bytes 3145736 | tf_op jit(solution)/shard_map/ppermute | solution.py:634
  220.5 72.5 %collective-permute-start.23 = (bf16[256,2048]{1,0:T(8,128)(2,1)}, bf16[256,2048]{1,0:T(8,128)(2,1)S(1)}, u32[]{:S(2)}, u32[]{:S(2)}) collective-permute-start(bf16[256,2048]{1,0:T(8,128)(2,1)} %collective-permute-done.15.refs_2_), channel_id=1, source_target_pairs={{0,8},{8,0},{16,24},{24,16},{1,9},{9,1},{17,25},{25,17},{2,10},{10... | collective-permute-start | bytes 3145736 | tf_op jit(solution)/shard_map/ppermute | solution.py:634
  222.3 40.2 %collective-permute-start.17 = (bf16[256,512]{1,0:T(8,128)(2,1)S(1)}, bf16[256,512]{1,0:T(8,128)(2,1)S(1)}, u32[]{:S(2)}, u32[]{:S(2)}) collective-permute-start(bf16[256,512]{1,0:T(8,128)(2,1)S(1)} %get-tuple-element.304), channel_id=1, source_target_pairs={{0,1},{1,0},{2,3},{3,2},{4,5},{5,4},{6,7},{7,6},{8,9},{9,8},{10,11... | collective-permute-start | bytes 786440 | tf_op jit(solution)/shard_map/ppermute | solution.py:608
  225.5 49.8 %collective-permute-start.18 = (bf16[256,512]{1,0:T(8,128)(2,1)S(1)}, bf16[256,512]{1,0:T(8,128)(2,1)S(1)}, u32[]{:S(2)}, u32[]{:S(2)}) collective-permute-start(bf16[256,512]{1,0:T(8,128)(2,1)S(1)} %get-tuple-element.303), channel_id=1, source_target_pairs={{0,2},{1,3},{2,0},{3,1},{4,6},{5,7},{6,4},{7,5},{8,10},{9,11},{10,... | collective-permute-start | bytes 786440 | tf_op jit(solution)/shard_map/ppermute | solution.py:608
  324.6 46.8 %collective-permute-start.27 = (bf16[256,2176]{1,0:T(8,128)(2,1)S(1)}, bf16[256,2176]{1,0:T(8,128)(2,1)S(1)}, u32[]{:S(2)}, u32[]{:S(2)}) collective-permute-start(bf16[256,2176]{1,0:T(8,128)(2,1)S(1)} %get-tuple-element.212.refs_0_), channel_id=1, source_target_pairs={{0,2},{1,3},{2,0},{3,1},{4,6},{5,7},{6,4},{7,5},{8,10},{9,11},{10,... | collective-permute-start | bytes 3342344 | tf_op jit(solution)/shard_map/ppermute | solution.py:608
  387.5 56.2 %collective-permute-start.30 = (bf16[256,2176]{1,0:T(8,128)(2,1)}, bf16[256,2176]{1,0:T(8,128)(2,1)}, u32[]{:S(2)}, u32[]{:S(2)}) collective-permute-start(bf16[256,2176]{1,0:T(8,128)(2,1)} %pad_maximum_fusion.1.refs_5_.refs_0_), channel_id=1, source_target_pairs={{0,1},{1,0},{2,3},{3,2},{4,5},{5,4},{6,7},{7,6},{8,9},{9,8},{10,11... | collective-permute-start | bytes 3342344 | tf_op jit(solution)/shard_map/ppermute | solution.py:608
  388.7 55.0 %collective-permute-start.31 = (bf16[256,2176]{1,0:T(8,128)(2,1)}, bf16[256,2176]{1,0:T(8,128)(2,1)}, u32[]{:S(2)}, u32[]{:S(2)}) collective-permute-start(bf16[256,2176]{1,0:T(8,128)(2,1)} %pad_maximum_fusion.1.refs_5_.refs_0_), channel_id=1, source_target_pairs={{0,2},{1,3},{2,0},{3,1},{4,6},{5,7},{6,4},{7,5},{8,10},{9,11},{10,... | collective-permute-start | bytes 3342344 | tf_op jit(solution)/shard_map/ppermute | solution.py:608
  498.4 48.5 %collective-permute-start.35 = (bf16[272,2048]{1,0:T(8,128)(2,1)}, bf16[272,2048]{1,0:T(8,128)(2,1)}, u32[]{:S(2)}, u32[]{:S(2)}) collective-permute-start(bf16[272,2048]{1,0:T(8,128)(2,1)} %get-tuple-element.232), channel_id=1, source_target_pairs={{0,3},{1,2},{2,1},{3,0},{4,7},{5,6},{6,5},{7,4},{8,11},{9,10},{10,... | collective-permute-start | bytes 3342344 | tf_op jit(solution)/shard_map/ppermute | solution.py:608
  584.5 43.8 %collective-permute-start.41 = (bf16[256,2048]{1,0:T(8,128)(2,1)}, bf16[256,2048]{1,0:T(8,128)(2,1)S(1)}, u32[]{:S(2)}, u32[]{:S(2)}) collective-permute-start(bf16[256,2048]{1,0:T(8,128)(2,1)} %get-tuple-element.266), channel_id=1, source_target_pairs={{0,2},{1,3},{2,0},{3,1},{4,6},{5,7},{6,4},{7,5},{8,10},{9,11},{10,... | collective-permute-start | bytes 3145736 | tf_op jit(solution)/shard_map/ppermute | solution.py:608
  586.0 87.8 %collective-permute-start.42 = (bf16[256,2048]{1,0:T(8,128)(2,1)}, bf16[256,2048]{1,0:T(8,128)(2,1)S(1)}, u32[]{:S(2)}, u32[]{:S(2)}) collective-permute-start(bf16[256,2048]{1,0:T(8,128)(2,1)} %get-tuple-element.267), channel_id=1, source_target_pairs={{0,3},{1,2},{2,1},{3,0},{4,7},{5,6},{6,5},{7,4},{8,11},{9,10},{10,... | collective-permute-start | bytes 3145736 | tf_op jit(solution)/shard_map/ppermute | solution.py:608
  628.3 37.7 %collective-permute-start.43 = (bf16[512,512]{1,0:T(8,128)(2,1)}, bf16[512,512]{1,0:T(8,128)(2,1)S(1)}, u32[]{:S(2)}, u32[]{:S(2)}) collective-permute-start(bf16[512,512]{1,0:T(8,128)(2,1)} %get-tuple-element.273), channel_id=1, source_target_pairs={{4,0},{5,1},{6,2},{7,3},{12,8},{13,9},{14,10},{15,11},{20,16},{21,... | collective-permute-start | bytes 1572872 | tf_op jit(solution)/shard_map/ppermute | solution.py:1118
  (119 other events, 2170.0 us)
Sparse Core Ops, SparseCore 0:
  32.3 53.7 all-gather.6
  114.3 157.9 all-gather.10
  274.2 102.8 all-gather.8
  583.6 84.7 all-gather.12

commit v3 on v2

--- a/solution.py
+++ b/solution.py
@@ -404,10 +404,9 @@
 
 def load_rows(refs, stores, sem):
     copies = []
-    stores = stores if isinstance(stores, tuple) else (stores,)
-    for index, store in enumerate(stores):
+    for some, store in zip(refs, stores):
         at = 0
-        for ref in refs[5 * index : 5 * index + 5]:
+        for ref in some:
             copies.append(
                 pltpu.make_async_copy(
                     ref, store.at[pl.ds(at, ref.shape[0]), :], sem.at[len(copies)]
@@ -427,7 +426,7 @@
 
     @pl.when(pl.program_id(0) == 0)
     def _():
-        load_rows(xs, x_all, sem)
+        load_rows((xs,), (x_all,), sem)
 
     block = gate_ref.shape[-1]
     gate_w = gate_ref[...].reshape(d, block)
@@ -448,7 +447,7 @@
 
 
 def feed_back_kernel(me_ref, *refs):
-    xs, ys, refs = (refs[:5], refs[5:10], refs[10:])
+    xs, ys, refs = (refs[:5], refs[5:9], refs[9:])
     (gate_ref, up_ref, down_ref, silu_ref, slope_ref, dlt_ref, rg_ref, ru_ref, lgu_ref, *refs) = refs
     (s0, s1, s2, s3, tgr_ref, tur_ref, x_all, y_all, acc_second, acc_inner, sem) = refs
     me = me_ref[0]
@@ -458,7 +457,7 @@
 
     @pl.when(j == 0)
     def _():
-        load_rows(list(xs) + list(ys), (x_all, y_all), sem)
+        load_rows((xs, ys), (x_all, y_all), sem)
         acc_second[...] = jnp.zeros_like(acc_second)
         acc_inner[...] = jnp.zeros_like(acc_inner)
 
@@ -498,7 +497,7 @@
 
 
 def down_kernel(*refs):
-    ys, refs = (refs[:5], refs[5:])
+    ys, refs = (refs[:4], refs[4:])
     (down_ref, act_ref, dlt_ref, dr_ref, o0, o1, o2, o3, tdl_ref, tdr_ref, *refs) = refs
     (y_all, acc, acc_inner, sem) = refs
     j = pl.program_id(0)
@@ -507,7 +506,7 @@
 
     @pl.when(j == 0)
     def _():
-        load_rows(ys, y_all, sem)
+        load_rows((ys,), (y_all,), sem)
         acc[...] = jnp.zeros_like(acc)
         acc_inner[...] = jnp.zeros_like(acc_inner)
 
@@ -821,14 +820,15 @@
     joint_w = lax.all_gather(joint_cut, ("s", "h"), axis=0, tiled=True)
 
     feed_parts, first_aug, out_held, _ = together(feed_parts, first_aug, out_held, joint_cut)
-    feed_sent, first_got, (rg, ru, dlt, lgu, olt, orr, dr_pad, dy_aug) = together(
-        sent(feed_parts), near_far(first_aug), (rg, ru, dlt, lgu, olt, orr, dr_pad, dy_aug)
-    )
-    out_held = collect_rest(after(out_held, first_got), seqs, halves)
-    feed_cut = natural(feed_sent, shape((2, TP * strip, slice_ff)))
-    feed_w = lax.all_gather(feed_cut[None], ("s", "h"), axis=0, tiled=True)
-
-    first_ends, out_held = together(corners(*first_got), out_held)
+    first_got, (rg, ru, dlt, lgu, olt, orr, dr_pad, dy_aug) = together(
+        near_far(first_aug), (rg, ru, dlt, lgu, olt, orr, dr_pad, dy_aug)
+    )
+    joint_w = after(joint_w, first_got)
+    down_w = lax.all_gather(after(down_weight, joint_w), ("s", "h"), axis=0, tiled=True)
+    feed_parts, out_held = after((feed_parts, out_held), first_got)
+    first_ends, out_held, feed_sent = together(
+        corners(*first_got), collect_rest(out_held, seqs, halves), sent(feed_parts)
+    )
     held_groups = tuple(sorted(out_held))
     out_mine = jnp.concatenate([out_held[i] for i in held_groups], axis=0)
     firsts = [first_aug, *first_got, *first_ends]
@@ -853,10 +853,14 @@
         near_far(out_mine),
         flip(out_mine, "s", 1),
     )
+    down_w, feed_sent = after((down_w, feed_sent), pieces)
+    feed_cut = natural(feed_sent, shape((2, TP * strip, slice_ff)))
+    feed_w = lax.all_gather(after(feed_cut, down_w)[None], ("s", "h"), axis=0, tiled=True)
     kv_all = jnp.concatenate(pieces + [kv], axis=0)
     key_rows = kv_all.shape[0]
     pairs_done = sum((high - low) * tile for low, high in ranges) * nq
 
+    out_ends = corners(*after(out_got, pieces))
     mixed, lse = pl.pallas_call(
         functools.partial(attend_kernel, tile, ranges),
         out_shape=(shape((TP, rows, qw)), shape((tokens, nq), F32)),
@@ -868,11 +872,10 @@
         name="attend",
     )(me_ref, q, kv_all, query_marks, key_marks)
 
-    out_got = after(out_got, mixed)
-    mine, out_ends, out_cores = together(
-        sent(mixed), corners(*out_got), [flip(block, "s", 1) for block in out_got]
-    )
-    down_w = lax.all_gather(after(down_weight, mixed), ("s", "h"), axis=0, tiled=True)
+    mixed_sent = after(mixed, out_ends)
+    mine, out_cores = together(
+        sent(mixed_sent), [flip(block, "s", 1) for block in after(out_got, mixed)]
+    )
     mine = jnp.stack(mine)
     end_cores = together(*[flip(block, "s", 1) for block in out_ends])
     out_blocks = [out_mine, *out_got, *out_ends, own_core, *out_cores, *end_cores]
@@ -920,12 +923,8 @@
 
     second_got = together(*near_far(second_aug))
     second_ends = corners(*second_got)
-    second_ends = together(*second_ends)
-    dy_aug = after(dy_aug, second_ends)
-    dy_far = swap(dy_aug, 3)
-    dy_ends = (dy_far[: rows // 2], dy_far[rows // 2 :])
-    dy_got = near_far(dy_aug)
-    dys = [dy_aug, *dy_got, *dy_ends]
+    dy_aug = after(dy_aug, second_got)
+    dys = sent([dy_aug] * TP)
     seconds = [second_aug, *second_got, *second_ends]
 
     block = max(256, own_ff)
@@ -959,7 +958,7 @@
         feed_back_kernel,
         grid=(steps,),
         in_specs=[SM]
-        + [ANY] * 10
+        + [ANY] * 9
         + weight_specs
         + [down_spec]
         + [wide_spec] * 2
@@ -983,7 +982,7 @@
     down = pl.pallas_call(
         down_kernel,
         grid=(steps,),
-        in_specs=[ANY] * 5 + [down_spec, wide_spec, low_spec, kept],
+        in_specs=[ANY] * 4 + [down_spec, wide_spec, low_spec, kept],
         out_specs=[pl.BlockSpec((rows, d), fixed, **once)] * 4
         + [term_spec, pl.BlockSpec((RANK, d), fixed)],
         scratch_shapes=[

time: 760 us -> 714 us (0.939)
  waiting for transfers between devices: 350 us -> 336 us
  Pallas kernels: 207 us -> 194 us
  starting transfers between devices: 102 us -> 91.9 us
    all_gather x2, waiting for transfers between devices: 0.02 us -> 35.8 us  [the longest x1 35.8 us: per_device(): lax.all_gather(after(feed_cut, down_w)[None], ('s', 'h'), axis=0, tiled=T...]
    ppermute x1, waiting for transfers between devices: 35.5 us -> 18.3 us  [per_device(): lax.ppermute(dslot[i * span:(i + 1) * span], 'h', [(b, a) for a, b in pai...]
    ppermute x1, waiting for transfers between devices: 38.4 us -> 23.5 us  [per_device(): lax.ppermute(kv[side * span:(side + 1) * span], 'h', pairs)]
    pallas_call x1, Pallas kernels: 15.3 us -> 1.78 us  [per_device(): pl.pallas_call(functools.partial(strips_kernel, tuple(layout), strip), ou...]
    ppermute x12, waiting for transfers between devices: 16.2 us -> 6.63 us  [flip(): return lax.ppermute(value, axis, [(i, i ^ bit) for i in range(size)])]
    ppermute x42, waiting for transfers between devices: 260 us -> 251 us  [swap(): return lax.ppermute(value, 't', [(i, i ^ r) for i in range(TP)])]
    unnamed x176 -> x204, local copies, waits for them, and re-layouts: 28 us -> 26.6 us
  transfers between devices with their start and end apart: 60 -> 60, of which waited for: 31 -> 33; matrix products, arithmetic and copies ran while one was open for 7% -> 6% of each run, Pallas kernels for 18% -> 18%
where the time goes in v3:
time: 714 us; the launch traced here: 709 us
  waiting for transfers between devices  336 us (47%)
  Pallas kernels  194 us (27%)
  starting transfers between devices  91.9 us (13%)
  local copies, waits for them, and re-layouts  49.4 us (7%)
  other arithmetic  21.1 us (3%)
  between operations  16 us (2%)
    ppermute x42, waiting for transfers between devices, swap(): return lax.ppermute(value, 't', [(i, i ^ r) for i in range(TP)])  251 us
    ppermute x42, starting transfers between devices, swap(): return lax.ppermute(value, 't', [(i, i ^ r) for i in range(TP)])  71 us
    pallas_call x1, Pallas kernels, per_device(): pl.pallas_call(feed_back_kernel, grid=(steps,), in_specs=[SM] + [ANY] * 9...  53.2 us
    all_gather x1, waiting for transfers between devices, per_device(): lax.all_gather(after(feed_cut, down_w)[None], ('s', 'h'), axis=0, tiled=T...  35.8 us
    pallas_call x1, Pallas kernels, per_device(): pl.pallas_call(gate_kernel, grid=(steps,), in_specs=[ANY] * 5 + weight_sp...  26.9 us
    unnamed x204, local copies, waits for them, and re-layouts  26.6 us
    ppermute x1, waiting for transfers between devices, per_device(): lax.ppermute(kv[side * span:(side + 1) * span], 'h', pairs)  23.5 us
    pallas_call x1, Pallas kernels, per_device(): pl.pallas_call(down_kernel, grid=(steps,), in_specs=[ANY] * 4 + [down_spe...  20.7 us
  transfers between devices with their start and end apart: 60, of which 33 were waited for; matrix products, arithmetic and copies ran while one was open for 6% of the time, Pallas kernels for 18%

profile of v3, /device:TPU:0, one launch (start us, length us, event | category | flops | bytes accessed | tf_op | source)
XLA Modules:
  0.0 709.3 jit_solution(6622208819173773946)
XLA Ops:
  54.6 18.3 %collective-permute-done.5.refs_2_.refs_5_ = bf16[256,2176]{1,0:T(8,128)(2,1)} collective-permute-done((bf16[256,2176]{1,0:T(8,128)(2,1)}, bf16[256,2176]{1,0:T(8,128)(2,1)}, u32[]{:S(2)}, u32[]{:S(2)}) %collective-permute-start.5) | collective-permute-done | bytes 1114144 | tf_op jit(solution)/shard_map/ppermute | solution.py:607
  72.9 15.9 %collective-permute-done.6.refs_3_.refs_6_ = bf16[256,2176]{1,0:T(8,128)(2,1)} collective-permute-done((bf16[256,2176]{1,0:T(8,128)(2,1)}, bf16[256,2176]{1,0:T(8,128)(2,1)}, u32[]{:S(2)}, u32[]{:S(2)}) %collective-permute-start.6) | collective-permute-done | bytes 1114144 | tf_op jit(solution)/shard_map/ppermute | solution.py:607
  110.1 12.5 %collective-permute-done.11.refs_2_ = bf16[2,64,2048]{2,1,0:T(8,128)(2,1)S(1)} collective-permute-done((bf16[2,64,2048]{2,1,0:T(8,128)(2,1)}, bf16[2,64,2048]{2,1,0:T(8,128)(2,1)S(1)}, u32[]{:S(2)}, u32[]{:S(2)}) %collective-permute-start.11) | collective-permute-done | bytes 524320 | tf_op jit(solution)/shard_map/ppermute | solution.py:607
  122.6 13.7 %collective-permute-done.12.refs_3_ = bf16[2,64,2048]{2,1,0:T(8,128)(2,1)S(1)} collective-permute-done((bf16[2,64,2048]{2,1,0:T(8,128)(2,1)}, bf16[2,64,2048]{2,1,0:T(8,128)(2,1)S(1)}, u32[]{:S(2)}, u32[]{:S(2)}) %collective-permute-start.12) | collective-permute-done | bytes 524320 | tf_op jit(solution)/shard_map/ppermute | solution.py:607
  136.4 19.6 %collective-permute-done.7.refs_4_.refs_7_ = bf16[128,2176]{1,0:T(8,128)(2,1)S(1)} collective-permute-done((bf16[128,2176]{1,0:T(8,128)(2,1)S(1)}, bf16[128,2176]{1,0:T(8,128)(2,1)S(1)}, u32[]{:S(2)}, u32[]{:S(2)}) %collective-permute-start.7) | collective-permute-done | bytes 557088 | tf_op jit(solution)/shard_map/ppermute | solution.py:607
  157.3 9.6 %qkv.1 = (bf16[1024,512]{1,0:T(8,128)(2,1)S(1)}, bf16[1024,512]{1,0:T(8,128)(2,1)S(1)}) custom-call(s32[2]{0:T(128)S(1)} %pad_add_fusion.2.me_ref, bf16[2048,1024]{1,0:T(8,128)(2,1)} %all-gather.7.cloned.1.call-done.refs_0_, bf16[256,2176]{1,0:T(8,128)(2,1)} %pad_maximum_fusion.refs_1_.refs_4_, bf16[256,2176]{1,0:T(8,128)(2,1)} %collective-permute-done.5.refs_2_.refs_5_, ...), custom_call_target="tpu_custom_call" | custom-call | flops 4563402752 | bytes 10485760 | tf_op jit(solution)/shard_map/qkv/pallas_call | solution.py:836
  174.2 23.5 %collective-permute-done.13 = bf16[512,512]{1,0:T(8,128)(2,1)S(1)} collective-permute-done((bf16[512,512]{1,0:T(8,128)(2,1)S(1)}, bf16[512,512]{1,0:T(8,128)(2,1)S(1)}, u32[]{:S(2)}, u32[]{:S(2)}) %collective-permute-start.13) | collective-permute-done | bytes 524320 | tf_op jit(solution)/shard_map/ppermute | solution.py:850
  213.5 10.0 %attend.1 = (bf16[4,256,512]{2,1,0:T(8,128)(2,1)S(1)}, f32[1024,4]{1,0:T(8,128)S(1)}) custom-call(s32[2]{0:T(128)S(1)} %pad_add_fusion.2.me_ref, bf16[1024,512]{1,0:T(8,128)(2,1)S(1)} %copy-done.47, bf16[1536,512]{1,0:T(8,128)(2,1)S(1)} %constant_dynamic-update-slice_fusion.kv_ref, s32[1024,1]{1,0:T(8,128)S(1)} %copy-done.37, ...), custom_call_target="tpu_custom_call" | custom-call | flops 2281701376 | bytes 6291456 | tf_op jit(solution)/shard_map/attend/pallas_call | solution.py:864
  238.2 10.8 %collective-permute-done.21 = bf16[256,512]{1,0:T(8,128)(2,1)S(1)} collective-permute-done((bf16[256,512]{1,0:T(8,128)(2,1)S(1)}, bf16[256,512]{1,0:T(8,128)(2,1)S(1)}, u32[]{:S(2)}, u32[]{:S(2)}) %collective-permute-start.21) | collective-permute-done | bytes 262176 | tf_op jit(solution)/shard_map/ppermute | solution.py:607
  267.4 18.3 %collective-permute-done.26.refs_1_ = bf16[256,2176]{1,0:T(8,128)(2,1)S(1)} collective-permute-done((bf16[256,2176]{1,0:T(8,128)(2,1)S(1)}, bf16[256,2176]{1,0:T(8,128)(2,1)S(1)}, u32[]{:S(2)}, u32[]{:S(2)}) %collective-permute-start.26) | collective-permute-done | bytes 1114144 | tf_op jit(solution)/shard_map/ppermute | solution.py:607
  285.7 28.1 %collective-permute-done.27.refs_2_ = bf16[256,2176]{1,0:T(8,128)(2,1)S(1)} collective-permute-done((bf16[256,2176]{1,0:T(8,128)(2,1)S(1)}, bf16[256,2176]{1,0:T(8,128)(2,1)S(1)}, u32[]{:S(2)}, u32[]{:S(2)}) %collective-permute-start.27) | collective-permute-done | bytes 1114144 | tf_op jit(solution)/shard_map/ppermute | solution.py:607
  319.2 20.1 %collective-permute-done.28.refs_3_ = bf16[128,2176]{1,0:T(8,128)(2,1)S(1)} collective-permute-done((bf16[128,2176]{1,0:T(8,128)(2,1)S(1)}, bf16[128,2176]{1,0:T(8,128)(2,1)S(1)}, u32[]{:S(2)}, u32[]{:S(2)}) %collective-permute-start.28) | collective-permute-done | bytes 557088 | tf_op jit(solution)/shard_map/ppermute | solution.py:607
  340.1 35.8 %all-gather.11.cloned.1.call-done = bf16[16,256,2048]{2,1,0:T(8,128)(2,1)} async-done(((bf16[2,256,2048]{2,1,0:T(8,128)(2,1)}), bf16[16,256,2048]{2,1,0:T(8,128)(2,1)}) %all-gather.11.cloned.1.call-update) | async-done | bytes 16777232 | tf_op jit(solution)/shard_map/all_gather | solution.py:858
  375.9 26.9 %gate.1 = (bf16[1024,2048]{1,0:T(8,128)(2,1)}, bf16[1024,2048]{1,0:T(8,128)(2,1)}, bf16[1024,2048]{1,0:T(8,128)(2,1)}) custom-call(bf16[256,2176]{1,0:T(8,128)(2,1)} %copy-done.45, bf16[256,2176]{1,0:T(8,128)(2,1)} %copy-done.68, bf16[256,2176]{1,0:T(8,128)(2,1)} %copy-done.69, bf16[128,2176]{1,0:T(8,128)(2,1)} %copy-done.95, ...), custom_call_target="tpu_custom_call" | custom-call | flops 17179869184 | bytes 33554432 | tf_op jit(solution)/shard_map/gate/pallas_call | solution.py:944
  402.9 53.2 %feed_back.1 = (bf16[272,2048]{1,0:T(8,128)(2,1)}, bf16[272,2048]{1,0:T(8,128)(2,1)}, bf16[272,2048]{1,0:T(8,128)(2,1)}, bf16[272,2048]{1,0:T(8,128)(2,1)}, f32[16,2048]{1,0:T(8,128)}, /*index=5*/f32[16,2048]{1,0:T(8,128)}) custom-call(s32[2]{0:T(128)} %copy-done.42, bf16[256,2176]{1,0:T(8,128)(2,1)} %copy-done.45, bf16[256,2176]{1,0:T(8,128)(2,1)} %copy-done.68, ...), custom_call_target="tpu_custom_call" | custom-call | flops 25769803776 | bytes 52428800 | tf_op jit(solution)/shard_map/feed_back/pallas_call | solution.py:957
  459.7 20.7 %down.1 = (bf16[256,2048]{1,0:T(8,128)(2,1)}, bf16[256,2048]{1,0:T(8,128)(2,1)}, bf16[256,2048]{1,0:T(8,128)(2,1)}, bf16[256,2048]{1,0:T(8,128)(2,1)}, f32[16,2048]{1,0:T(8,128)}, /*index=5*/f32[16,2048]{1,0:T(8,128)}) custom-call(bf16[256,2176]{1,0:T(8,128)(2,1)} %pad_maximum_fusion.1.refs_5_.refs_0_, ...), custom_call_target="tpu_custom_call" | custom-call | flops 8589934592 | bytes 25165824 | tf_op jit(solution)/shard_map/down/pallas_call | solution.py:982
  485.4 22.9 %collective-permute-done.35.p3 = bf16[272,2048]{1,0:T(8,128)(2,1)} collective-permute-done((bf16[272,2048]{1,0:T(8,128)(2,1)}, bf16[272,2048]{1,0:T(8,128)(2,1)}, u32[]{:S(2)}, u32[]{:S(2)}) %collective-permute-start.35) | collective-permute-done | bytes 1114144 | tf_op jit(solution)/shard_map/ppermute | solution.py:607
  509.2 10.7 %out_back.1 = (bf16[4,304,512]{2,1,0:T(8,128)(2,1)}, f32[256,2048]{1,0:T(8,128)}) custom-call(s32[2]{0:T(128)S(1)} %copy-done.43, bf16[272,2048]{1,0:T(8,128)(2,1)S(1)} %copy-done.20, bf16[272,2048]{1,0:T(8,128)(2,1)} %collective-permute-done.33.p1, bf16[272,2048]{1,0:T(8,128)(2,1)} %collective-permute-done.34.p2, ...), custom_call_target="tpu_custom_call" | custom-call | flops 2147483648 | bytes 16777216 | tf_op jit(solution)/shard_map/out_back/pallas_call | solution.py:1050
  546.4 20.6 %attend_back.1 = (bf16[1024,512]{1,0:T(8,128)(2,1)}, f32[1024,512]{1,0:T(8,128)}, bf16[512,512]{1,0:T(8,128)(2,1)}) custom-call(s32[2]{0:T(128)} %copy-done.42, bf16[1024,512]{1,0:T(8,128)(2,1)} %copy-done.46, bf16[1536,512]{1,0:T(8,128)(2,1)} %copy-done.39, s32[1024,1]{1,0:T(8,128)} %copy.76.qpos_ref, s32[1,1536]{1,0:T(1,128)} %copy-done.44, ...), custom_call_target="tpu_custom_call" | custom-call | flops 5704253440 | bytes 12582912 | tf_op jit(solution)/shard_map/attend_back/pallas_call | solution.py:1095
  567.7 15.6 %collective-permute-done.41 = bf16[256,2048]{1,0:T(8,128)(2,1)S(1)} collective-permute-done((bf16[256,2048]{1,0:T(8,128)(2,1)}, bf16[256,2048]{1,0:T(8,128)(2,1)S(1)}, u32[]{:S(2)}, u32[]{:S(2)}) %collective-permute-start.41) | collective-permute-done | bytes 1048608 | tf_op jit(solution)/shard_map/ppermute | solution.py:607
  585.4 18.3 %collective-permute-done.43.refs_0_ = bf16[512,512]{1,0:T(8,128)(2,1)S(1)} collective-permute-done((bf16[512,512]{1,0:T(8,128)(2,1)}, bf16[512,512]{1,0:T(8,128)(2,1)S(1)}, u32[]{:S(2)}, u32[]{:S(2)}) %collective-permute-start.43) | collective-permute-done | bytes 524320 | tf_op jit(solution)/shard_map/ppermute | solution.py:1117
  614.1 10.9 %joint_back.1 = (bf16[256,2048]{1,0:T(8,128)(2,1)}, bf16[256,2048]{1,0:T(8,128)(2,1)}, bf16[256,2048]{1,0:T(8,128)(2,1)}, bf16[256,2048]{1,0:T(8,128)(2,1)}) custom-call(s32[2]{0:T(128)} %copy-done.42, bf16[2048,1024]{1,0:T(8,128)(2,1)} %all-gather.7.cloned.1.call-done.refs_0_, bf16[1024,1024]{1,0:T(8,128)(2,1)} %get-tuple-element.294.refs_1_, ...), custom_call_target="tpu_custom_call" | custom-call | flops 4294967296 | bytes 16777216 | tf_op jit(solution)/shard_map/joint_back/pallas_call | solution.py:1145
  627.8 8.9 %collective-permute-start.45 = (bf16[256,2048]{1,0:T(8,128)(2,1)}, bf16[256,2048]{1,0:T(8,128)(2,1)S(1)}, u32[]{:S(2)}, u32[]{:S(2)}) collective-permute-start(bf16[256,2048]{1,0:T(8,128)(2,1)} %get-tuple-element.299), channel_id=1, source_target_pairs={{0,2},{1,3},{2,0},{3,1},{4,6},{5,7},{6,4},{7,5},{8,10},{9,11},{10,... | collective-permute-start | bytes 3145736 | tf_op jit(solution)/shard_map/ppermute | solution.py:607
  645.9 12.6 %collective-permute-start.46 = (bf16[256,2048]{1,0:T(8,128)(2,1)}, bf16[256,2048]{1,0:T(8,128)(2,1)}, u32[]{:S(2)}, u32[]{:S(2)}) collective-permute-start(bf16[256,2048]{1,0:T(8,128)(2,1)} %get-tuple-element.300), channel_id=1, source_target_pairs={{0,3},{1,2},{2,1},{3,0},{4,7},{5,6},{6,5},{7,4},{8,11},{9,10},{10,... | collective-permute-start | bytes 3145736 | tf_op jit(solution)/shard_map/ppermute | solution.py:607
  (402 shorter events, 235.5 us)
Async XLA Ops:
  7.2 81.6 %all-gather.7.cloned.1.call-start = ((), (), s32[]{:S(2)}) async-start(), calls=%async_computation | async-start | bytes 4718592 | tf_op jit(solution)/shard_map/all_gather | solution.py:820
  32.2 168.3 %all-gather.9.cloned.1.call-start = ((), (), s32[]{:S(2)}) async-start(), calls=%async_computation.1 | async-start | bytes 9437184 | tf_op jit(solution)/shard_map/all_gather | solution.py:827
  46.6 42.2 %collective-permute-start.6 = (bf16[256,2176]{1,0:T(8,128)(2,1)}, bf16[256,2176]{1,0:T(8,128)(2,1)}, u32[]{:S(2)}, u32[]{:S(2)}) collective-permute-start(bf16[256,2176]{1,0:T(8,128)(2,1)} %pad_maximum_fusion.refs_1_.refs_4_), channel_id=1, source_target_pairs={{0,2},{1,3},{2,0},{3,1},{4,6},{5,7},{6,4},{7,5},{8,10},{9,11},{10,... | collective-permute-start | bytes 3342344 | tf_op jit(solution)/shard_map/ppermute | solution.py:607
  88.8 287.1 %all-gather.11.cloned.1.call-start = ((), (), s32[]{:S(2)}) async-start(), calls=%async_computation.2 | async-start | bytes 18874368 | tf_op jit(solution)/shard_map/all_gather | solution.py:858
  96.6 39.8 %collective-permute-start.12 = (bf16[2,64,2048]{2,1,0:T(8,128)(2,1)}, bf16[2,64,2048]{2,1,0:T(8,128)(2,1)S(1)}, u32[]{:S(2)}, u32[]{:S(2)}) collective-permute-start(bf16[2,64,2048]{2,1,0:T(8,128)(2,1)} %get-tuple-element.196), channel_id=1, source_target_pairs={{0,3},{1,2},{2,1},{3,0},{4,7},{5,6},{6,5},{7,4},{8,11},{9,10},{10,... | collective-permute-start | bytes 1572872 | tf_op jit(solution)/shard_map/ppermute | solution.py:607
  98.5 57.5 %collective-permute-start.7 = (bf16[128,2176]{1,0:T(8,128)(2,1)S(1)}, bf16[128,2176]{1,0:T(8,128)(2,1)S(1)}, u32[]{:S(2)}, u32[]{:S(2)}) collective-permute-start(bf16[128,2176]{1,0:T(8,128)(2,1)S(1)} %slice.102), channel_id=1, source_target_pairs={{0,2},{1,3},{2,0},{3,1},{4,6},{5,7},{6,4},{7,5},{8,10},{9,11},{10,... | collective-permute-start | bytes 1671176 | tf_op jit(solution)/shard_map/ppermute | solution.py:607
  98.6 57.4 %collective-permute-start.8 = (bf16[128,2176]{1,0:T(8,128)(2,1)S(1)}, bf16[128,2176]{1,0:T(8,128)(2,1)S(1)}, u32[]{:S(2)}, u32[]{:S(2)}) collective-permute-start(bf16[128,2176]{1,0:T(8,128)(2,1)S(1)} %slice.103), channel_id=1, source_target_pairs={{0,1},{1,0},{2,3},{3,2},{4,5},{5,4},{6,7},{7,6},{8,9},{9,8},{10,11... | collective-permute-start | bytes 1671176 | tf_op jit(solution)/shard_map/ppermute | solution.py:607
  168.0 29.7 %collective-permute-start.14 = (bf16[256,2048]{1,0:T(8,128)(2,1)S(1)}, bf16[256,2048]{1,0:T(8,128)(2,1)S(1)}, u32[]{:S(2)}, u32[]{:S(2)}) collective-permute-start(bf16[256,2048]{1,0:T(8,128)(2,1)S(1)} %pad_maximum_fusion.2.refs_0_), channel_id=1, source_target_pairs={{0,1},{1,0},{2,3},{3,2},{4,5},{5,4},{6,7},{7,6},{8,9},{9,8},{10,11... | collective-permute-start | bytes 3145736 | tf_op jit(solution)/shard_map/ppermute | solution.py:607
  168.0 29.7 %collective-permute-start.15 = (bf16[256,2048]{1,0:T(8,128)(2,1)S(1)}, bf16[256,2048]{1,0:T(8,128)(2,1)S(1)}, u32[]{:S(2)}, u32[]{:S(2)}) collective-permute-start(bf16[256,2048]{1,0:T(8,128)(2,1)S(1)} %pad_maximum_fusion.2.refs_0_), channel_id=1, source_target_pairs={{0,2},{1,3},{2,0},{3,1},{4,6},{5,7},{6,4},{7,5},{8,10},{9,11},{10,... | collective-permute-start | bytes 3145736 | tf_op jit(solution)/shard_map/ppermute | solution.py:607
  170.6 28.9 %collective-permute-start.16 = (bf16[256,2048]{1,0:T(8,128)(2,1)S(1)}, bf16[256,2048]{1,0:T(8,128)(2,1)S(1)}, u32[]{:S(2)}, u32[]{:S(2)}) collective-permute-start(bf16[256,2048]{1,0:T(8,128)(2,1)S(1)} %pad_maximum_fusion.2.refs_0_), channel_id=1, source_target_pairs={{0,8},{8,0},{16,24},{24,16},{1,9},{9,1},{17,25},{25,17},{2,10},{10... | collective-permute-start | bytes 3145736 | tf_op jit(solution)/shard_map/ppermute | solution.py:633
  170.7 27.1 %collective-permute-start.13 = (bf16[512,512]{1,0:T(8,128)(2,1)S(1)}, bf16[512,512]{1,0:T(8,128)(2,1)S(1)}, u32[]{:S(2)}, u32[]{:S(2)}) collective-permute-start(bf16[512,512]{1,0:T(8,128)(2,1)S(1)} %slice.107), channel_id=1, source_target_pairs={{0,4},{1,5},{2,6},{3,7},{8,12},{9,13},{10,14},{11,15},{16,20},{17,... | collective-permute-start | bytes 1572872 | tf_op jit(solution)/shard_map/ppermute | solution.py:850
  206.6 455.4 %all-gather.13.cloned.1.call-start = ((), (), s32[]{:S(2)}) async-start(), calls=%async_computation.3 | async-start | bytes 6082560 | tf_op jit(solution)/shard_map/all_gather | solution.py:1093
  264.4 49.4 %collective-permute-start.27 = (bf16[256,2176]{1,0:T(8,128)(2,1)S(1)}, bf16[256,2176]{1,0:T(8,128)(2,1)S(1)}, u32[]{:S(2)}, u32[]{:S(2)}) collective-permute-start(bf16[256,2176]{1,0:T(8,128)(2,1)S(1)} %get-tuple-element.228.refs_0_), channel_id=1, source_target_pairs={{0,2},{1,3},{2,0},{3,1},{4,6},{5,7},{6,4},{7,5},{8,10},{9,11},{10,... | collective-permute-start | bytes 3342344 | tf_op jit(solution)/shard_map/ppermute | solution.py:607
  315.7 87.2 %collective-permute-start.30 = (bf16[256,2176]{1,0:T(8,128)(2,1)}, bf16[256,2176]{1,0:T(8,128)(2,1)}, u32[]{:S(2)}, u32[]{:S(2)}) collective-permute-start(bf16[256,2176]{1,0:T(8,128)(2,1)} %pad_maximum_fusion.1.refs_5_.refs_0_), channel_id=1, source_target_pairs={{0,1},{1,0},{2,3},{3,2},{4,5},{5,4},{6,7},{7,6},{8,9},{9,8},{10,11... | collective-permute-start | bytes 3342344 | tf_op jit(solution)/shard_map/ppermute | solution.py:607
  316.0 86.8 %collective-permute-start.31 = (bf16[256,2176]{1,0:T(8,128)(2,1)}, bf16[256,2176]{1,0:T(8,128)(2,1)}, u32[]{:S(2)}, u32[]{:S(2)}) collective-permute-start(bf16[256,2176]{1,0:T(8,128)(2,1)} %pad_maximum_fusion.1.refs_5_.refs_0_), channel_id=1, source_target_pairs={{0,2},{1,3},{2,0},{3,1},{4,6},{5,7},{6,4},{7,5},{8,10},{9,11},{10,... | collective-permute-start | bytes 3342344 | tf_op jit(solution)/shard_map/ppermute | solution.py:607
  318.1 84.8 %collective-permute-start.32 = (bf16[256,2176]{1,0:T(8,128)(2,1)}, bf16[256,2176]{1,0:T(8,128)(2,1)}, u32[]{:S(2)}, u32[]{:S(2)}) collective-permute-start(bf16[256,2176]{1,0:T(8,128)(2,1)} %pad_maximum_fusion.1.refs_5_.refs_0_), channel_id=1, source_target_pairs={{0,3},{1,2},{2,1},{3,0},{4,7},{5,6},{6,5},{7,4},{8,11},{9,10},{10,... | collective-permute-start | bytes 3342344 | tf_op jit(solution)/shard_map/ppermute | solution.py:607
  456.1 27.1 %collective-permute-start.33 = (bf16[272,2048]{1,0:T(8,128)(2,1)}, bf16[272,2048]{1,0:T(8,128)(2,1)}, u32[]{:S(2)}, u32[]{:S(2)}) collective-permute-start(bf16[272,2048]{1,0:T(8,128)(2,1)} %get-tuple-element.250), channel_id=1, source_target_pairs={{0,1},{1,0},{2,3},{3,2},{4,5},{5,4},{6,7},{7,6},{8,9},{9,8},{10,11... | collective-permute-start | bytes 3342344 | tf_op jit(solution)/shard_map/ppermute | solution.py:607
  457.7 27.7 %collective-permute-start.34 = (bf16[272,2048]{1,0:T(8,128)(2,1)}, bf16[272,2048]{1,0:T(8,128)(2,1)}, u32[]{:S(2)}, u32[]{:S(2)}) collective-permute-start(bf16[272,2048]{1,0:T(8,128)(2,1)} %get-tuple-element.251), channel_id=1, source_target_pairs={{0,2},{1,3},{2,0},{3,1},{4,6},{5,7},{6,4},{7,5},{8,10},{9,11},{10,... | collective-permute-start | bytes 3342344 | tf_op jit(solution)/shard_map/ppermute | solution.py:607
  457.7 50.6 %collective-permute-start.35 = (bf16[272,2048]{1,0:T(8,128)(2,1)}, bf16[272,2048]{1,0:T(8,128)(2,1)}, u32[]{:S(2)}, u32[]{:S(2)}) collective-permute-start(bf16[272,2048]{1,0:T(8,128)(2,1)} %get-tuple-element.252), channel_id=1, source_target_pairs={{0,3},{1,2},{2,1},{3,0},{4,7},{5,6},{6,5},{7,4},{8,11},{9,10},{10,... | collective-permute-start | bytes 3342344 | tf_op jit(solution)/shard_map/ppermute | solution.py:607
  544.4 38.9 %collective-permute-start.41 = (bf16[256,2048]{1,0:T(8,128)(2,1)}, bf16[256,2048]{1,0:T(8,128)(2,1)S(1)}, u32[]{:S(2)}, u32[]{:S(2)}) collective-permute-start(bf16[256,2048]{1,0:T(8,128)(2,1)} %get-tuple-element.286), channel_id=1, source_target_pairs={{0,2},{1,3},{2,0},{3,1},{4,6},{5,7},{6,4},{7,5},{8,10},{9,11},{10,... | collective-permute-start | bytes 3145736 | tf_op jit(solution)/shard_map/ppermute | solution.py:607
  546.4 67.6 %collective-permute-start.42 = (bf16[256,2048]{1,0:T(8,128)(2,1)}, bf16[256,2048]{1,0:T(8,128)(2,1)S(1)}, u32[]{:S(2)}, u32[]{:S(2)}) collective-permute-start(bf16[256,2048]{1,0:T(8,128)(2,1)} %get-tuple-element.287), channel_id=1, source_target_pairs={{0,3},{1,2},{2,1},{3,0},{4,7},{5,6},{6,5},{7,4},{8,11},{9,10},{10,... | collective-permute-start | bytes 3145736 | tf_op jit(solution)/shard_map/ppermute | solution.py:607
  625.0 37.0 %collective-permute-start.44 = (bf16[256,2048]{1,0:T(8,128)(2,1)}, bf16[256,2048]{1,0:T(8,128)(2,1)S(1)}, u32[]{:S(2)}, u32[]{:S(2)}) collective-permute-start(bf16[256,2048]{1,0:T(8,128)(2,1)} %get-tuple-element.298), channel_id=1, source_target_pairs={{0,1},{1,0},{2,3},{3,2},{4,5},{5,4},{6,7},{7,6},{8,9},{9,8},{10,11... | collective-permute-start | bytes 3145736 | tf_op jit(solution)/shard_map/ppermute | solution.py:607
  627.8 34.2 %collective-permute-start.45 = (bf16[256,2048]{1,0:T(8,128)(2,1)}, bf16[256,2048]{1,0:T(8,128)(2,1)S(1)}, u32[]{:S(2)}, u32[]{:S(2)}) collective-permute-start(bf16[256,2048]{1,0:T(8,128)(2,1)} %get-tuple-element.299), channel_id=1, source_target_pairs={{0,2},{1,3},{2,0},{3,1},{4,6},{5,7},{6,4},{7,5},{8,10},{9,11},{10,... | collective-permute-start | bytes 3145736 | tf_op jit(solution)/shard_map/ppermute | solution.py:607
  645.9 32.7 %collective-permute-start.46 = (bf16[256,2048]{1,0:T(8,128)(2,1)}, bf16[256,2048]{1,0:T(8,128)(2,1)}, u32[]{:S(2)}, u32[]{:S(2)}) collective-permute-start(bf16[256,2048]{1,0:T(8,128)(2,1)} %get-tuple-element.300), channel_id=1, source_target_pairs={{0,3},{1,2},{2,1},{3,0},{4,7},{5,6},{6,5},{7,4},{8,11},{9,10},{10,... | collective-permute-start | bytes 3145736 | tf_op jit(solution)/shard_map/ppermute | solution.py:607
  (133 other events, 2283.7 us)
Sparse Core Ops, SparseCore 0:
  32.3 54.0 all-gather.6
  88.9 89.8 all-gather.8
  206.7 169.1 all-gather.10
  542.8 88.6 all-gather.12

commit v4 on v3

--- a/solution.py
+++ b/solution.py
@@ -136,19 +136,14 @@
             feeds[r][1, :, g * wide : (g + 1) * wide] = up_ref[:, at]
 
 
-def natural_kernel(count, me_ref, *refs):
-    parts, (out_ref, sem) = (refs[:count], refs[-2:])
-    me = me_ref[0]
-    strip = parts[0].shape[-2]
-    copies = []
-    for r, ref in enumerate(parts):
-        rows = pl.ds(pl.multiple_of((me ^ r) * strip, strip), strip)
-        to = out_ref.at[rows, :] if len(ref.shape) == 2 else out_ref.at[:, rows, :]
-        copies.append(pltpu.make_async_copy(ref, to, sem.at[r]))
-    for copy in copies:
-        copy.start()
-    for copy in copies:
-        copy.wait()
+def natural_kernel(me_ref, r0, r1, r2, r3, out_ref):
+    strip = r0.shape[-2]
+    for r, ref in enumerate((r0, r1, r2, r3)):
+        rows = pl.ds(pl.multiple_of((me_ref[0] ^ r) * strip, strip), strip)
+        if len(ref.shape) == 2:
+            out_ref[rows, :] = ref[...]
+        else:
+            out_ref[:, rows, :] = ref[...]
 
 
 def strips_kernel(layout, strip, me_ref, *refs):
@@ -749,17 +744,16 @@
             for r in range(TP)
         ]
 
-    def natural(parts, out, *others):
+    def natural(parts, out):
         return pl.pallas_call(
-            functools.partial(natural_kernel, TP),
+            natural_kernel,
             out_shape=out,
-            in_specs=[SM] + [ANY] * (TP + len(others)),
-            out_specs=ANY,
-            scratch_shapes=[pltpu.SemaphoreType.DMA((TP,))],
-            compiler_params=params(8),
+            in_specs=[SM] + [VM] * TP,
+            out_specs=VM,
+            compiler_params=params(24),
             cost_estimate=cost(0, 4 * MIB),
             name="natural",
-        )(me_ref, *parts, *others)
+        )(me_ref, *parts)
 
     def ff_slice(value):
         return lax.dynamic_index_in_dim(
@@ -829,6 +823,7 @@
     first_ends, out_held, feed_sent = together(
         corners(*first_got), collect_rest(out_held, seqs, halves), sent(feed_parts)
     )
+    feed_cut = natural(feed_sent, shape((2, TP * strip, slice_ff)))
     held_groups = tuple(sorted(out_held))
     out_mine = jnp.concatenate([out_held[i] for i in held_groups], axis=0)
     firsts = [first_aug, *first_got, *first_ends]
@@ -853,8 +848,7 @@
         near_far(out_mine),
         flip(out_mine, "s", 1),
     )
-    down_w, feed_sent = after((down_w, feed_sent), pieces)
-    feed_cut = natural(feed_sent, shape((2, TP * strip, slice_ff)))
+    down_w, feed_cut = after((down_w, feed_cut), pieces)
     feed_w = lax.all_gather(after(feed_cut, down_w)[None], ("s", "h"), axis=0, tiled=True)
     kv_all = jnp.concatenate(pieces + [kv], axis=0)
     key_rows = kv_all.shape[0]

time: 714 us -> 721 us (level)
  starting transfers between devices: 91.9 us -> 103 us
    ppermute x12, starting transfers between devices: 15.1 us -> 29.9 us  [flip(): return lax.ppermute(value, axis, [(i, i ^ bit) for i in range(size)])]
    unnamed x204 -> x184, local copies, waits for them, and re-layouts: 26.6 us -> 21.4 us
  transfers between devices with their start and end apart: 60 -> 60, of which waited for: 33 -> 36; matrix products, arithmetic and copies ran while one was open for 6% -> 7% of each run, Pallas kernels for 18% -> 18%
where the time goes in v4:
time: 721 us; the launch traced here: 716 us
  waiting for transfers between devices  333 us (46%)
  Pallas kernels  195 us (27%)
  starting transfers between devices  103 us (14%)
  local copies, waits for them, and re-layouts  46.1 us (6%)
  other arithmetic  22.4 us (3%)
  between operations  16 us (2%)
    ppermute x42, waiting for transfers between devices, swap(): return lax.ppermute(value, 't', [(i, i ^ r) for i in range(TP)])  258 us
    ppermute x42, starting transfers between devices, swap(): return lax.ppermute(value, 't', [(i, i ^ r) for i in range(TP)])  65.8 us
    pallas_call x1, Pallas kernels, per_device(): pl.pallas_call(feed_back_kernel, grid=(steps,), in_specs=[SM] + [ANY] * 9...  53.2 us
    all_gather x1, waiting for transfers between devices, per_device(): lax.all_gather(after(feed_cut, down_w)[None], ('s', 'h'), axis=0, tiled=T...  30.2 us
    ppermute x12, starting transfers between devices, flip(): return lax.ppermute(value, axis, [(i, i ^ bit) for i in range(size)])  29.9 us
    pallas_call x1, Pallas kernels, per_device(): pl.pallas_call(gate_kernel, grid=(steps,), in_specs=[ANY] * 5 + weight_sp...  26.9 us
    ppermute x1, waiting for transfers between devices, per_device(): lax.ppermute(kv[side * span:(side + 1) * span], 'h', pairs)  21.4 us
    unnamed x184, local copies, waits for them, and re-layouts  21.4 us
  transfers between devices with their start and end apart: 60, of which 36 were waited for; matrix products, arithmetic and copies ran while one was open for 7% of the time, Pallas kernels for 18%

profile of v4, /device:TPU:0, one launch (start us, length us, event | category | flops | bytes accessed | tf_op | source)
XLA Modules:
  0.0 715.9 jit_solution(2626437367711870823)
XLA Ops:
  55.3 15.9 %collective-permute-done.5.refs_2_.refs_5_ = bf16[256,2176]{1,0:T(8,128)(2,1)} collective-permute-done((bf16[256,2176]{1,0:T(8,128)(2,1)}, bf16[256,2176]{1,0:T(8,128)(2,1)}, u32[]{:S(2)}, u32[]{:S(2)}) %collective-permute-start.5) | collective-permute-done | bytes 1114144 | tf_op jit(solution)/shard_map/ppermute | solution.py:602
  71.2 15.9 %collective-permute-done.6.refs_3_.refs_6_ = bf16[256,2176]{1,0:T(8,128)(2,1)} collective-permute-done((bf16[256,2176]{1,0:T(8,128)(2,1)}, bf16[256,2176]{1,0:T(8,128)(2,1)}, u32[]{:S(2)}, u32[]{:S(2)}) %collective-permute-start.6) | collective-permute-done | bytes 1114144 | tf_op jit(solution)/shard_map/ppermute | solution.py:602
  110.4 12.9 %collective-permute-done.11.r2 = bf16[2,64,2048]{2,1,0:T(8,128)(2,1)S(1)} collective-permute-done((bf16[2,64,2048]{2,1,0:T(8,128)(2,1)S(1)}, bf16[2,64,2048]{2,1,0:T(8,128)(2,1)S(1)}, u32[]{:S(2)}, u32[]{:S(2)}) %collective-permute-start.11) | collective-permute-done | bytes 524320 | tf_op jit(solution)/shard_map/ppermute | solution.py:602
  123.2 14.4 %collective-permute-done.12.r3 = bf16[2,64,2048]{2,1,0:T(8,128)(2,1)S(1)} collective-permute-done((bf16[2,64,2048]{2,1,0:T(8,128)(2,1)S(1)}, bf16[2,64,2048]{2,1,0:T(8,128)(2,1)S(1)}, u32[]{:S(2)}, u32[]{:S(2)}) %collective-permute-start.12) | collective-permute-done | bytes 524320 | tf_op jit(solution)/shard_map/ppermute | solution.py:602
  137.6 19.6 %collective-permute-done.7.refs_4_.refs_7_ = bf16[128,2176]{1,0:T(8,128)(2,1)S(1)} collective-permute-done((bf16[128,2176]{1,0:T(8,128)(2,1)S(1)}, bf16[128,2176]{1,0:T(8,128)(2,1)S(1)}, u32[]{:S(2)}, u32[]{:S(2)}) %collective-permute-start.7) | collective-permute-done | bytes 557088 | tf_op jit(solution)/shard_map/ppermute | solution.py:602
  158.5 9.6 %qkv.1 = (bf16[1024,512]{1,0:T(8,128)(2,1)S(1)}, bf16[1024,512]{1,0:T(8,128)(2,1)S(1)}) custom-call(s32[2]{0:T(128)S(1)} %pad_add_fusion.2.me_ref, bf16[2048,1024]{1,0:T(8,128)(2,1)} %all-gather.7.cloned.1.call-done.refs_0_, bf16[256,2176]{1,0:T(8,128)(2,1)} %pad_maximum_fusion.refs_1_.refs_4_, bf16[256,2176]{1,0:T(8,128)(2,1)} %collective-permute-done.5.refs_2_.refs_5_, ...), custom_call_target="tpu_custom_call" | custom-call | flops 4563402752 | bytes 10485760 | tf_op jit(solution)/shard_map/qkv/pallas_call | solution.py:831
  178.9 21.4 %collective-permute-done.13 = bf16[512,512]{1,0:T(8,128)(2,1)} collective-permute-done((bf16[512,512]{1,0:T(8,128)(2,1)}, bf16[512,512]{1,0:T(8,128)(2,1)}, u32[]{:S(2)}, u32[]{:S(2)}) %collective-permute-start.13) | collective-permute-done | bytes 524320 | tf_op jit(solution)/shard_map/ppermute | solution.py:845
  208.1 10.0 %attend.1 = (bf16[4,256,512]{2,1,0:T(8,128)(2,1)S(1)}, f32[1024,4]{1,0:T(8,128)S(1)}) custom-call(s32[2]{0:T(128)S(1)} %pad_add_fusion.2.me_ref, bf16[1024,512]{1,0:T(8,128)(2,1)S(1)} %copy-done.41, bf16[1536,512]{1,0:T(8,128)(2,1)S(1)} %constant_dynamic-update-slice_fusion.kv_ref, s32[1024,1]{1,0:T(8,128)S(1)} %copy-done.25, ...), custom_call_target="tpu_custom_call" | custom-call | flops 2281701376 | bytes 6291456 | tf_op jit(solution)/shard_map/attend/pallas_call | solution.py:858
  234.7 11.7 %collective-permute-done.21 = bf16[256,512]{1,0:T(8,128)(2,1)S(1)} collective-permute-done((bf16[256,512]{1,0:T(8,128)(2,1)S(1)}, bf16[256,512]{1,0:T(8,128)(2,1)S(1)}, u32[]{:S(2)}, u32[]{:S(2)}) %collective-permute-start.21) | collective-permute-done | bytes 262176 | tf_op jit(solution)/shard_map/ppermute | solution.py:602
  266.3 20.5 %collective-permute-done.26.refs_1_ = bf16[256,2176]{1,0:T(8,128)(2,1)S(1)} collective-permute-done((bf16[256,2176]{1,0:T(8,128)(2,1)S(1)}, bf16[256,2176]{1,0:T(8,128)(2,1)S(1)}, u32[]{:S(2)}, u32[]{:S(2)}) %collective-permute-start.26) | collective-permute-done | bytes 1114144 | tf_op jit(solution)/shard_map/ppermute | solution.py:602
  286.9 21.9 %collective-permute-done.27.refs_2_ = bf16[256,2176]{1,0:T(8,128)(2,1)S(1)} collective-permute-done((bf16[256,2176]{1,0:T(8,128)(2,1)S(1)}, bf16[256,2176]{1,0:T(8,128)(2,1)S(1)}, u32[]{:S(2)}, u32[]{:S(2)}) %collective-permute-start.27) | collective-permute-done | bytes 1114144 | tf_op jit(solution)/shard_map/ppermute | solution.py:602
  315.0 21.2 %collective-permute-done.28.refs_3_ = bf16[128,2176]{1,0:T(8,128)(2,1)S(1)} collective-permute-done((bf16[128,2176]{1,0:T(8,128)(2,1)S(1)}, bf16[128,2176]{1,0:T(8,128)(2,1)S(1)}, u32[]{:S(2)}, u32[]{:S(2)}) %collective-permute-start.28) | collective-permute-done | bytes 557088 | tf_op jit(solution)/shard_map/ppermute | solution.py:602
  337.1 30.2 %all-gather.11.cloned.1.call-done = bf16[16,256,2048]{2,1,0:T(8,128)(2,1)} async-done(((bf16[2,256,2048]{2,1,0:T(8,128)(2,1)}), bf16[16,256,2048]{2,1,0:T(8,128)(2,1)}) %all-gather.11.cloned.1.call-update) | async-done | bytes 16777232 | tf_op jit(solution)/shard_map/all_gather | solution.py:852
  367.3 26.9 %gate.1 = (bf16[1024,2048]{1,0:T(8,128)(2,1)}, bf16[1024,2048]{1,0:T(8,128)(2,1)}, bf16[1024,2048]{1,0:T(8,128)(2,1)}) custom-call(bf16[256,2176]{1,0:T(8,128)(2,1)} %copy-done.33, bf16[256,2176]{1,0:T(8,128)(2,1)} %copy-done.60, bf16[256,2176]{1,0:T(8,128)(2,1)} %copy-done.61, bf16[128,2176]{1,0:T(8,128)(2,1)} %copy-done.85, ...), custom_call_target="tpu_custom_call" | custom-call | flops 17179869184 | bytes 33554432 | tf_op jit(solution)/shard_map/gate/pallas_call | solution.py:938
  397.9 53.2 %feed_back.1 = (bf16[272,2048]{1,0:T(8,128)(2,1)}, bf16[272,2048]{1,0:T(8,128)(2,1)}, bf16[272,2048]{1,0:T(8,128)(2,1)}, bf16[272,2048]{1,0:T(8,128)(2,1)}, f32[16,2048]{1,0:T(8,128)}, /*index=5*/f32[16,2048]{1,0:T(8,128)}) custom-call(s32[2]{0:T(128)} %copy-done.30, bf16[256,2176]{1,0:T(8,128)(2,1)} %copy-done.33, bf16[256,2176]{1,0:T(8,128)(2,1)} %copy-done.60, ...), custom_call_target="tpu_custom_call" | custom-call | flops 25769803776 | bytes 52428800 | tf_op jit(solution)/shard_map/feed_back/pallas_call | solution.py:951
  454.7 20.7 %down.1 = (bf16[256,2048]{1,0:T(8,128)(2,1)}, bf16[256,2048]{1,0:T(8,128)(2,1)}, bf16[256,2048]{1,0:T(8,128)(2,1)}, bf16[256,2048]{1,0:T(8,128)(2,1)}, f32[16,2048]{1,0:T(8,128)}, /*index=5*/f32[16,2048]{1,0:T(8,128)}) custom-call(bf16[256,2176]{1,0:T(8,128)(2,1)} %pad_maximum_fusion.1.refs_5_.refs_0_, ...), custom_call_target="tpu_custom_call" | custom-call | flops 8589934592 | bytes 25165824 | tf_op jit(solution)/shard_map/down/pallas_call | solution.py:976
  479.1 23.2 %collective-permute-done.35.p3 = bf16[272,2048]{1,0:T(8,128)(2,1)} collective-permute-done((bf16[272,2048]{1,0:T(8,128)(2,1)}, bf16[272,2048]{1,0:T(8,128)(2,1)}, u32[]{:S(2)}, u32[]{:S(2)}) %collective-permute-start.35) | collective-permute-done | bytes 1114144 | tf_op jit(solution)/shard_map/ppermute | solution.py:602
  503.2 10.7 %out_back.1 = (bf16[4,304,512]{2,1,0:T(8,128)(2,1)}, f32[256,2048]{1,0:T(8,128)}) custom-call(s32[2]{0:T(128)S(1)} %copy-done.31, bf16[272,2048]{1,0:T(8,128)(2,1)S(1)} %copy-done.16, bf16[272,2048]{1,0:T(8,128)(2,1)} %collective-permute-done.33.p1, bf16[272,2048]{1,0:T(8,128)(2,1)} %collective-permute-done.34.p2, ...), custom_call_target="tpu_custom_call" | custom-call | flops 2147483648 | bytes 16777216 | tf_op jit(solution)/shard_map/out_back/pallas_call | solution.py:1044
  542.4 20.6 %attend_back.1 = (bf16[1024,512]{1,0:T(8,128)(2,1)}, f32[1024,512]{1,0:T(8,128)}, bf16[512,512]{1,0:T(8,128)(2,1)}) custom-call(s32[2]{0:T(128)} %copy-done.30, bf16[1024,512]{1,0:T(8,128)(2,1)} %copy-done.40, bf16[1536,512]{1,0:T(8,128)(2,1)} %copy-done.27, s32[1024,1]{1,0:T(8,128)} %copy.76.qpos_ref, s32[1,1536]{1,0:T(1,128)} %copy-done.32, ...), custom_call_target="tpu_custom_call" | custom-call | flops 5704253440 | bytes 12582912 | tf_op jit(solution)/shard_map/attend_back/pallas_call | solution.py:1089
  563.7 14.4 %collective-permute-done.41 = bf16[256,2048]{1,0:T(8,128)(2,1)S(1)} collective-permute-done((bf16[256,2048]{1,0:T(8,128)(2,1)}, bf16[256,2048]{1,0:T(8,128)(2,1)S(1)}, u32[]{:S(2)}, u32[]{:S(2)}) %collective-permute-start.41) | collective-permute-done | bytes 1048608 | tf_op jit(solution)/shard_map/ppermute | solution.py:602
  580.2 17.7 %collective-permute-done.43.refs_0_ = bf16[512,512]{1,0:T(8,128)(2,1)S(1)} collective-permute-done((bf16[512,512]{1,0:T(8,128)(2,1)}, bf16[512,512]{1,0:T(8,128)(2,1)S(1)}, u32[]{:S(2)}, u32[]{:S(2)}) %collective-permute-start.43) | collective-permute-done | bytes 524320 | tf_op jit(solution)/shard_map/ppermute | solution.py:1111
  613.2 10.9 %joint_back.1 = (bf16[256,2048]{1,0:T(8,128)(2,1)}, bf16[256,2048]{1,0:T(8,128)(2,1)}, bf16[256,2048]{1,0:T(8,128)(2,1)}, bf16[256,2048]{1,0:T(8,128)(2,1)}) custom-call(s32[2]{0:T(128)} %copy-done.30, bf16[2048,1024]{1,0:T(8,128)(2,1)} %all-gather.7.cloned.1.call-done.refs_0_, bf16[1024,1024]{1,0:T(8,128)(2,1)} %get-tuple-element.288.refs_1_, ...), custom_call_target="tpu_custom_call" | custom-call | flops 4294967296 | bytes 16777216 | tf_op jit(solution)/shard_map/joint_back/pallas_call | solution.py:1139
  642.6 10.6 %collective-permute-start.46 = (bf16[256,2048]{1,0:T(8,128)(2,1)}, bf16[256,2048]{1,0:T(8,128)(2,1)}, u32[]{:S(2)}, u32[]{:S(2)}) collective-permute-start(bf16[256,2048]{1,0:T(8,128)(2,1)} %get-tuple-element.294), channel_id=1, source_target_pairs={{0,3},{1,2},{2,1},{3,0},{4,7},{5,6},{6,5},{7,4},{8,11},{9,10},{10,... | collective-permute-start | bytes 3145736 | tf_op jit(solution)/shard_map/ppermute | solution.py:602
  675.6 14.1 %collective-permute-start.52 = (bf16[2,16,1664]{2,1,0:T(8,128)(2,1)S(1)}, bf16[2,16,1664]{2,1,0:T(8,128)(2,1)S(1)}, u32[]{:S(2)}, u32[]{:S(2)}) collective-permute-start(bf16[2,16,1664]{2,1,0:T(8,128)(2,1)S(1)} %pad_maximum_fusion.8), channel_id=1, source_target_pairs={{0,16},{8,24},{16,0},{24,8},{1,17},{9,25},{17,1},{25,9},{2,18},{10... | collective-permute-start | bytes 319496 | tf_op jit(solution)/shard_map/ppermute | solution.py:628
  (382 shorter events, 251.8 us)
Async XLA Ops:
  7.2 79.9 %all-gather.7.cloned.1.call-start = ((), (), s32[]{:S(2)}) async-start(), calls=%async_computation | async-start | bytes 4718592 | tf_op jit(solution)/shard_map/all_gather | solution.py:814
  31.5 168.9 %all-gather.9.cloned.1.call-start = ((), (), s32[]{:S(2)}) async-start(), calls=%async_computation.1 | async-start | bytes 9437184 | tf_op jit(solution)/shard_map/all_gather | solution.py:821
  46.0 41.1 %collective-permute-start.6 = (bf16[256,2176]{1,0:T(8,128)(2,1)}, bf16[256,2176]{1,0:T(8,128)(2,1)}, u32[]{:S(2)}, u32[]{:S(2)}) collective-permute-start(bf16[256,2176]{1,0:T(8,128)(2,1)} %pad_maximum_fusion.refs_1_.refs_4_), channel_id=1, source_target_pairs={{0,2},{1,3},{2,0},{3,1},{4,6},{5,7},{6,4},{7,5},{8,10},{9,11},{10,... | collective-permute-start | bytes 3342344 | tf_op jit(solution)/shard_map/ppermute | solution.py:602
  87.1 280.2 %all-gather.11.cloned.1.call-start = ((), (), s32[]{:S(2)}) async-start(), calls=%async_computation.2 | async-start | bytes 18874368 | tf_op jit(solution)/shard_map/all_gather | solution.py:852
  97.1 40.5 %collective-permute-start.12 = (bf16[2,64,2048]{2,1,0:T(8,128)(2,1)S(1)}, bf16[2,64,2048]{2,1,0:T(8,128)(2,1)S(1)}, u32[]{:S(2)}, u32[]{:S(2)}) collective-permute-start(bf16[2,64,2048]{2,1,0:T(8,128)(2,1)S(1)} %copy-done.35), channel_id=1, source_target_pairs={{0,3},{1,2},{2,1},{3,0},{4,7},{5,6},{6,5},{7,4},{8,11},{9,10},{10,... | collective-permute-start | bytes 1572872 | tf_op jit(solution)/shard_map/ppermute | solution.py:602
  99.0 58.2 %collective-permute-start.7 = (bf16[128,2176]{1,0:T(8,128)(2,1)S(1)}, bf16[128,2176]{1,0:T(8,128)(2,1)S(1)}, u32[]{:S(2)}, u32[]{:S(2)}) collective-permute-start(bf16[128,2176]{1,0:T(8,128)(2,1)S(1)} %slice.102), channel_id=1, source_target_pairs={{0,2},{1,3},{2,0},{3,1},{4,6},{5,7},{6,4},{7,5},{8,10},{9,11},{10,... | collective-permute-start | bytes 1671176 | tf_op jit(solution)/shard_map/ppermute | solution.py:602
  99.2 58.0 %collective-permute-start.8 = (bf16[128,2176]{1,0:T(8,128)(2,1)S(1)}, bf16[128,2176]{1,0:T(8,128)(2,1)S(1)}, u32[]{:S(2)}, u32[]{:S(2)}) collective-permute-start(bf16[128,2176]{1,0:T(8,128)(2,1)S(1)} %slice.103), channel_id=1, source_target_pairs={{0,1},{1,0},{2,3},{3,2},{4,5},{5,4},{6,7},{7,6},{8,9},{9,8},{10,11... | collective-permute-start | bytes 1671176 | tf_op jit(solution)/shard_map/ppermute | solution.py:602
  168.2 32.1 %collective-permute-start.14 = (bf16[256,2048]{1,0:T(8,128)(2,1)S(1)}, bf16[256,2048]{1,0:T(8,128)(2,1)}, u32[]{:S(2)}, u32[]{:S(2)}) collective-permute-start(bf16[256,2048]{1,0:T(8,128)(2,1)S(1)} %pad_maximum_fusion.2.refs_0_), channel_id=1, source_target_pairs={{0,1},{1,0},{2,3},{3,2},{4,5},{5,4},{6,7},{7,6},{8,9},{9,8},{10,11... | collective-permute-start | bytes 3145736 | tf_op jit(solution)/shard_map/ppermute | solution.py:602
  168.3 32.0 %collective-permute-start.15 = (bf16[256,2048]{1,0:T(8,128)(2,1)S(1)}, bf16[256,2048]{1,0:T(8,128)(2,1)}, u32[]{:S(2)}, u32[]{:S(2)}) collective-permute-start(bf16[256,2048]{1,0:T(8,128)(2,1)S(1)} %pad_maximum_fusion.2.refs_0_), channel_id=1, source_target_pairs={{0,2},{1,3},{2,0},{3,1},{4,6},{5,7},{6,4},{7,5},{8,10},{9,11},{10,... | collective-permute-start | bytes 3145736 | tf_op jit(solution)/shard_map/ppermute | solution.py:602
  170.7 29.6 %collective-permute-start.16 = (bf16[256,2048]{1,0:T(8,128)(2,1)S(1)}, bf16[256,2048]{1,0:T(8,128)(2,1)}, u32[]{:S(2)}, u32[]{:S(2)}) collective-permute-start(bf16[256,2048]{1,0:T(8,128)(2,1)S(1)} %pad_maximum_fusion.2.refs_0_), channel_id=1, source_target_pairs={{0,8},{8,0},{16,24},{24,16},{1,9},{9,1},{17,25},{25,17},{2,10},{10... | collective-permute-start | bytes 3145736 | tf_op jit(solution)/shard_map/ppermute | solution.py:628
  171.6 28.8 %collective-permute-start.13 = (bf16[512,512]{1,0:T(8,128)(2,1)}, bf16[512,512]{1,0:T(8,128)(2,1)}, u32[]{:S(2)}, u32[]{:S(2)}) collective-permute-start(bf16[512,512]{1,0:T(8,128)(2,1)} %slice.107), channel_id=1, source_target_pairs={{0,4},{1,5},{2,6},{3,7},{8,12},{9,13},{10,14},{11,15},{16,20},{17,... | collective-permute-start | bytes 1572872 | tf_op jit(solution)/shard_map/ppermute | solution.py:845
  200.4 456.3 %all-gather.13.cloned.1.call-start = ((), (), s32[]{:S(2)}) async-start(), calls=%async_computation.3 | async-start | bytes 6082560 | tf_op jit(solution)/shard_map/all_gather | solution.py:1087
  218.2 28.2 %collective-permute-start.22 = (bf16[256,2048]{1,0:T(8,128)(2,1)}, bf16[256,2048]{1,0:T(8,128)(2,1)S(1)}, u32[]{:S(2)}, u32[]{:S(2)}) collective-permute-start(bf16[256,2048]{1,0:T(8,128)(2,1)} %collective-permute-done.14.refs_1_), channel_id=1, source_target_pairs={{0,8},{8,0},{16,24},{24,16},{1,9},{9,1},{17,25},{25,17},{2,10},{10... | collective-permute-start | bytes 3145736 | tf_op jit(solution)/shard_map/ppermute | solution.py:628
  218.2 28.1 %collective-permute-start.23 = (bf16[256,2048]{1,0:T(8,128)(2,1)}, bf16[256,2048]{1,0:T(8,128)(2,1)S(1)}, u32[]{:S(2)}, u32[]{:S(2)}) collective-permute-start(bf16[256,2048]{1,0:T(8,128)(2,1)} %collective-permute-done.15.refs_2_), channel_id=1, source_target_pairs={{0,8},{8,0},{16,24},{24,16},{1,9},{9,1},{17,25},{25,17},{2,10},{10... | collective-permute-start | bytes 3145736 | tf_op jit(solution)/shard_map/ppermute | solution.py:628
  263.4 45.3 %collective-permute-start.27 = (bf16[256,2176]{1,0:T(8,128)(2,1)S(1)}, bf16[256,2176]{1,0:T(8,128)(2,1)S(1)}, u32[]{:S(2)}, u32[]{:S(2)}) collective-permute-start(bf16[256,2176]{1,0:T(8,128)(2,1)S(1)} %get-tuple-element.225.refs_0_), channel_id=1, source_target_pairs={{0,2},{1,3},{2,0},{3,1},{4,6},{5,7},{6,4},{7,5},{8,10},{9,11},{10,... | collective-permute-start | bytes 3342344 | tf_op jit(solution)/shard_map/ppermute | solution.py:602
  311.5 82.8 %collective-permute-start.30 = (bf16[256,2176]{1,0:T(8,128)(2,1)}, bf16[256,2176]{1,0:T(8,128)(2,1)}, u32[]{:S(2)}, u32[]{:S(2)}) collective-permute-start(bf16[256,2176]{1,0:T(8,128)(2,1)} %pad_maximum_fusion.1.refs_5_.refs_0_), channel_id=1, source_target_pairs={{0,1},{1,0},{2,3},{3,2},{4,5},{5,4},{6,7},{7,6},{8,9},{9,8},{10,11... | collective-permute-start | bytes 3342344 | tf_op jit(solution)/shard_map/ppermute | solution.py:602
  313.5 80.8 %collective-permute-start.31 = (bf16[256,2176]{1,0:T(8,128)(2,1)}, bf16[256,2176]{1,0:T(8,128)(2,1)}, u32[]{:S(2)}, u32[]{:S(2)}) collective-permute-start(bf16[256,2176]{1,0:T(8,128)(2,1)} %pad_maximum_fusion.1.refs_5_.refs_0_), channel_id=1, source_target_pairs={{0,2},{1,3},{2,0},{3,1},{4,6},{5,7},{6,4},{7,5},{8,10},{9,11},{10,... | collective-permute-start | bytes 3342344 | tf_op jit(solution)/shard_map/ppermute | solution.py:602
  313.5 84.4 %collective-permute-start.32 = (bf16[256,2176]{1,0:T(8,128)(2,1)}, bf16[256,2176]{1,0:T(8,128)(2,1)}, u32[]{:S(2)}, u32[]{:S(2)}) collective-permute-start(bf16[256,2176]{1,0:T(8,128)(2,1)} %pad_maximum_fusion.1.refs_5_.refs_0_), channel_id=1, source_target_pairs={{0,3},{1,2},{2,1},{3,0},{4,7},{5,6},{6,5},{7,4},{8,11},{9,10},{10,... | collective-permute-start | bytes 3342344 | tf_op jit(solution)/shard_map/ppermute | solution.py:602
  451.3 51.0 %collective-permute-start.35 = (bf16[272,2048]{1,0:T(8,128)(2,1)}, bf16[272,2048]{1,0:T(8,128)(2,1)}, u32[]{:S(2)}, u32[]{:S(2)}) collective-permute-start(bf16[272,2048]{1,0:T(8,128)(2,1)} %get-tuple-element.246), channel_id=1, source_target_pairs={{0,3},{1,2},{2,1},{3,0},{4,7},{5,6},{6,5},{7,4},{8,11},{9,10},{10,... | collective-permute-start | bytes 3342344 | tf_op jit(solution)/shard_map/ppermute | solution.py:602
  540.1 38.0 %collective-permute-start.41 = (bf16[256,2048]{1,0:T(8,128)(2,1)}, bf16[256,2048]{1,0:T(8,128)(2,1)S(1)}, u32[]{:S(2)}, u32[]{:S(2)}) collective-permute-start(bf16[256,2048]{1,0:T(8,128)(2,1)} %get-tuple-element.280), channel_id=1, source_target_pairs={{0,2},{1,3},{2,0},{3,1},{4,6},{5,7},{6,4},{7,5},{8,10},{9,11},{10,... | collective-permute-start | bytes 3145736 | tf_op jit(solution)/shard_map/ppermute | solution.py:602
  541.6 71.6 %collective-permute-start.42 = (bf16[256,2048]{1,0:T(8,128)(2,1)}, bf16[256,2048]{1,0:T(8,128)(2,1)S(1)}, u32[]{:S(2)}, u32[]{:S(2)}) collective-permute-start(bf16[256,2048]{1,0:T(8,128)(2,1)} %get-tuple-element.281), channel_id=1, source_target_pairs={{0,3},{1,2},{2,1},{3,0},{4,7},{5,6},{6,5},{7,4},{8,11},{9,10},{10,... | collective-permute-start | bytes 3145736 | tf_op jit(solution)/shard_map/ppermute | solution.py:602
  624.1 32.6 %collective-permute-start.44 = (bf16[256,2048]{1,0:T(8,128)(2,1)}, bf16[256,2048]{1,0:T(8,128)(2,1)S(1)}, u32[]{:S(2)}, u32[]{:S(2)}) collective-permute-start(bf16[256,2048]{1,0:T(8,128)(2,1)} %get-tuple-element.292), channel_id=1, source_target_pairs={{0,1},{1,0},{2,3},{3,2},{4,5},{5,4},{6,7},{7,6},{8,9},{9,8},{10,11... | collective-permute-start | bytes 3145736 | tf_op jit(solution)/shard_map/ppermute | solution.py:602
  628.7 28.0 %collective-permute-start.45 = (bf16[256,2048]{1,0:T(8,128)(2,1)}, bf16[256,2048]{1,0:T(8,128)(2,1)S(1)}, u32[]{:S(2)}, u32[]{:S(2)}) collective-permute-start(bf16[256,2048]{1,0:T(8,128)(2,1)} %get-tuple-element.293), channel_id=1, source_target_pairs={{0,2},{1,3},{2,0},{3,1},{4,6},{5,7},{6,4},{7,5},{8,10},{9,11},{10,... | collective-permute-start | bytes 3145736 | tf_op jit(solution)/shard_map/ppermute | solution.py:602
  642.6 30.6 %collective-permute-start.46 = (bf16[256,2048]{1,0:T(8,128)(2,1)}, bf16[256,2048]{1,0:T(8,128)(2,1)}, u32[]{:S(2)}, u32[]{:S(2)}) collective-permute-start(bf16[256,2048]{1,0:T(8,128)(2,1)} %get-tuple-element.294), channel_id=1, source_target_pairs={{0,3},{1,2},{2,1},{3,0},{4,7},{5,6},{6,5},{7,4},{8,11},{9,10},{10,... | collective-permute-start | bytes 3145736 | tf_op jit(solution)/shard_map/ppermute | solution.py:602
  (123 other events, 2186.9 us)
Sparse Core Ops, SparseCore 0:
  31.6 54.0 all-gather.6
  87.6 90.5 all-gather.8
  200.5 166.7 all-gather.10
  539.0 89.0 all-gather.12
